TPU v7x, 512 devices: a whole 4x4x16 slice. The times are simulated.
512 devices in a mesh: blk: 16 (over x, z_hi, core), head: 32 (over y, z_lo).
Axes of the slice: x: 4, y: 4, z: 16 (z_hi: 2, z_lo: 8; z = z_hi * 8 + z_lo), core: 2. Of those that a mesh axis runs over, the one named last changes fastest.
Arguments:
- queries: bfloat16 [16, 32, 256, 128], P('blk', 'head'), may hold values from -24 to 24
- keys: bfloat16 [16, 32, 256, 128], P('blk', 'head'), may hold values from -6 to 6
- values: bfloat16 [16, 32, 256, 128], P('blk', 'head'), may hold values from -6 to 6
- grad_out: bfloat16 [16, 32, 256, 128], P('blk', 'head'), may hold values from -384 to 384
- key_tiles: int32 [64, 32], replicated, may hold values from 0 to 64, as said below
- work_lists: int32 [16, 32, 2], replicated, may hold values from 0 to 3, as said below
Outputs:
- grad_queries: bfloat16 [16, 32, 256, 128], P('blk', 'head')
- grad_keys: bfloat16 [16, 32, 256, 128], P('blk', 'head')
- grad_values: bfloat16 [16, 32, 256, 128], P('blk', 'head')
Inputs may be any that keep to these rules, and one draw needn't show every extreme that they name: `key_tiles`: each row lists distinct key tiles in rising order, always its own tile, then is filled up with 64; a row lists at most 32 tiles, and the first tile of every section lists exactly 32. `work_lists`: for each section and head n, the lists of slots 2 n and 2 n + 1 together hold each of the section's 4 tiles once.
All inputs are finite; a program needn't handle non-finite values.
Results may differ from a plain program's by a relative error of at most 0.018.
Values may be sent and summed in bfloat16 or wider, within the bound.
No kernel may reach another device: no remote copies, remote signals or barrier semaphores. Data moves between devices by JAX's collectives and lax.ppermute only.
A program may use at most 64 MiB of HBM per device.

v0:
```python
import jax
import jax.numpy as jnp
from jax import lax
from jax.sharding import PartitionSpec as P

TILE = 128


def swapped(value, axis, stride):
    mask = 2**stride
    pairs = [(source, source ^ mask) for source in range(lax.axis_size(axis))]
    return lax.ppermute(value, axis, pairs)


def from_behind(block, axis, distance):
    devices = range(lax.axis_size(axis))
    route = [((i - distance) % len(devices), i) for i in devices]
    return lax.ppermute(block, axis, route)


def tile_matches(tile_lists, key_ids):
    return jnp.any(tile_lists[:, None, :] == key_ids[None, :, None], axis=2)


def token_mask(matched, tile_rows):
    query_count, key_count = matched.shape
    expanded = jnp.broadcast_to(
        matched[:, None, :, None], (query_count, tile_rows, key_count, tile_rows)
    )
    return expanded.reshape(query_count * tile_rows, key_count * tile_rows)


def scaled_scores(query_rows, key_rows):
    return jnp.dot(query_rows, key_rows.T, preferred_element_type=jnp.float32) * query_rows.shape[
        1
    ] ** (-0.5)


def forward_turn(query_rows, key_value, allowed, running):
    running_top, running_sum, running_out = running
    scores = scaled_scores(query_rows, key_value[0])
    row_top = jnp.max(jnp.where(allowed, scores, -1e30), axis=1)
    new_top = jnp.maximum(running_top, row_top)
    factor = jnp.exp(running_top - new_top)
    weights = jnp.where(allowed, jnp.exp(scores - new_top[:, None]), 0.0)
    running_sum = running_sum * factor + jnp.sum(weights, axis=1)
    product = jnp.dot(weights, key_value[1].astype(jnp.float32), precision=lax.Precision.HIGHEST)
    running_out = running_out * factor[:, None] + product
    return (new_top, running_sum, running_out)


def backward_terms(query_rows, grad_rows, row_stats, key_value, allowed):
    scores = scaled_scores(query_rows, key_value[0])
    probability = jnp.where(allowed, jnp.exp(scores - row_stats[0][:, None]), 0.0)
    probs_b = probability.astype(jnp.bfloat16)
    grad_v = jnp.dot(probs_b.T, grad_rows, preferred_element_type=jnp.float32)
    grad_probs = jnp.dot(grad_rows, key_value[1].T, preferred_element_type=jnp.float32)
    grad_scores = (probability * (grad_probs - row_stats[1][:, None])).astype(jnp.bfloat16)
    grad_q = jnp.dot(grad_scores, key_value[0], preferred_element_type=jnp.float32)
    grad_k = jnp.dot(grad_scores.T, query_rows, preferred_element_type=jnp.float32)
    return (grad_q, jnp.stack([grad_k, grad_v]))


def on_device(queries, keys, values, grad_out, key_tiles, work_lists):
    cycle_size = lax.axis_size("blk")
    section = lax.axis_index("blk")
    head_slot = lax.axis_index("head")
    pair_half = head_slot % 2
    rows_half = queries.shape[2]
    head_dim = queries.shape[3]
    tiles_dev = rows_half // TILE
    tiles_sec = 2 * tiles_dev
    rows_sec = tiles_sec * TILE
    home_data = jnp.stack([queries[0, 0], keys[0, 0], values[0, 0], grad_out[0, 0]])
    partner_data = swapped(home_data, "head", 0)
    section_data = jnp.where(
        pair_half == 0,
        jnp.concatenate([home_data, partner_data], axis=1),
        jnp.concatenate([partner_data, home_data], axis=1),
    )
    sec_kv = section_data[1:3]
    tile_view = section_data.reshape(4, tiles_sec, TILE, head_dim)
    my_work = work_lists[section, head_slot]
    query_rows = tile_view[0][my_work].reshape(rows_half, head_dim)
    grad_rows = tile_view[3][my_work].reshape(rows_half, head_dim)
    my_lists = key_tiles[section * tiles_sec + my_work]
    local_ids = jnp.arange(tiles_sec, dtype=jnp.int32)

    def mask_for(tile_lists, visited):
        return token_mask(tile_matches(tile_lists, visited * tiles_sec + local_ids), TILE)

    start = (
        jnp.full((rows_half,), -1e30, jnp.float32),
        jnp.zeros((rows_half,), jnp.float32),
        jnp.zeros((rows_half, head_dim), jnp.float32),
    )

    def forward_step(cycle_turn, carried):
        key_value, running = carried
        visited = (section - cycle_turn) % cycle_size
        running = forward_turn(query_rows, key_value, mask_for(my_lists, visited), running)
        key_value = from_behind(key_value, "blk", 1)
        return (key_value, running)

    key_value, running = lax.fori_loop(0, cycle_size - 1, forward_step, (sec_kv, start))
    running = forward_turn(
        query_rows, key_value, mask_for(my_lists, (section + 1) % cycle_size), running
    )
    running_top, running_sum, running_out = running
    log_norm = running_top + jnp.log(running_sum)
    attended = running_out / running_sum[:, None]
    delta_rows = jnp.sum(grad_rows.astype(jnp.float32) * attended, axis=1)
    row_stats = jnp.stack([log_norm, delta_rows])
    zero_partials = jnp.zeros((2, rows_sec, head_dim), jnp.float32)
    zero_query = jnp.zeros((rows_half, head_dim), jnp.float32)

    def key_step(cycle_turn, carried):
        key_value, partials, grad_query = carried
        visited = (section + 1 + cycle_turn) % cycle_size
        term_q, term_kv = backward_terms(
            query_rows, grad_rows, row_stats, key_value, mask_for(my_lists, visited)
        )
        key_value = from_behind(key_value, "blk", -1)
        partials = from_behind((partials + term_kv).astype(jnp.bfloat16), "blk", -1).astype(
            jnp.float32
        )
        return (key_value, partials, grad_query + term_q)

    key_value, partials, grad_query = lax.fori_loop(
        0, cycle_size - 1, key_step, (key_value, zero_partials, zero_query)
    )
    term_q, term_kv = backward_terms(
        query_rows, grad_rows, row_stats, key_value, mask_for(my_lists, section)
    )
    partials = partials + term_kv
    grad_query = grad_query + term_q
    outgoing = lax.dynamic_slice_in_dim(partials, (1 - pair_half) * rows_half, rows_half, 1)
    incoming = swapped(outgoing.astype(jnp.bfloat16), "head", 0).astype(outgoing.dtype)
    combined = lax.dynamic_slice_in_dim(partials, pair_half * rows_half, rows_half, 1) + incoming
    softmax_scale = head_dim ** (-0.5)
    grad_keys = (combined[0] * softmax_scale).astype(jnp.bfloat16)
    grad_values = combined[1].astype(jnp.bfloat16)
    grad_queries = (grad_query * softmax_scale).astype(jnp.bfloat16)
    return (grad_queries[None, None], grad_keys[None, None], grad_values[None, None])


def solution(mesh):
    in_specs = (
        P("blk", "head", None, None),
        P("blk", "head", None, None),
        P("blk", "head", None, None),
        P("blk", "head", None, None),
        P(),
        P(),
    )
    out_specs = (
        P("blk", "head", None, None),
        P("blk", "head", None, None),
        P("blk", "head", None, None),
    )
    return jax.shard_map(
        on_device, mesh=mesh, in_specs=in_specs, out_specs=out_specs, check_vma=False
    )
```

profile of v0, /device:TPU:80, one launch (start us, length us, event | category | flops | bytes accessed | tf_op | source)
XLA Modules:
  0.0 812.8 jit_solution(175633787058209929)
XLA Ops:
  12.6 282.2 %while.42 = (s32[]{:T(128)}, bf16[2,512,128]{2,1,0:T(8,128)(2,1)S(1)}, f32[256]{0:T(256)S(1)}, f32[256]{0:T(256)S(1)}, f32[256,128]{1,0:T(8,128)S(1)}, /*index=5...) while((s32[]{:T(128)}, ...), condition=%wide.region_4.5_spmd.clone, body=%wide.region_0.4_spmd.clone.sunk | while | flops 236029696 | bytes 4276842 | solution.py:105
  16.1 18.2 %collective-permute-done = bf16[2,512,128]{2,1,0:T(8,128)(2,1)S(1)} collective-permute-done((bf16[2,512,128]{2,1,0:T(8,128)(2,1)S(1)}, bf16[2,512,128]{2,1,0:T(8,128)(2,1)S(1)}, u32[]{:S(2)}, u32[]{:S(2)}) %collective-permute-start) | collective-permute-done | bytes 262176 | tf_op jit(solution)/shard_map/while/body/eval_jaxpr/ppermute | solution.py:18
  37.8 16.0 %collective-permute-done = bf16[2,512,128]{2,1,0:T(8,128)(2,1)S(1)} collective-permute-done((bf16[2,512,128]{2,1,0:T(8,128)(2,1)S(1)}, bf16[2,512,128]{2,1,0:T(8,128)(2,1)S(1)}, u32[]{:S(2)}, u32[]{:S(2)}) %collective-permute-start) | collective-permute-done | bytes 262176 | tf_op jit(solution)/shard_map/while/body/eval_jaxpr/ppermute | solution.py:18
  57.3 15.0 %collective-permute-done = bf16[2,512,128]{2,1,0:T(8,128)(2,1)S(1)} collective-permute-done((bf16[2,512,128]{2,1,0:T(8,128)(2,1)S(1)}, bf16[2,512,128]{2,1,0:T(8,128)(2,1)S(1)}, u32[]{:S(2)}, u32[]{:S(2)}) %collective-permute-start) | collective-permute-done | bytes 262176 | tf_op jit(solution)/shard_map/while/body/eval_jaxpr/ppermute | solution.py:18
  75.8 15.0 %collective-permute-done = bf16[2,512,128]{2,1,0:T(8,128)(2,1)S(1)} collective-permute-done((bf16[2,512,128]{2,1,0:T(8,128)(2,1)S(1)}, bf16[2,512,128]{2,1,0:T(8,128)(2,1)S(1)}, u32[]{:S(2)}, u32[]{:S(2)}) %collective-permute-start) | collective-permute-done | bytes 262176 | tf_op jit(solution)/shard_map/while/body/eval_jaxpr/ppermute | solution.py:18
  94.4 15.0 %collective-permute-done = bf16[2,512,128]{2,1,0:T(8,128)(2,1)S(1)} collective-permute-done((bf16[2,512,128]{2,1,0:T(8,128)(2,1)S(1)}, bf16[2,512,128]{2,1,0:T(8,128)(2,1)S(1)}, u32[]{:S(2)}, u32[]{:S(2)}) %collective-permute-start) | collective-permute-done | bytes 262176 | tf_op jit(solution)/shard_map/while/body/eval_jaxpr/ppermute | solution.py:18
  112.9 15.0 %collective-permute-done = bf16[2,512,128]{2,1,0:T(8,128)(2,1)S(1)} collective-permute-done((bf16[2,512,128]{2,1,0:T(8,128)(2,1)S(1)}, bf16[2,512,128]{2,1,0:T(8,128)(2,1)S(1)}, u32[]{:S(2)}, u32[]{:S(2)}) %collective-permute-start) | collective-permute-done | bytes 262176 | tf_op jit(solution)/shard_map/while/body/eval_jaxpr/ppermute | solution.py:18
  131.5 15.0 %collective-permute-done = bf16[2,512,128]{2,1,0:T(8,128)(2,1)S(1)} collective-permute-done((bf16[2,512,128]{2,1,0:T(8,128)(2,1)S(1)}, bf16[2,512,128]{2,1,0:T(8,128)(2,1)S(1)}, u32[]{:S(2)}, u32[]{:S(2)}) %collective-permute-start) | collective-permute-done | bytes 262176 | tf_op jit(solution)/shard_map/while/body/eval_jaxpr/ppermute | solution.py:18
  150.0 15.0 %collective-permute-done = bf16[2,512,128]{2,1,0:T(8,128)(2,1)S(1)} collective-permute-done((bf16[2,512,128]{2,1,0:T(8,128)(2,1)S(1)}, bf16[2,512,128]{2,1,0:T(8,128)(2,1)S(1)}, u32[]{:S(2)}, u32[]{:S(2)}) %collective-permute-start) | collective-permute-done | bytes 262176 | tf_op jit(solution)/shard_map/while/body/eval_jaxpr/ppermute | solution.py:18
  168.5 15.0 %collective-permute-done = bf16[2,512,128]{2,1,0:T(8,128)(2,1)S(1)} collective-permute-done((bf16[2,512,128]{2,1,0:T(8,128)(2,1)S(1)}, bf16[2,512,128]{2,1,0:T(8,128)(2,1)S(1)}, u32[]{:S(2)}, u32[]{:S(2)}) %collective-permute-start) | collective-permute-done | bytes 262176 | tf_op jit(solution)/shard_map/while/body/eval_jaxpr/ppermute | solution.py:18
  187.1 15.0 %collective-permute-done = bf16[2,512,128]{2,1,0:T(8,128)(2,1)S(1)} collective-permute-done((bf16[2,512,128]{2,1,0:T(8,128)(2,1)S(1)}, bf16[2,512,128]{2,1,0:T(8,128)(2,1)S(1)}, u32[]{:S(2)}, u32[]{:S(2)}) %collective-permute-start) | collective-permute-done | bytes 262176 | tf_op jit(solution)/shard_map/while/body/eval_jaxpr/ppermute | solution.py:18
  205.6 15.0 %collective-permute-done = bf16[2,512,128]{2,1,0:T(8,128)(2,1)S(1)} collective-permute-done((bf16[2,512,128]{2,1,0:T(8,128)(2,1)S(1)}, bf16[2,512,128]{2,1,0:T(8,128)(2,1)S(1)}, u32[]{:S(2)}, u32[]{:S(2)}) %collective-permute-start) | collective-permute-done | bytes 262176 | tf_op jit(solution)/shard_map/while/body/eval_jaxpr/ppermute | solution.py:18
  224.1 15.0 %collective-permute-done = bf16[2,512,128]{2,1,0:T(8,128)(2,1)S(1)} collective-permute-done((bf16[2,512,128]{2,1,0:T(8,128)(2,1)S(1)}, bf16[2,512,128]{2,1,0:T(8,128)(2,1)S(1)}, u32[]{:S(2)}, u32[]{:S(2)}) %collective-permute-start) | collective-permute-done | bytes 262176 | tf_op jit(solution)/shard_map/while/body/eval_jaxpr/ppermute | solution.py:18
  242.7 15.0 %collective-permute-done = bf16[2,512,128]{2,1,0:T(8,128)(2,1)S(1)} collective-permute-done((bf16[2,512,128]{2,1,0:T(8,128)(2,1)S(1)}, bf16[2,512,128]{2,1,0:T(8,128)(2,1)S(1)}, u32[]{:S(2)}, u32[]{:S(2)}) %collective-permute-start) | collective-permute-done | bytes 262176 | tf_op jit(solution)/shard_map/while/body/eval_jaxpr/ppermute | solution.py:18
  261.2 15.0 %collective-permute-done = bf16[2,512,128]{2,1,0:T(8,128)(2,1)S(1)} collective-permute-done((bf16[2,512,128]{2,1,0:T(8,128)(2,1)S(1)}, bf16[2,512,128]{2,1,0:T(8,128)(2,1)S(1)}, u32[]{:S(2)}, u32[]{:S(2)}) %collective-permute-start) | collective-permute-done | bytes 262176 | tf_op jit(solution)/shard_map/while/body/eval_jaxpr/ppermute | solution.py:18
  279.7 15.0 %collective-permute-done = bf16[2,512,128]{2,1,0:T(8,128)(2,1)S(1)} collective-permute-done((bf16[2,512,128]{2,1,0:T(8,128)(2,1)S(1)}, bf16[2,512,128]{2,1,0:T(8,128)(2,1)S(1)}, u32[]{:S(2)}, u32[]{:S(2)}) %collective-permute-start) | collective-permute-done | bytes 262176 | tf_op jit(solution)/shard_map/while/body/eval_jaxpr/ppermute | solution.py:18
  297.0 506.4 %while.43 = (s32[]{:T(128)}, bf16[2,512,128]{2,1,0:T(8,128)(2,1)S(1)}, f32[2,512,128]{2,1,0:T(8,128)S(1)}, f32[256,128]{1,0:T(8,128)S(1)}, s32[2,32]{1,0:T(2,128...) while((s32[]{:T(128)}, ...), condition=%wide.region_11.12_spmd.clone, body=%wide.region_9.11_spmd.clone.sunk | while | flops 169411072 | bytes 8784545 | solution.py:129
  307.8 34.5 %collective-permute-start.1 = (bf16[2,512,128]{2,1,0:T(8,128)(2,1)S(1)}, bf16[2,512,128]{2,1,0:T(8,128)(2,1)S(1)}, u32[]{:S(2)}, u32[]{:S(2)}) collective-permute-start(bf16[2,512,128]{2,1,0:T(8,128)(2,1)S(1)} %copy.65), channel_id=1, source_target_pairs={{32,0},{64,32},{96,64},{128,96},{160,128},{192,160},{224,192},{256... | collective-permute-start | bytes 786440 | tf_op jit(solution)/shard_map/while/body/eval_jaxpr/ppermute | solution.py:18
  342.6 16.0 %collective-permute-done.1 = bf16[2,512,128]{2,1,0:T(8,128)(2,1)S(1)} collective-permute-done((bf16[2,512,128]{2,1,0:T(8,128)(2,1)S(1)}, bf16[2,512,128]{2,1,0:T(8,128)(2,1)S(1)}, u32[]{:S(2)}, u32[]{:S(2)}) %collective-permute-start.1) | collective-permute-done | bytes 262176 | tf_op jit(solution)/shard_map/while/body/eval_jaxpr/ppermute | solution.py:18
  544.8 20.3 %collective-permute-done.1 = bf16[2,512,128]{2,1,0:T(8,128)(2,1)S(1)} collective-permute-done((bf16[2,512,128]{2,1,0:T(8,128)(2,1)S(1)}, bf16[2,512,128]{2,1,0:T(8,128)(2,1)S(1)}, u32[]{:S(2)}, u32[]{:S(2)}) %collective-permute-start.1) | collective-permute-done | bytes 262176 | tf_op jit(solution)/shard_map/while/body/eval_jaxpr/ppermute | solution.py:18
  581.3 15.7 %collective-permute-start.1 = (bf16[2,512,128]{2,1,0:T(8,128)(2,1)S(1)}, bf16[2,512,128]{2,1,0:T(8,128)(2,1)S(1)}, u32[]{:S(2)}, u32[]{:S(2)}) collective-permute-start(bf16[2,512,128]{2,1,0:T(8,128)(2,1)S(1)} %copy.65), channel_id=1, source_target_pairs={{32,0},{64,32},{96,64},{128,96},{160,128},{192,160},{224,192},{256... | collective-permute-start | bytes 786440 | tf_op jit(solution)/shard_map/while/body/eval_jaxpr/ppermute | solution.py:18
  597.3 16.8 %collective-permute-done.1 = bf16[2,512,128]{2,1,0:T(8,128)(2,1)S(1)} collective-permute-done((bf16[2,512,128]{2,1,0:T(8,128)(2,1)S(1)}, bf16[2,512,128]{2,1,0:T(8,128)(2,1)S(1)}, u32[]{:S(2)}, u32[]{:S(2)}) %collective-permute-start.1) | collective-permute-done | bytes 262176 | tf_op jit(solution)/shard_map/while/body/eval_jaxpr/ppermute | solution.py:18
  630.3 19.5 %collective-permute-start.1 = (bf16[2,512,128]{2,1,0:T(8,128)(2,1)S(1)}, bf16[2,512,128]{2,1,0:T(8,128)(2,1)S(1)}, u32[]{:S(2)}, u32[]{:S(2)}) collective-permute-start(bf16[2,512,128]{2,1,0:T(8,128)(2,1)S(1)} %copy.65), channel_id=1, source_target_pairs={{32,0},{64,32},{96,64},{128,96},{160,128},{192,160},{224,192},{256... | collective-permute-start | bytes 786440 | tf_op jit(solution)/shard_map/while/body/eval_jaxpr/ppermute | solution.py:18
  679.2 23.4 %collective-permute-start.1 = (bf16[2,512,128]{2,1,0:T(8,128)(2,1)S(1)}, bf16[2,512,128]{2,1,0:T(8,128)(2,1)S(1)}, u32[]{:S(2)}, u32[]{:S(2)}) collective-permute-start(bf16[2,512,128]{2,1,0:T(8,128)(2,1)S(1)} %copy.65), channel_id=1, source_target_pairs={{32,0},{64,32},{96,64},{128,96},{160,128},{192,160},{224,192},{256... | collective-permute-start | bytes 786440 | tf_op jit(solution)/shard_map/while/body/eval_jaxpr/ppermute | solution.py:18
  (437 shorter events, 433.9 us)
Async XLA Ops:
  12.6 21.7 %collective-permute-start = (bf16[2,512,128]{2,1,0:T(8,128)(2,1)S(1)}, bf16[2,512,128]{2,1,0:T(8,128)(2,1)S(1)}, u32[]{:S(2)}, u32[]{:S(2)}) collective-permute-start(bf16[2,512,128]{2,1,0:T(8,128)(2,1)S(1)} %copy.51), channel_id=1, source_target_pairs={{480,0},{0,32},{32,64},{64,96},{96,128},{128,160},{160,192},{192,2... | collective-permute-start | bytes 786440 | tf_op jit(solution)/shard_map/while/body/eval_jaxpr/ppermute | solution.py:18
  34.4 19.4 %collective-permute-start = (bf16[2,512,128]{2,1,0:T(8,128)(2,1)S(1)}, bf16[2,512,128]{2,1,0:T(8,128)(2,1)S(1)}, u32[]{:S(2)}, u32[]{:S(2)}) collective-permute-start(bf16[2,512,128]{2,1,0:T(8,128)(2,1)S(1)} %copy.51), channel_id=1, source_target_pairs={{480,0},{0,32},{32,64},{64,96},{96,128},{128,160},{160,192},{192,2... | collective-permute-start | bytes 786440 | tf_op jit(solution)/shard_map/while/body/eval_jaxpr/ppermute | solution.py:18
  53.8 18.5 %collective-permute-start = (bf16[2,512,128]{2,1,0:T(8,128)(2,1)S(1)}, bf16[2,512,128]{2,1,0:T(8,128)(2,1)S(1)}, u32[]{:S(2)}, u32[]{:S(2)}) collective-permute-start(bf16[2,512,128]{2,1,0:T(8,128)(2,1)S(1)} %copy.51), channel_id=1, source_target_pairs={{480,0},{0,32},{32,64},{64,96},{96,128},{128,160},{160,192},{192,2... | collective-permute-start | bytes 786440 | tf_op jit(solution)/shard_map/while/body/eval_jaxpr/ppermute | solution.py:18
  109.4 18.5 %collective-permute-start = (bf16[2,512,128]{2,1,0:T(8,128)(2,1)S(1)}, bf16[2,512,128]{2,1,0:T(8,128)(2,1)S(1)}, u32[]{:S(2)}, u32[]{:S(2)}) collective-permute-start(bf16[2,512,128]{2,1,0:T(8,128)(2,1)S(1)} %copy.51), channel_id=1, source_target_pairs={{480,0},{0,32},{32,64},{64,96},{96,128},{128,160},{160,192},{192,2... | collective-permute-start | bytes 786440 | tf_op jit(solution)/shard_map/while/body/eval_jaxpr/ppermute | solution.py:18
  128.0 18.5 %collective-permute-start = (bf16[2,512,128]{2,1,0:T(8,128)(2,1)S(1)}, bf16[2,512,128]{2,1,0:T(8,128)(2,1)S(1)}, u32[]{:S(2)}, u32[]{:S(2)}) collective-permute-start(bf16[2,512,128]{2,1,0:T(8,128)(2,1)S(1)} %copy.51), channel_id=1, source_target_pairs={{480,0},{0,32},{32,64},{64,96},{96,128},{128,160},{160,192},{192,2... | collective-permute-start | bytes 786440 | tf_op jit(solution)/shard_map/while/body/eval_jaxpr/ppermute | solution.py:18
  146.5 18.5 %collective-permute-start = (bf16[2,512,128]{2,1,0:T(8,128)(2,1)S(1)}, bf16[2,512,128]{2,1,0:T(8,128)(2,1)S(1)}, u32[]{:S(2)}, u32[]{:S(2)}) collective-permute-start(bf16[2,512,128]{2,1,0:T(8,128)(2,1)S(1)} %copy.51), channel_id=1, source_target_pairs={{480,0},{0,32},{32,64},{64,96},{96,128},{128,160},{160,192},{192,2... | collective-permute-start | bytes 786440 | tf_op jit(solution)/shard_map/while/body/eval_jaxpr/ppermute | solution.py:18
  298.5 44.0 %collective-permute-start.2 = (bf16[2,512,128]{2,1,0:T(8,128)(2,1)S(1)}, bf16[2,512,128]{2,1,0:T(8,128)(2,1)S(1)}, u32[]{:S(2)}, u32[]{:S(2)}) collective-permute-start(bf16[2,512,128]{2,1,0:T(8,128)(2,1)S(1)} %fusion.108), channel_id=1, source_target_pairs={{32,0},{64,32},{96,64},{128,96},{160,128},{192,160},{224,192},{256... | collective-permute-start | bytes 786440 | tf_op jit(solution)/shard_map/while/body/eval_jaxpr/ppermute | solution.py:18
  307.8 50.8 %collective-permute-start.1 = (bf16[2,512,128]{2,1,0:T(8,128)(2,1)S(1)}, bf16[2,512,128]{2,1,0:T(8,128)(2,1)S(1)}, u32[]{:S(2)}, u32[]{:S(2)}) collective-permute-start(bf16[2,512,128]{2,1,0:T(8,128)(2,1)S(1)} %copy.65), channel_id=1, source_target_pairs={{32,0},{64,32},{96,64},{128,96},{160,128},{192,160},{224,192},{256... | collective-permute-start | bytes 786440 | tf_op jit(solution)/shard_map/while/body/eval_jaxpr/ppermute | solution.py:18
  360.1 19.9 %collective-permute-start.2 = (bf16[2,512,128]{2,1,0:T(8,128)(2,1)S(1)}, bf16[2,512,128]{2,1,0:T(8,128)(2,1)S(1)}, u32[]{:S(2)}, u32[]{:S(2)}) collective-permute-start(bf16[2,512,128]{2,1,0:T(8,128)(2,1)S(1)} %fusion.108), channel_id=1, source_target_pairs={{32,0},{64,32},{96,64},{128,96},{160,128},{192,160},{224,192},{256... | collective-permute-start | bytes 786440 | tf_op jit(solution)/shard_map/while/body/eval_jaxpr/ppermute | solution.py:18
  384.4 20.5 %collective-permute-start.2 = (bf16[2,512,128]{2,1,0:T(8,128)(2,1)S(1)}, bf16[2,512,128]{2,1,0:T(8,128)(2,1)S(1)}, u32[]{:S(2)}, u32[]{:S(2)}) collective-permute-start(bf16[2,512,128]{2,1,0:T(8,128)(2,1)S(1)} %fusion.108), channel_id=1, source_target_pairs={{32,0},{64,32},{96,64},{128,96},{160,128},{192,160},{224,192},{256... | collective-permute-start | bytes 786440 | tf_op jit(solution)/shard_map/while/body/eval_jaxpr/ppermute | solution.py:18
  409.1 22.9 %collective-permute-start.2 = (bf16[2,512,128]{2,1,0:T(8,128)(2,1)S(1)}, bf16[2,512,128]{2,1,0:T(8,128)(2,1)S(1)}, u32[]{:S(2)}, u32[]{:S(2)}) collective-permute-start(bf16[2,512,128]{2,1,0:T(8,128)(2,1)S(1)} %fusion.108), channel_id=1, source_target_pairs={{32,0},{64,32},{96,64},{128,96},{160,128},{192,160},{224,192},{256... | collective-permute-start | bytes 786440 | tf_op jit(solution)/shard_map/while/body/eval_jaxpr/ppermute | solution.py:18
  436.4 20.1 %collective-permute-start.2 = (bf16[2,512,128]{2,1,0:T(8,128)(2,1)S(1)}, bf16[2,512,128]{2,1,0:T(8,128)(2,1)S(1)}, u32[]{:S(2)}, u32[]{:S(2)}) collective-permute-start(bf16[2,512,128]{2,1,0:T(8,128)(2,1)S(1)} %fusion.108), channel_id=1, source_target_pairs={{32,0},{64,32},{96,64},{128,96},{160,128},{192,160},{224,192},{256... | collective-permute-start | bytes 786440 | tf_op jit(solution)/shard_map/while/body/eval_jaxpr/ppermute | solution.py:18
  461.0 25.6 %collective-permute-start.2 = (bf16[2,512,128]{2,1,0:T(8,128)(2,1)S(1)}, bf16[2,512,128]{2,1,0:T(8,128)(2,1)S(1)}, u32[]{:S(2)}, u32[]{:S(2)}) collective-permute-start(bf16[2,512,128]{2,1,0:T(8,128)(2,1)S(1)} %fusion.108), channel_id=1, source_target_pairs={{32,0},{64,32},{96,64},{128,96},{160,128},{192,160},{224,192},{256... | collective-permute-start | bytes 786440 | tf_op jit(solution)/shard_map/while/body/eval_jaxpr/ppermute | solution.py:18
  491.0 20.2 %collective-permute-start.2 = (bf16[2,512,128]{2,1,0:T(8,128)(2,1)S(1)}, bf16[2,512,128]{2,1,0:T(8,128)(2,1)S(1)}, u32[]{:S(2)}, u32[]{:S(2)}) collective-permute-start(bf16[2,512,128]{2,1,0:T(8,128)(2,1)S(1)} %fusion.108), channel_id=1, source_target_pairs={{32,0},{64,32},{96,64},{128,96},{160,128},{192,160},{224,192},{256... | collective-permute-start | bytes 786440 | tf_op jit(solution)/shard_map/while/body/eval_jaxpr/ppermute | solution.py:18
  515.6 29.1 %collective-permute-start.2 = (bf16[2,512,128]{2,1,0:T(8,128)(2,1)S(1)}, bf16[2,512,128]{2,1,0:T(8,128)(2,1)S(1)}, u32[]{:S(2)}, u32[]{:S(2)}) collective-permute-start(bf16[2,512,128]{2,1,0:T(8,128)(2,1)S(1)} %fusion.108), channel_id=1, source_target_pairs={{32,0},{64,32},{96,64},{128,96},{160,128},{192,160},{224,192},{256... | collective-permute-start | bytes 786440 | tf_op jit(solution)/shard_map/while/body/eval_jaxpr/ppermute | solution.py:18
  530.3 34.9 %collective-permute-start.1 = (bf16[2,512,128]{2,1,0:T(8,128)(2,1)S(1)}, bf16[2,512,128]{2,1,0:T(8,128)(2,1)S(1)}, u32[]{:S(2)}, u32[]{:S(2)}) collective-permute-start(bf16[2,512,128]{2,1,0:T(8,128)(2,1)S(1)} %copy.65), channel_id=1, source_target_pairs={{32,0},{64,32},{96,64},{128,96},{160,128},{192,160},{224,192},{256... | collective-permute-start | bytes 786440 | tf_op jit(solution)/shard_map/while/body/eval_jaxpr/ppermute | solution.py:18
  566.6 30.6 %collective-permute-start.2 = (bf16[2,512,128]{2,1,0:T(8,128)(2,1)S(1)}, bf16[2,512,128]{2,1,0:T(8,128)(2,1)S(1)}, u32[]{:S(2)}, u32[]{:S(2)}) collective-permute-start(bf16[2,512,128]{2,1,0:T(8,128)(2,1)S(1)} %fusion.108), channel_id=1, source_target_pairs={{32,0},{64,32},{96,64},{128,96},{160,128},{192,160},{224,192},{256... | collective-permute-start | bytes 786440 | tf_op jit(solution)/shard_map/while/body/eval_jaxpr/ppermute | solution.py:18
  581.3 32.8 %collective-permute-start.1 = (bf16[2,512,128]{2,1,0:T(8,128)(2,1)S(1)}, bf16[2,512,128]{2,1,0:T(8,128)(2,1)S(1)}, u32[]{:S(2)}, u32[]{:S(2)}) collective-permute-start(bf16[2,512,128]{2,1,0:T(8,128)(2,1)S(1)} %copy.65), channel_id=1, source_target_pairs={{32,0},{64,32},{96,64},{128,96},{160,128},{192,160},{224,192},{256... | collective-permute-start | bytes 786440 | tf_op jit(solution)/shard_map/while/body/eval_jaxpr/ppermute | solution.py:18
  615.6 34.5 %collective-permute-start.2 = (bf16[2,512,128]{2,1,0:T(8,128)(2,1)S(1)}, bf16[2,512,128]{2,1,0:T(8,128)(2,1)S(1)}, u32[]{:S(2)}, u32[]{:S(2)}) collective-permute-start(bf16[2,512,128]{2,1,0:T(8,128)(2,1)S(1)} %fusion.108), channel_id=1, source_target_pairs={{32,0},{64,32},{96,64},{128,96},{160,128},{192,160},{224,192},{256... | collective-permute-start | bytes 786440 | tf_op jit(solution)/shard_map/while/body/eval_jaxpr/ppermute | solution.py:18
  630.3 32.7 %collective-permute-start.1 = (bf16[2,512,128]{2,1,0:T(8,128)(2,1)S(1)}, bf16[2,512,128]{2,1,0:T(8,128)(2,1)S(1)}, u32[]{:S(2)}, u32[]{:S(2)}) collective-permute-start(bf16[2,512,128]{2,1,0:T(8,128)(2,1)S(1)} %copy.65), channel_id=1, source_target_pairs={{32,0},{64,32},{96,64},{128,96},{160,128},{192,160},{224,192},{256... | collective-permute-start | bytes 786440 | tf_op jit(solution)/shard_map/while/body/eval_jaxpr/ppermute | solution.py:18
  664.5 38.3 %collective-permute-start.2 = (bf16[2,512,128]{2,1,0:T(8,128)(2,1)S(1)}, bf16[2,512,128]{2,1,0:T(8,128)(2,1)S(1)}, u32[]{:S(2)}, u32[]{:S(2)}) collective-permute-start(bf16[2,512,128]{2,1,0:T(8,128)(2,1)S(1)} %fusion.108), channel_id=1, source_target_pairs={{32,0},{64,32},{96,64},{128,96},{160,128},{192,160},{224,192},{256... | collective-permute-start | bytes 786440 | tf_op jit(solution)/shard_map/while/body/eval_jaxpr/ppermute | solution.py:18
  679.2 32.6 %collective-permute-start.1 = (bf16[2,512,128]{2,1,0:T(8,128)(2,1)S(1)}, bf16[2,512,128]{2,1,0:T(8,128)(2,1)S(1)}, u32[]{:S(2)}, u32[]{:S(2)}) collective-permute-start(bf16[2,512,128]{2,1,0:T(8,128)(2,1)S(1)} %copy.65), channel_id=1, source_target_pairs={{32,0},{64,32},{96,64},{128,96},{160,128},{192,160},{224,192},{256... | collective-permute-start | bytes 786440 | tf_op jit(solution)/shard_map/while/body/eval_jaxpr/ppermute | solution.py:18
  736.2 18.6 %collective-permute-start.2 = (bf16[2,512,128]{2,1,0:T(8,128)(2,1)S(1)}, bf16[2,512,128]{2,1,0:T(8,128)(2,1)S(1)}, u32[]{:S(2)}, u32[]{:S(2)}) collective-permute-start(bf16[2,512,128]{2,1,0:T(8,128)(2,1)S(1)} %fusion.108), channel_id=1, source_target_pairs={{32,0},{64,32},{96,64},{128,96},{160,128},{192,160},{224,192},{256... | collective-permute-start | bytes 786440 | tf_op jit(solution)/shard_map/while/body/eval_jaxpr/ppermute | solution.py:18
  759.1 18.6 %collective-permute-start.2 = (bf16[2,512,128]{2,1,0:T(8,128)(2,1)S(1)}, bf16[2,512,128]{2,1,0:T(8,128)(2,1)S(1)}, u32[]{:S(2)}, u32[]{:S(2)}) collective-permute-start(bf16[2,512,128]{2,1,0:T(8,128)(2,1)S(1)} %fusion.108), channel_id=1, source_target_pairs={{32,0},{64,32},{96,64},{128,96},{160,128},{192,160},{224,192},{256... | collective-permute-start | bytes 786440 | tf_op jit(solution)/shard_map/while/body/eval_jaxpr/ppermute | solution.py:18
  (29 other events, 345.5 us)
where the time goes:
time: 815 us; the launch traced here: 813 us
  starting transfers between devices  376 us (46%)
  waiting for transfers between devices  376 us (46%)
  matrix products  35 us (4%)
  other arithmetic  14.2 us (2%)
  local copies, waits for them, and re-layouts  8.36 us (1%)
    ppermute x45, starting transfers between devices, from_behind(): return lax.ppermute(block, axis, route)  370 us
    ppermute x45, waiting for transfers between devices, from_behind(): return lax.ppermute(block, axis, route)  367 us
  transfers between devices with their start and end apart: 47, of which 42 were waited for; matrix products, arithmetic and copies ran while one was open for 4% of the time, Pallas kernels for 0%

commit v1 on v0

v1 whole, which is shorter than its diff:
```python
import functools

import jax
import jax.numpy as jnp
from jax import lax
from jax.experimental import pallas as pl
from jax.experimental.pallas import tpu as pltpu
from jax.sharding import Mesh, PartitionSpec as P

TILE = 128
HD = 128
HALF = 256
NX = 4
NCHUNK = 4
BLOCKS = 2 * NX
ROWS = BLOCKS * HALF
SCALE = HD**-0.5
SCALE2 = SCALE * 1.4426950408889634
FAR = 1e30


def dot_t(a, b):
    return lax.dot_general(a, b, (((1,), (1,)), ((), ())), preferred_element_type=jnp.float32)


def dot_n(a, b):
    return jnp.dot(a, b, preferred_element_type=jnp.float32)


def mask_kernel(tiles_ref, across_ref, far_ref, live_ref, same_ref, table_ref):
    x, zh, core, half = (lax.axis_index(name) for name in ("x", "zh", "c", "p"))
    tiles = tiles_ref[...]
    for k in range(2 * NCHUNK):
        chunk_zh = zh if k // 2 % 2 == 0 else 1 - zh
        chunk_core = core if k // 4 == 0 else 1 - core
        key_id = (4 * x + 2 * chunk_zh + chunk_core) * 4 + 2 * half + k % 2
        hit = jnp.where(tiles == key_id, 0.0, FAR)
        table_ref[k] = jnp.broadcast_to(jnp.min(hit, axis=1, keepdims=True), (64, TILE))
    for n in range(NX):
        first = (4 * n + 2 * zh + core) * 4
        nearest = jnp.full((4, TILE), FAR, jnp.float32)
        for k in range(2 * NCHUNK):
            four = table_ref[k, pl.ds(first, 4), :]
            nearest = jnp.minimum(nearest, four)
            for h in range(2):
                far_ref[n, h, k : k + 1, :TILE] = four[2 * h : 2 * h + 1]
                far_ref[n, h, k : k + 1, TILE:] = four[2 * h + 1 : 2 * h + 2]
        live_ref[n] = (jnp.min(nearest) < 1.0).astype(jnp.int32)


def stats_kernel(
    live_ref, qg_ref, own_ref, across_ref, core_ref, core_across_ref, far_ref, out_ref
):
    chunks = (own_ref, across_ref, core_ref, core_across_ref)

    def group(n, carry):
        @pl.when(live_ref[n] > 0)
        def _():
            for h in range(2):
                q = qg_ref[n, h, 0]
                g = qg_ref[n, h, 1]
                far = far_ref[n, h]
                scores = []
                top = jnp.full((1, HALF), -FAR, jnp.float32)
                for i, chunk in enumerate(chunks):
                    s = dot_t(chunk[0], q)
                    for t in range(2):
                        st = s[t * TILE : (t + 1) * TILE]
                        scores.append(st)
                        k = 2 * i + t
                        near = jnp.max(st, axis=0, keepdims=True) - far[k : k + 1]
                        top = jnp.maximum(top, near)
                top = top * SCALE2
                total = jnp.zeros((1, HALF), jnp.float32)
                weighted = jnp.zeros((1, HALF), jnp.float32)
                for i, chunk in enumerate(chunks):
                    gp = dot_t(chunk[1], g)
                    for t in range(2):
                        k = 2 * i + t
                        e = jnp.exp2(scores[k] * SCALE2 - (top + 4.0 * far[k : k + 1]))
                        total = total + jnp.sum(e, axis=0, keepdims=True)
                        weighted = weighted + jnp.sum(
                            e * gp[t * TILE : (t + 1) * TILE], axis=0, keepdims=True
                        )
                some = total > 0.0
                safe = jnp.where(some, total, 1.0)
                lse = jnp.where(some, top + jnp.log2(safe), -FAR)
                mean = jnp.where(some, weighted / safe, 0.0)
                for j in range(BLOCKS):
                    out_ref[j, n, h, :, :HALF] = lse
                    out_ref[j, n, h, :, HALF:] = mean

        @pl.when(live_ref[n] == 0)
        def _():
            for j in range(BLOCKS):
                for h in range(2):
                    out_ref[j, n, h, :, :HALF] = jnp.full((1, HALF), -FAR, jnp.float32)
                    out_ref[j, n, h, :, HALF:] = jnp.zeros((1, HALF), jnp.float32)

        return carry

    lax.fori_loop(0, NX, group, 0)


def grads_kernel(
    live_ref,
    work_ref,
    qg_ref,
    own_ref,
    across_ref,
    core_ref,
    core_across_ref,
    far_ref,
    stats_ref,
    keep_ref,
    send_ref,
    dq_ref,
    dk_acc,
    dv_acc,
    kt_ref,
    ds_ref,
):
    zh, core, head = (lax.axis_index(name) for name in ("zh", "c", "n"))
    chunks = (own_ref, across_ref, core_ref, core_across_ref)
    dk_acc[...] = jnp.zeros_like(dk_acc)
    dv_acc[...] = jnp.zeros_like(dv_acc)
    for i, chunk in enumerate(chunks):
        kt_ref[:, i * HALF : (i + 1) * HALF] = chunk[0].T

    def group(n, carry):
        section = 4 * n + 2 * zh + core

        def slot(wanted):
            found = jnp.int32(3)
            for w in range(3):
                found = jnp.where(work_ref[section, 4 * head + w] == wanted, w, found)
            return found

        @pl.when(live_ref[n] > 0)
        def _():
            q_all = qg_ref[n, :, 0].reshape(2 * HALF, HD)
            g_all = qg_ref[n, :, 1].reshape(2 * HALF, HD)
            rows_stats = []
            for h in range(2):
                lse_parts = [stats_ref[j, n, h, :, :HALF] for j in range(BLOCKS)]
                top = functools.reduce(jnp.maximum, lse_parts)
                total = jnp.zeros((1, HALF), jnp.float32)
                weighted = jnp.zeros((1, HALF), jnp.float32)
                for j in range(BLOCKS):
                    w = jnp.exp2(lse_parts[j] - top)
                    total = total + w
                    weighted = weighted + w * stats_ref[j, n, h, :, HALF:]
                rows_stats.append((top + jnp.log2(total), weighted / total))
            for i, chunk in enumerate(chunks):
                rows = slice(i * HALF, (i + 1) * HALF)
                ps, ds = [], []
                for h in range(2):
                    lse, delta = rows_stats[h]
                    s = dot_t(chunk[0], qg_ref[n, h, 0])
                    gp = dot_t(chunk[1], qg_ref[n, h, 1])
                    p_parts, d_parts = [], []
                    for t in range(2):
                        k = 2 * i + t
                        part = slice(t * TILE, (t + 1) * TILE)
                        shift = lse + 4.0 * far_ref[n, h, k : k + 1, :]
                        p = jnp.exp2(s[part] * SCALE2 - shift)
                        p_parts.append(p.astype(jnp.bfloat16))
                        d_parts.append((p * (gp[part] - delta)).astype(jnp.bfloat16))
                    ps.append(jnp.concatenate(p_parts, axis=0))
                    d = jnp.concatenate(d_parts, axis=0)
                    ds.append(d)
                    ds_ref[h, rows] = d
                dv_acc[rows] += dot_n(jnp.concatenate(ps, axis=1), g_all)
                dk_acc[rows] += dot_n(jnp.concatenate(ds, axis=1), q_all)
            for h in range(2):
                dq = (dot_n(kt_ref[...], ds_ref[h]) * SCALE).T.astype(jnp.bfloat16)
                dq_ref[n, slot(2 * h)] = dq[:TILE]
                dq_ref[n, slot(2 * h + 1)] = dq[TILE:]

        @pl.when(live_ref[n] == 0)
        def _():
            dq_ref[n] = jnp.zeros((4, TILE, HD), jnp.bfloat16)

        return carry

    lax.fori_loop(0, NX, group, 0)
    for i in range(2):
        rows = slice(i * HALF, (i + 1) * HALF)
        keep_ref[i, 0] = dk_acc[rows] * SCALE
        keep_ref[i, 1] = dv_acc[rows]
        rows = slice((i + 2) * HALF, (i + 3) * HALF)
        send_ref[i, 0] = (dk_acc[rows] * SCALE).astype(jnp.bfloat16)
        send_ref[i, 1] = dv_acc[rows].astype(jnp.bfloat16)


VMEM = pl.BlockSpec(memory_space=pltpu.VMEM)
SMEM = pl.BlockSpec(memory_space=pltpu.SMEM)


def flipped(value, axis):
    return lax.ppermute(value, axis, [(0, 1), (1, 0)])


def run_masks(tiles, across):
    return pl.pallas_call(
        mask_kernel,
        out_shape=[
            jax.ShapeDtypeStruct((NX, 2, 2 * NCHUNK, HALF), jnp.float32),
            jax.ShapeDtypeStruct((NX,), jnp.int32),
            jax.ShapeDtypeStruct(across.shape, across.dtype),
        ],
        in_specs=[VMEM, pl.BlockSpec(memory_space=pl.ANY)],
        out_specs=[VMEM, SMEM, pl.BlockSpec(memory_space=pl.ANY)],
        input_output_aliases={1: 2},
        scratch_shapes=[pltpu.VMEM((2 * NCHUNK, 64, TILE), jnp.float32)],
        compiler_params=pltpu.CompilerParams(vmem_limit_bytes=8 * 1024 * 1024),
        cost_estimate=pl.CostEstimate(flops=10**11, bytes_accessed=2**20, transcendentals=0),
        name="masks",
    )(tiles, across)


def run_stats(live, qg, kv, far):
    return pl.pallas_call(
        stats_kernel,
        out_shape=jax.ShapeDtypeStruct((BLOCKS, NX, 2, 1, 2 * HALF), jnp.float32),
        in_specs=[SMEM] + [VMEM] * 6,
        out_specs=VMEM,
        compiler_params=pltpu.CompilerParams(vmem_limit_bytes=32 * 1024 * 1024),
        cost_estimate=pl.CostEstimate(flops=10**9, bytes_accessed=2**21, transcendentals=2**21),
        name="stats",
    )(live, qg, *kv, far)


def run_grads(live, work, qg, kv, far, stats):
    return pl.pallas_call(
        grads_kernel,
        out_shape=[
            jax.ShapeDtypeStruct((2, 2, HALF, HD), jnp.float32),
            jax.ShapeDtypeStruct((2, 2, HALF, HD), jnp.bfloat16),
            jax.ShapeDtypeStruct((NX, 4, TILE, HD), jnp.bfloat16),
        ],
        in_specs=[SMEM, SMEM] + [VMEM] * 7,
        out_specs=[VMEM] * 3,
        scratch_shapes=[
            pltpu.VMEM((NCHUNK * HALF, HD), jnp.float32),
            pltpu.VMEM((NCHUNK * HALF, HD), jnp.float32),
            pltpu.VMEM((HD, NCHUNK * HALF), jnp.bfloat16),
            pltpu.VMEM((2, NCHUNK * HALF, HALF), jnp.bfloat16),
        ],
        compiler_params=pltpu.CompilerParams(vmem_limit_bytes=24 * 1024 * 1024),
        cost_estimate=pl.CostEstimate(flops=2 * 10**9, bytes_accessed=2**21, transcendentals=2**21),
        name="grads",
    )(live, work, qg, *kv, far, stats)


def finish_kernel(mine_ref, across_ref, dk_ref, dv_ref):
    dk_ref[...] = (mine_ref[0] + across_ref[0].astype(jnp.float32)).astype(jnp.bfloat16)
    dv_ref[...] = (mine_ref[1] + across_ref[1].astype(jnp.float32)).astype(jnp.bfloat16)


def run_finish(mine, across):
    return pl.pallas_call(
        finish_kernel,
        out_shape=[jax.ShapeDtypeStruct((HALF, HD), jnp.bfloat16)] * 2,
        in_specs=[VMEM, VMEM],
        out_specs=[VMEM, VMEM],
        compiler_params=pltpu.CompilerParams(vmem_limit_bytes=8 * 1024 * 1024),
        cost_estimate=pl.CostEstimate(flops=10**11, bytes_accessed=2**20, transcendentals=0),
        name="finish",
    )(mine, across)


def on_device(queries, keys, values, grad_out, key_tiles, work_lists):
    own_qg = jnp.stack([queries[0, 0], grad_out[0, 0]])
    both_qg = lax.all_gather(own_qg, "p")
    own_kv = jnp.stack([keys[0, 0], values[0, 0]])
    own_kv, both_qg = lax.optimization_barrier((own_kv, both_qg))
    across_kv = flipped(own_kv, "zh")
    core_kv = flipped(own_kv, "c")
    spread = jnp.broadcast_to(both_qg[None], (NX,) + both_qg.shape)
    all_qg = lax.all_to_all(spread, "x", 0, 0)
    far, live, across_kv = run_masks(key_tiles, across_kv)
    core_across_kv = flipped(across_kv, "c")
    work = work_lists.reshape(16, 64)
    kv = (own_kv, across_kv, core_kv, core_across_kv)

    stats = run_stats(live, all_qg, kv, far)
    stats = lax.all_to_all(stats, ("x", "p"), 0, 0)
    keep, send, dq = run_grads(live, work, all_qg, kv, far, stats)

    total = keep + flipped(send, "c").astype(jnp.float32)
    dkv_out = total[1].astype(jnp.bfloat16)
    from_across = flipped(dkv_out, "zh")
    dq_parts = lax.all_to_all(dq, "x", 0, 0)
    dq_sum = jnp.sum(dq_parts.astype(jnp.float32), axis=0).astype(jnp.bfloat16)
    dq_sum = lax.all_to_all(dq_sum.reshape(2, HALF, HD), "p", 0, 0)
    grad_queries = jnp.sum(dq_sum.astype(jnp.float32), axis=0).astype(jnp.bfloat16)
    grad_keys, grad_values = run_finish(total[0], from_across)
    return grad_queries[None, None], grad_keys[None, None], grad_values[None, None]


def solution(mesh):
    devices = mesh.devices.reshape(4, 2, 2, 16, 2)
    fine = Mesh(devices, ("x", "zh", "c", "n", "p"))
    spec = P(("x", "zh", "c"), ("n", "p"), None, None)
    return jax.shard_map(
        on_device,
        mesh=fine,
        in_specs=(spec, spec, spec, spec, P(), P()),
        out_specs=(spec, spec, spec),
        check_vma=False,
    )
```

time: 815 us -> 99.5 us (0.12)
  the two profiles are of different devices: /device:TPU:80 before, /device:TPU:58 now
where the time goes in v1:
time: 99.5 us; the launch traced here: 98.8 us
  starting transfers between devices  44.6 us (45%)
  waiting for transfers between devices  29.1 us (29%)
  Pallas kernels  14.4 us (14%)
  blocking collectives  6.05 us (6%)
  other arithmetic  2.33 us (2%)
  local copies, waits for them, and re-layouts  1.48 us (1%)
    ppermute x5, starting transfers between devices, flipped(): return lax.ppermute(value, axis, [(0, 1), (1, 0)])  26.8 us
    ppermute x5, waiting for transfers between devices, flipped(): return lax.ppermute(value, axis, [(0, 1), (1, 0)])  15.1 us
    pallas_call x1, Pallas kernels, run_grads(): pl.pallas_call(grads_kernel, out_shape=[jax.ShapeDtypeStruct((2, 2, HALF,...  7.81 us
    all_to_all x1, waiting for transfers between devices, on_device(): all_qg = lax.all_to_all(spread, 'x', 0, 0)  7.25 us
    all_gather x1, blocking collectives, on_device(): both_qg = lax.all_gather(own_qg, 'p')  6.05 us
    pallas_call x1, Pallas kernels, run_stats(): pl.pallas_call(stats_kernel, out_shape=jax.ShapeDtypeStruct((BLOCKS, NX,...  5.07 us
    all_to_all x1, starting transfers between devices, on_device(): dq_sum = lax.all_to_all(dq_sum.reshape(2, HALF, HD), 'p', 0, 0)  5 us
    all_to_all x1, starting transfers between devices, on_device(): all_qg = lax.all_to_all(spread, 'x', 0, 0)  4.96 us
  transfers between devices with their start and end apart: 9, of which 6 were waited for; matrix products, arithmetic and copies ran while one was open for 2% of the time, Pallas kernels for 2%

profile of v1, /device:TPU:58, one launch (start us, length us, event | category | flops | bytes accessed | tf_op | source)
XLA Modules:
  0.0 98.8 jit_solution(16904311539156873043)
XLA Ops:
  0.6 0.9 pad_maximum_fusion.1
  1.5 6.0 %all-gather = bf16[4,256,128]{2,1,0:T(8,128)(2,1)S(1)} all-gather(bf16[2,256,128]{2,1,0:T(8,128)(2,1)S(1)} %pad_maximum_fusion.1), channel_id=2, replica_groups=mesh['x'=4,'zh'=2,'c'=2,'n'=16,'p'=2] {'p'}, dimensions={0}, use_global_device_ids=true | all-gather | bytes 393216 | tf_op jit(solution)/shard_map/all_gather | solution.py:275
  7.6 14.8 %collective-permute-start = (bf16[2,256,128]{2,1,0:T(8,128)(2,1)S(1)}, bf16[2,256,128]{2,1,0:T(8,128)(2,1)S(1)}, u32[]{:S(2)}, u32[]{:S(2)}) collective-permute-start(bf16[2,256,128]{2,1,0:T(8,128)(2,1)S(1)} %pad_maximum_fusion.own_ref), channel_id=1, source_target_pairs={{0,64},{64,0},{1,65},{65,1},{2,66},{66,2},{3,67},{67,3},{4,68},{68... | collective-permute-start | bytes 393224 | tf_op jit(solution)/shard_map/ppermute | solution.py:201
  22.4 1.9 %collective-permute-start.1 = (bf16[2,256,128]{2,1,0:T(8,128)(2,1)S(1)}, bf16[2,256,128]{2,1,0:T(8,128)(2,1)S(1)}, u32[]{:S(2)}, u32[]{:S(2)}) collective-permute-start(bf16[2,256,128]{2,1,0:T(8,128)(2,1)S(1)} %pad_maximum_fusion.own_ref), channel_id=1, source_target_pairs={{0,32},{32,0},{1,33},{33,1},{2,34},{34,2},{3,35},{35,3},{4,36},{36... | collective-permute-start | bytes 393224 | tf_op jit(solution)/shard_map/ppermute | solution.py:201
  24.4 1.2 %broadcast_in_dim.15 = bf16[4,2,2,256,128]{4,3,2,1,0:T(8,128)(2,1)} broadcast(bf16[2,2,256,128]{3,2,1,0:T(8,128)(2,1)S(1)} %bitcast.14), dimensions={1,2,3,4} | broadcast | bytes 1310720 | tf_op jit(solution)/shard_map/broadcast_in_dim | solution.py:280
  25.6 5.0 %all-to-all-start = ((bf16[4,2,2,256,128]{4,3,2,1,0:T(8,128)(2,1)}), bf16[4,2,2,256,128]{4,3,2,1,0:T(8,128)(2,1)S(1)}, u32[]{:S(2)}, u32[]{:S(2)}) async-start(bf16[4,2,2,256,128]{4,3,2,1,0:T(8,128)(2,1)} %broadcast_in_dim.15), calls=%async_computation | async-start | bytes 2097152 | tf_op jit(solution)/shard_map/all_to_all | solution.py:281
  30.6 2.8 %collective-permute-done.across_ref = bf16[2,256,128]{2,1,0:T(8,128)(2,1)S(1)} collective-permute-done((bf16[2,256,128]{2,1,0:T(8,128)(2,1)S(1)}, bf16[2,256,128]{2,1,0:T(8,128)(2,1)S(1)}, u32[]{:S(2)}, u32[]{:S(2)}) %collective-permute-start) | collective-permute-done | bytes 131104 | tf_op jit(solution)/shard_map/ppermute | solution.py:201
  33.4 0.9 masks.1
  34.3 1.9 %collective-permute-start.2 = (bf16[2,256,128]{2,1,0:T(8,128)(2,1)S(1)}, bf16[2,256,128]{2,1,0:T(8,128)(2,1)S(1)}, u32[]{:S(2)}, u32[]{:S(2)}) collective-permute-start(bf16[2,256,128]{2,1,0:T(8,128)(2,1)S(1)} %get-tuple-element.16.across_ref), channel_id=1, source_target_pairs={{0,32},{32,0},{1,33},{33,1},{2,34},{34,2},{3,35},{35,3},{4,36},{36... | collective-permute-start | bytes 393224 | tf_op jit(solution)/shard_map/ppermute | solution.py:201
  36.3 1.3 %collective-permute-done.2.core_across_ref = bf16[2,256,128]{2,1,0:T(8,128)(2,1)S(1)} collective-permute-done((bf16[2,256,128]{2,1,0:T(8,128)(2,1)S(1)}, bf16[2,256,128]{2,1,0:T(8,128)(2,1)S(1)}, u32[]{:S(2)}, u32[]{:S(2)}) %collective-permute-start.2) | collective-permute-done | bytes 131104 | tf_op jit(solution)/shard_map/ppermute | solution.py:201
  37.6 7.2 %all-to-all-done.qg_ref = bf16[4,2,2,256,128]{4,3,2,1,0:T(8,128)(2,1)S(1)} async-done(((bf16[4,2,2,256,128]{4,3,2,1,0:T(8,128)(2,1)}), bf16[4,2,2,256,128]{4,3,2,1,0:T(8,128)(2,1)S(1)}, u32[]{:S(2)}, u32[]{:S(2)}) %all-to-all-start) | async-done | bytes 1048608 | tf_op jit(solution)/shard_map/all_to_all | solution.py:281
  44.8 5.1 %stats.1 = f32[8,4,2,1,512]{4,3,2,1,0:T(1,128)} custom-call(s32[4]{0:T(128)S(1)} %get-tuple-element.14.live_ref, bf16[4,2,2,256,128]{4,3,2,1,0:T(8,128)(2,1)S(1)} %all-to-all-done.qg_ref, bf16[2,256,128]{2,1,0:T(8,128)(2,1)S(1)} %pad_maximum_fusion.own_ref, bf16[2,256,128]{2,1,0:T(8,128)(2,1)S(1)} %get-tuple-element.16.across_ref, ...), custom_call_target="tpu_custom_call" | custom-call | flops 1000000000 | bytes 2097152 | tf_op jit(solution)/shard_map/stats/pallas_call | solution.py:223
  49.9 4.3 %all-to-all-start.1 = ((f32[8,4,2,1,512]{4,3,2,1,0:T(1,128)}), f32[8,4,2,1,512]{4,3,2,1,0:T(1,128)S(1)}, u32[]{:S(2)}, u32[]{:S(2)}) async-start(f32[8,4,2,1,512]{4,3,2,1,0:T(1,128)} %stats.1), calls=%async_computation.1 | async-start | bytes 262144 | tf_op jit(solution)/shard_map/all_to_all | solution.py:288
  54.4 4.4 %all-to-all-done.1.stats_ref = f32[8,4,2,1,512]{4,3,2,1,0:T(1,128)S(1)} async-done(((f32[8,4,2,1,512]{4,3,2,1,0:T(1,128)}), f32[8,4,2,1,512]{4,3,2,1,0:T(1,128)S(1)}, u32[]{:S(2)}, u32[]{:S(2)}) %all-to-all-start.1) | async-done | bytes 131104 | tf_op jit(solution)/shard_map/all_to_all | solution.py:288
  58.7 7.8 %grads.1 = (f32[2,2,256,128]{3,2,1,0:T(8,128)S(1)}, bf16[2,2,256,128]{3,2,1,0:T(8,128)(2,1)S(1)}, bf16[4,4,128,128]{3,2,1,0:T(8,128)(2,1)}) custom-call(s32[4]{0:T(128)S(1)} %get-tuple-element.14.live_ref, s32[16,64]{1,0:T(8,128)S(1)} %copy.20.work_ref, bf16[4,2,2,256,128]{4,3,2,1,0:T(8,128)(2,1)S(1)} %all-to-all-done.qg_ref, ...), custom_call_target="tpu_custom_call" | custom-call | flops 2000000000 | bytes 2097152 | tf_op jit(solution)/shard_map/grads/pallas_call | solution.py:235
  66.6 1.9 %collective-permute-start.3 = (bf16[2,2,256,128]{3,2,1,0:T(8,128)(2,1)S(1)}, bf16[2,2,256,128]{3,2,1,0:T(8,128)(2,1)S(1)}, u32[]{:S(2)}, u32[]{:S(2)}) collective-permute-start(bf16[2,2,256,128]{3,2,1,0:T(8,128)(2,1)S(1)} %get-tuple-element.20), channel_id=1, source_target_pairs={{0,32},{32,0},{1,33},{33,1},{2,34},{34,2},{3,35},{35,3},{4,36},{36... | collective-permute-start | bytes 786440 | tf_op jit(solution)/shard_map/ppermute | solution.py:201
  68.5 3.6 %all-to-all-start.2 = ((bf16[4,4,128,128]{3,2,1,0:T(8,128)(2,1)}), bf16[4,4,128,128]{3,2,1,0:T(8,128)(2,1)S(1)}, u32[]{:S(2)}, u32[]{:S(2)}) async-start(bf16[4,4,128,128]{3,2,1,0:T(8,128)(2,1)} %get-tuple-element.18), calls=%async_computation.2 | async-start | bytes 1048576 | tf_op jit(solution)/shard_map/all_to_all | solution.py:294
  72.1 6.2 %collective-permute-start.4 = (bf16[2,256,128]{2,1,0:T(8,128)(2,1)S(1)}, bf16[2,256,128]{2,1,0:T(8,128)(2,1)S(1)}, u32[]{:S(2)}, u32[]{:S(2)}) collective-permute-start(bf16[2,256,128]{2,1,0:T(8,128)(2,1)S(1)} %fusion), channel_id=1, source_target_pairs={{0,64},{64,0},{1,65},{65,1},{2,66},{66,2},{3,67},{67,3},{4,68},{68... | collective-permute-start | bytes 393224 | tf_op jit(solution)/shard_map/ppermute | solution.py:201
  78.3 2.4 %all-to-all-done.2 = bf16[4,4,128,128]{3,2,1,0:T(8,128)(2,1)S(1)} async-done(((bf16[4,4,128,128]{3,2,1,0:T(8,128)(2,1)}), bf16[4,4,128,128]{3,2,1,0:T(8,128)(2,1)S(1)}, u32[]{:S(2)}, u32[]{:S(2)}) %all-to-all-start.2) | async-done | bytes 524320 | tf_op jit(solution)/shard_map/all_to_all | solution.py:294
  80.7 0.7 reduce_sum.24
  81.4 5.0 %all-to-all-start.3 = ((bf16[2,256,128]{2,1,0:T(8,128)(2,1)}), bf16[2,256,128]{2,1,0:T(8,128)(2,1)S(1)}, u32[]{:S(2)}, u32[]{:S(2)}) async-start(bf16[2,256,128]{2,1,0:T(8,128)(2,1)} %bitcast.6), calls=%async_computation.3 | async-start | bytes 262144 | tf_op jit(solution)/shard_map/all_to_all | solution.py:296
  86.4 11.0 %collective-permute-done.4.across_ref = bf16[2,256,128]{2,1,0:T(8,128)(2,1)S(1)} collective-permute-done((bf16[2,256,128]{2,1,0:T(8,128)(2,1)S(1)}, bf16[2,256,128]{2,1,0:T(8,128)(2,1)S(1)}, u32[]{:S(2)}, u32[]{:S(2)}) %collective-permute-start.4) | collective-permute-done | bytes 131104 | tf_op jit(solution)/shard_map/ppermute | solution.py:201
  97.4 0.7 finish.1
  98.1 0.7 reduce_sum.25
  (18 shorter events, 0.4 us)
Async XLA Ops:
  1.5 6.1 %copy-start = (bf16[1,1,256,128]{3,2,1,0:T(8,128)(2,1)S(1)}, bf16[1,1,256,128]{3,2,1,0:T(8,128)(2,1)}, u32[]{:S(2)}) copy-start(bf16[1,1,256,128]{3,2,1,0:T(8,128)(2,1)} %param.8) | copy-start | bytes 196612
  1.5 6.1 %copy-start.1 = (bf16[1,1,256,128]{3,2,1,0:T(8,128)(2,1)S(1)}, bf16[1,1,256,128]{3,2,1,0:T(8,128)(2,1)}, u32[]{:S(2)}) copy-start(bf16[1,1,256,128]{3,2,1,0:T(8,128)(2,1)} %param.7) | copy-start | bytes 196612
  7.6 25.8 %collective-permute-start = (bf16[2,256,128]{2,1,0:T(8,128)(2,1)S(1)}, bf16[2,256,128]{2,1,0:T(8,128)(2,1)S(1)}, u32[]{:S(2)}, u32[]{:S(2)}) collective-permute-start(bf16[2,256,128]{2,1,0:T(8,128)(2,1)S(1)} %pad_maximum_fusion.own_ref), channel_id=1, source_target_pairs={{0,64},{64,0},{1,65},{65,1},{2,66},{66,2},{3,67},{67,3},{4,68},{68... | collective-permute-start | bytes 393224 | tf_op jit(solution)/shard_map/ppermute | solution.py:201
  22.4 13.8 %collective-permute-start.1 = (bf16[2,256,128]{2,1,0:T(8,128)(2,1)S(1)}, bf16[2,256,128]{2,1,0:T(8,128)(2,1)S(1)}, u32[]{:S(2)}, u32[]{:S(2)}) collective-permute-start(bf16[2,256,128]{2,1,0:T(8,128)(2,1)S(1)} %pad_maximum_fusion.own_ref), channel_id=1, source_target_pairs={{0,32},{32,0},{1,33},{33,1},{2,34},{34,2},{3,35},{35,3},{4,36},{36... | collective-permute-start | bytes 393224 | tf_op jit(solution)/shard_map/ppermute | solution.py:201
  25.6 5.0 %copy-start.2 = (s32[64,32]{0,1:T(8,128)S(1)}, s32[64,32]{0,1:T(8,128)}, u32[]{:S(2)}) copy-start(s32[64,32]{0,1:T(8,128)} %param.10) | copy-start | bytes 24580
  25.6 19.3 %all-to-all-start = ((bf16[4,2,2,256,128]{4,3,2,1,0:T(8,128)(2,1)}), bf16[4,2,2,256,128]{4,3,2,1,0:T(8,128)(2,1)S(1)}, u32[]{:S(2)}, u32[]{:S(2)}) async-start(bf16[4,2,2,256,128]{4,3,2,1,0:T(8,128)(2,1)} %broadcast_in_dim.15), calls=%async_computation | async-start | bytes 2097152 | tf_op jit(solution)/shard_map/all_to_all | solution.py:281
  34.3 3.2 %collective-permute-start.2 = (bf16[2,256,128]{2,1,0:T(8,128)(2,1)S(1)}, bf16[2,256,128]{2,1,0:T(8,128)(2,1)S(1)}, u32[]{:S(2)}, u32[]{:S(2)}) collective-permute-start(bf16[2,256,128]{2,1,0:T(8,128)(2,1)S(1)} %get-tuple-element.16.across_ref), channel_id=1, source_target_pairs={{0,32},{32,0},{1,33},{33,1},{2,34},{34,2},{3,35},{35,3},{4,36},{36... | collective-permute-start | bytes 393224 | tf_op jit(solution)/shard_map/ppermute | solution.py:201
  49.9 4.3 %copy-start.3 = (s32[16,32,2]{1,2,0:T(2,128)S(1)}, s32[16,32,2]{1,2,0:T(2,128)}, u32[]{:S(2)}) copy-start(s32[16,32,2]{1,2,0:T(2,128)} %param.11) | copy-start | bytes 12292
  49.9 8.8 %all-to-all-start.1 = ((f32[8,4,2,1,512]{4,3,2,1,0:T(1,128)}), f32[8,4,2,1,512]{4,3,2,1,0:T(1,128)S(1)}, u32[]{:S(2)}, u32[]{:S(2)}) async-start(f32[8,4,2,1,512]{4,3,2,1,0:T(1,128)} %stats.1), calls=%async_computation.1 | async-start | bytes 262144 | tf_op jit(solution)/shard_map/all_to_all | solution.py:288
  66.6 5.5 %collective-permute-start.3 = (bf16[2,2,256,128]{3,2,1,0:T(8,128)(2,1)S(1)}, bf16[2,2,256,128]{3,2,1,0:T(8,128)(2,1)S(1)}, u32[]{:S(2)}, u32[]{:S(2)}) collective-permute-start(bf16[2,2,256,128]{3,2,1,0:T(8,128)(2,1)S(1)} %get-tuple-element.20), channel_id=1, source_target_pairs={{0,32},{32,0},{1,33},{33,1},{2,34},{34,2},{3,35},{35,3},{4,36},{36... | collective-permute-start | bytes 786440 | tf_op jit(solution)/shard_map/ppermute | solution.py:201
  68.5 12.2 %all-to-all-start.2 = ((bf16[4,4,128,128]{3,2,1,0:T(8,128)(2,1)}), bf16[4,4,128,128]{3,2,1,0:T(8,128)(2,1)S(1)}, u32[]{:S(2)}, u32[]{:S(2)}) async-start(bf16[4,4,128,128]{3,2,1,0:T(8,128)(2,1)} %get-tuple-element.18), calls=%async_computation.2 | async-start | bytes 1048576 | tf_op jit(solution)/shard_map/all_to_all | solution.py:294
  72.1 25.3 %collective-permute-start.4 = (bf16[2,256,128]{2,1,0:T(8,128)(2,1)S(1)}, bf16[2,256,128]{2,1,0:T(8,128)(2,1)S(1)}, u32[]{:S(2)}, u32[]{:S(2)}) collective-permute-start(bf16[2,256,128]{2,1,0:T(8,128)(2,1)S(1)} %fusion), channel_id=1, source_target_pairs={{0,64},{64,0},{1,65},{65,1},{2,66},{66,2},{3,67},{67,3},{4,68},{68... | collective-permute-start | bytes 393224 | tf_op jit(solution)/shard_map/ppermute | solution.py:201
  81.4 16.7 %all-to-all-start.3 = ((bf16[2,256,128]{2,1,0:T(8,128)(2,1)}), bf16[2,256,128]{2,1,0:T(8,128)(2,1)S(1)}, u32[]{:S(2)}, u32[]{:S(2)}) async-start(bf16[2,256,128]{2,1,0:T(8,128)(2,1)} %bitcast.6), calls=%async_computation.3 | async-start | bytes 262144 | tf_op jit(solution)/shard_map/all_to_all | solution.py:296

commit v2 on v1

--- a/solution.py
+++ b/solution.py
@@ -27,13 +27,16 @@
     return jnp.dot(a, b, preferred_element_type=jnp.float32)
 
 
-def mask_kernel(tiles_ref, across_ref, far_ref, live_ref, same_ref, table_ref):
+def mask_kernel(tiles_ref, own_ref, across_ref, far_ref, live_ref, mine_ref, table_ref):
+    mine_ref[0] = own_ref[...]
+    mine_ref[1] = across_ref[...]
     x, zh, core, half = (lax.axis_index(name) for name in ("x", "zh", "c", "p"))
     tiles = tiles_ref[...]
     for k in range(2 * NCHUNK):
         chunk_zh = zh if k // 2 % 2 == 0 else 1 - zh
         chunk_core = core if k // 4 == 0 else 1 - core
-        key_id = (4 * x + 2 * chunk_zh + chunk_core) * 4 + 2 * half + k % 2
+        chunk_half = half if k // 2 % 2 == 0 else 1 - half
+        key_id = (4 * x + 2 * chunk_zh + chunk_core) * 4 + 2 * chunk_half + k % 2
         hit = jnp.where(tiles == key_id, 0.0, FAR)
         table_ref[k] = jnp.broadcast_to(jnp.min(hit, axis=1, keepdims=True), (64, TILE))
     for n in range(NX):
@@ -48,10 +51,8 @@
         live_ref[n] = (jnp.min(nearest) < 1.0).astype(jnp.int32)
 
 
-def stats_kernel(
-    live_ref, qg_ref, own_ref, across_ref, core_ref, core_across_ref, far_ref, out_ref
-):
-    chunks = (own_ref, across_ref, core_ref, core_across_ref)
+def stats_kernel(live_ref, qg_ref, mine_ref, mate_ref, far_ref, out_ref):
+    chunks = (mine_ref.at[0], mine_ref.at[1], mate_ref.at[0], mate_ref.at[1])
 
     def group(n, carry):
         @pl.when(live_ref[n] > 0)
@@ -106,10 +107,8 @@
     live_ref,
     work_ref,
     qg_ref,
-    own_ref,
-    across_ref,
-    core_ref,
-    core_across_ref,
+    mine_ref,
+    mate_ref,
     far_ref,
     stats_ref,
     keep_ref,
@@ -121,21 +120,13 @@
     ds_ref,
 ):
     zh, core, head = (lax.axis_index(name) for name in ("zh", "c", "n"))
-    chunks = (own_ref, across_ref, core_ref, core_across_ref)
+    chunks = (mine_ref.at[0], mine_ref.at[1], mate_ref.at[0], mate_ref.at[1])
     dk_acc[...] = jnp.zeros_like(dk_acc)
     dv_acc[...] = jnp.zeros_like(dv_acc)
     for i, chunk in enumerate(chunks):
         kt_ref[:, i * HALF : (i + 1) * HALF] = chunk[0].T
 
     def group(n, carry):
-        section = 4 * n + 2 * zh + core
-
-        def slot(wanted):
-            found = jnp.int32(3)
-            for w in range(3):
-                found = jnp.where(work_ref[section, 4 * head + w] == wanted, w, found)
-            return found
-
         @pl.when(live_ref[n] > 0)
         def _():
             q_all = qg_ref[n, :, 0].reshape(2 * HALF, HD)
@@ -174,8 +165,12 @@
                 dk_acc[rows] += dot_n(jnp.concatenate(ds, axis=1), q_all)
             for h in range(2):
                 dq = (dot_n(kt_ref[...], ds_ref[h]) * SCALE).T.astype(jnp.bfloat16)
-                dq_ref[n, slot(2 * h)] = dq[:TILE]
-                dq_ref[n, slot(2 * h + 1)] = dq[TILE:]
+                for t in range(2):
+                    slot = jnp.int32(3)
+                    for w in range(3):
+                        listed = work_ref[4 * n + 2 * zh + core, 4 * head + w]
+                        slot = jnp.where(listed == 2 * h + t, w, slot)
+                    dq_ref[n, slot] = dq[t * TILE : (t + 1) * TILE]
 
         @pl.when(live_ref[n] == 0)
         def _():
@@ -201,29 +196,32 @@
     return lax.ppermute(value, axis, [(0, 1), (1, 0)])
 
 
-def run_masks(tiles, across):
+def across(value):
+    return lax.ppermute(value, ("zh", "p"), [(0, 3), (1, 2), (2, 1), (3, 0)])
+
+
+def run_masks(tiles, own, arrived):
     return pl.pallas_call(
         mask_kernel,
         out_shape=[
             jax.ShapeDtypeStruct((NX, 2, 2 * NCHUNK, HALF), jnp.float32),
             jax.ShapeDtypeStruct((NX,), jnp.int32),
-            jax.ShapeDtypeStruct(across.shape, across.dtype),
+            jax.ShapeDtypeStruct((2,) + own.shape, own.dtype),
         ],
-        in_specs=[VMEM, pl.BlockSpec(memory_space=pl.ANY)],
-        out_specs=[VMEM, SMEM, pl.BlockSpec(memory_space=pl.ANY)],
-        input_output_aliases={1: 2},
+        in_specs=[VMEM] * 3,
+        out_specs=[VMEM, SMEM, VMEM],
         scratch_shapes=[pltpu.VMEM((2 * NCHUNK, 64, TILE), jnp.float32)],
         compiler_params=pltpu.CompilerParams(vmem_limit_bytes=8 * 1024 * 1024),
         cost_estimate=pl.CostEstimate(flops=10**11, bytes_accessed=2**20, transcendentals=0),
         name="masks",
-    )(tiles, across)
+    )(tiles, own, arrived)
 
 
 def run_stats(live, qg, kv, far):
     return pl.pallas_call(
         stats_kernel,
         out_shape=jax.ShapeDtypeStruct((BLOCKS, NX, 2, 1, 2 * HALF), jnp.float32),
-        in_specs=[SMEM] + [VMEM] * 6,
+        in_specs=[SMEM] + [VMEM] * 4,
         out_specs=VMEM,
         compiler_params=pltpu.CompilerParams(vmem_limit_bytes=32 * 1024 * 1024),
         cost_estimate=pl.CostEstimate(flops=10**9, bytes_accessed=2**21, transcendentals=2**21),
@@ -239,7 +237,7 @@
             jax.ShapeDtypeStruct((2, 2, HALF, HD), jnp.bfloat16),
             jax.ShapeDtypeStruct((NX, 4, TILE, HD), jnp.bfloat16),
         ],
-        in_specs=[SMEM, SMEM] + [VMEM] * 7,
+        in_specs=[SMEM, SMEM] + [VMEM] * 5,
         out_specs=[VMEM] * 3,
         scratch_shapes=[
             pltpu.VMEM((NCHUNK * HALF, HD), jnp.float32),
@@ -253,21 +251,39 @@
     )(live, work, qg, *kv, far, stats)
 
 
-def finish_kernel(mine_ref, across_ref, dk_ref, dv_ref):
-    dk_ref[...] = (mine_ref[0] + across_ref[0].astype(jnp.float32)).astype(jnp.bfloat16)
-    dv_ref[...] = (mine_ref[1] + across_ref[1].astype(jnp.float32)).astype(jnp.bfloat16)
-
-
-def run_finish(mine, across):
+def finish_kernel(total_ref, arrived_ref, dk_ref, dv_ref):
+    dk_ref[...] = (total_ref[0, 0] + arrived_ref[0].astype(jnp.float32)).astype(jnp.bfloat16)
+    dv_ref[...] = (total_ref[0, 1] + arrived_ref[1].astype(jnp.float32)).astype(jnp.bfloat16)
+
+
+def run_finish(total, arrived):
     return pl.pallas_call(
         finish_kernel,
         out_shape=[jax.ShapeDtypeStruct((HALF, HD), jnp.bfloat16)] * 2,
-        in_specs=[VMEM, VMEM],
-        out_specs=[VMEM, VMEM],
+        in_specs=[VMEM] * 2,
+        out_specs=[VMEM] * 2,
         compiler_params=pltpu.CompilerParams(vmem_limit_bytes=8 * 1024 * 1024),
         cost_estimate=pl.CostEstimate(flops=10**11, bytes_accessed=2**20, transcendentals=0),
         name="finish",
-    )(mine, across)
+    )(total, arrived)
+
+
+def sum_kernel(parts_ref, dq_ref):
+    dq = parts_ref[0].astype(jnp.float32)
+    for j in range(1, BLOCKS):
+        dq = dq + parts_ref[j].astype(jnp.float32)
+    dq_ref[...] = dq.astype(jnp.bfloat16)
+
+
+def run_sum(parts):
+    return pl.pallas_call(
+        sum_kernel,
+        out_shape=jax.ShapeDtypeStruct((HALF, HD), jnp.bfloat16),
+        in_specs=[VMEM],
+        out_specs=VMEM,
+        compiler_params=pltpu.CompilerParams(vmem_limit_bytes=8 * 1024 * 1024),
+        name="sum",
+    )(parts)
 
 
 def on_device(queries, keys, values, grad_out, key_tiles, work_lists):
@@ -275,14 +291,12 @@
     both_qg = lax.all_gather(own_qg, "p")
     own_kv = jnp.stack([keys[0, 0], values[0, 0]])
     own_kv, both_qg = lax.optimization_barrier((own_kv, both_qg))
-    across_kv = flipped(own_kv, "zh")
-    core_kv = flipped(own_kv, "c")
+    across_kv = across(own_kv)
     spread = jnp.broadcast_to(both_qg[None], (NX,) + both_qg.shape)
     all_qg = lax.all_to_all(spread, "x", 0, 0)
-    far, live, across_kv = run_masks(key_tiles, across_kv)
-    core_across_kv = flipped(across_kv, "c")
+    far, live, mine = run_masks(key_tiles, own_kv, across_kv)
+    kv = (mine, flipped(mine, "c"))
     work = work_lists.reshape(16, 64)
-    kv = (own_kv, across_kv, core_kv, core_across_kv)
 
     stats = run_stats(live, all_qg, kv, far)
     stats = lax.all_to_all(stats, ("x", "p"), 0, 0)
@@ -290,13 +304,13 @@
 
     total = keep + flipped(send, "c").astype(jnp.float32)
     dkv_out = total[1].astype(jnp.bfloat16)
-    from_across = flipped(dkv_out, "zh")
-    dq_parts = lax.all_to_all(dq, "x", 0, 0)
-    dq_sum = jnp.sum(dq_parts.astype(jnp.float32), axis=0).astype(jnp.bfloat16)
-    dq_sum = lax.all_to_all(dq_sum.reshape(2, HALF, HD), "p", 0, 0)
-    grad_queries = jnp.sum(dq_sum.astype(jnp.float32), axis=0).astype(jnp.bfloat16)
-    grad_keys, grad_values = run_finish(total[0], from_across)
-    return grad_queries[None, None], grad_keys[None, None], grad_values[None, None]
+    dkv_out, dq = lax.optimization_barrier((dkv_out, dq))
+    from_across = across(dkv_out)
+    dq = dq.reshape(BLOCKS, HALF, HD)
+    dq_parts = lax.all_to_all(dq, ("x", "p"), 0, 0)
+    grad_keys, grad_values = run_finish(total, from_across)
+    outs = (run_sum(dq_parts), grad_keys, grad_values)
+    return tuple(out[None, None] for out in outs)
 
 
 def solution(mesh):

time: 99.5 us -> 94.9 us (0.954)
  the two profiles are of different devices: /device:TPU:58 before, /device:TPU:1 now
where the time goes in v2:
time: 94.9 us; the launch traced here: 94.3 us
  starting transfers between devices  52.8 us (56%)
  waiting for transfers between devices  22.5 us (24%)
  Pallas kernels  10.2 us (11%)
  blocking collectives  5.61 us (6%)
  local copies, waits for them, and re-layouts  1.45 us (2%)
  other arithmetic  0.96 us (1%)
    ppermute x2, starting transfers between devices, across(): return lax.ppermute(value, ('zh', 'p'), [(0, 3), (1, 2), (2, 1), (3, 0)])  24.2 us
    ppermute x2, starting transfers between devices, flipped(): return lax.ppermute(value, axis, [(0, 1), (1, 0)])  14 us
    ppermute x2, waiting for transfers between devices, across(): return lax.ppermute(value, ('zh', 'p'), [(0, 3), (1, 2), (2, 1), (3, 0)])  8.11 us
    all_to_all x1, starting transfers between devices, on_device(): dq_parts = lax.all_to_all(dq, ('x', 'p'), 0, 0)  5.93 us
    all_gather x1, blocking collectives, on_device(): both_qg = lax.all_gather(own_qg, 'p')  5.61 us
    all_to_all x1, waiting for transfers between devices, on_device(): stats = lax.all_to_all(stats, ('x', 'p'), 0, 0)  5.39 us
    pallas_call x1, Pallas kernels, run_grads(): pl.pallas_call(grads_kernel, out_shape=[jax.ShapeDtypeStruct((2, 2, HALF,...  4.75 us
    all_to_all x1, starting transfers between devices, on_device(): stats = lax.all_to_all(stats, ('x', 'p'), 0, 0)  4.55 us
  transfers between devices with their start and end apart: 7, of which 6 were waited for; matrix products, arithmetic and copies ran while one was open for 1% of the time, Pallas kernels for 2%

profile of v2, /device:TPU:1, one launch (start us, length us, event | category | flops | bytes accessed | tf_op | source)
XLA Modules:
  0.0 94.3 jit_solution(14285809057569736908)
XLA Ops:
  0.6 0.9 pad_maximum_fusion.1
  1.5 5.6 %all-gather = bf16[4,256,128]{2,1,0:T(8,128)(2,1)S(1)} all-gather(bf16[2,256,128]{2,1,0:T(8,128)(2,1)S(1)} %pad_maximum_fusion.1), channel_id=2, replica_groups=mesh['x'=4,'zh'=2,'c'=2,'n'=16,'p'=2] {'p'}, dimensions={0}, use_global_device_ids=true | all-gather | bytes 393216 | tf_op jit(solution)/shard_map/all_gather | solution.py:291
  7.2 15.4 %collective-permute-start = (bf16[2,256,128]{2,1,0:T(8,128)(2,1)S(1)}, bf16[2,256,128]{2,1,0:T(8,128)(2,1)S(1)}, u32[]{:S(2)}, u32[]{:S(2)}) collective-permute-start(bf16[2,256,128]{2,1,0:T(8,128)(2,1)S(1)} %pad_maximum_fusion.own_ref), channel_id=1, source_target_pairs={{0,65},{1,64},{64,1},{65,0},{2,67},{3,66},{66,3},{67,2},{4,69},{5,... | collective-permute-start | bytes 393224 | tf_op jit(solution)/shard_map/ppermute | solution.py:200
  22.6 1.2 %broadcast_in_dim.15 = bf16[4,2,2,256,128]{4,3,2,1,0:T(8,128)(2,1)} broadcast(bf16[2,2,256,128]{3,2,1,0:T(8,128)(2,1)S(1)} %bitcast.12), dimensions={1,2,3,4} | broadcast | bytes 1310720 | tf_op jit(solution)/shard_map/broadcast_in_dim | solution.py:295
  23.8 4.1 %all-to-all-start = ((bf16[4,2,2,256,128]{4,3,2,1,0:T(8,128)(2,1)}), bf16[4,2,2,256,128]{4,3,2,1,0:T(8,128)(2,1)S(1)}, u32[]{:S(2)}, u32[]{:S(2)}) async-start(bf16[4,2,2,256,128]{4,3,2,1,0:T(8,128)(2,1)} %broadcast_in_dim.15), calls=%async_computation | async-start | bytes 2097152 | tf_op jit(solution)/shard_map/all_to_all | solution.py:296
  27.9 0.1 copy.14.tiles_ref
  28.0 0.9 masks.1
  28.9 8.2 %collective-permute-start.1 = (bf16[2,2,256,128]{3,2,1,0:T(8,128)(2,1)S(1)}, bf16[2,2,256,128]{3,2,1,0:T(8,128)(2,1)S(1)}, u32[]{:S(2)}, u32[]{:S(2)}) collective-permute-start(bf16[2,2,256,128]{3,2,1,0:T(8,128)(2,1)S(1)} %get-tuple-element.18.mine_ref), channel_id=1, source_target_pairs={{0,32},{32,0},{1,33},{33,1},{2,34},{34,2},{3,35},{35,3},{4,36},{36... | collective-permute-start | bytes 786440 | tf_op jit(solution)/shard_map/ppermute | solution.py:196
  37.2 1.1 %collective-permute-done.1.mate_ref = bf16[2,2,256,128]{3,2,1,0:T(8,128)(2,1)S(1)} collective-permute-done((bf16[2,2,256,128]{3,2,1,0:T(8,128)(2,1)S(1)}, bf16[2,2,256,128]{3,2,1,0:T(8,128)(2,1)S(1)}, u32[]{:S(2)}, u32[]{:S(2)}) %collective-permute-start.1) | collective-permute-done | bytes 262176 | tf_op jit(solution)/shard_map/ppermute | solution.py:196
  38.3 2.6 %all-to-all-done.qg_ref = bf16[4,2,2,256,128]{4,3,2,1,0:T(8,128)(2,1)S(1)} async-done(((bf16[4,2,2,256,128]{4,3,2,1,0:T(8,128)(2,1)}), bf16[4,2,2,256,128]{4,3,2,1,0:T(8,128)(2,1)S(1)}, u32[]{:S(2)}, u32[]{:S(2)}) %all-to-all-start) | async-done | bytes 1048608 | tf_op jit(solution)/shard_map/all_to_all | solution.py:296
  40.9 3.1 %stats.1 = f32[8,4,2,1,512]{4,3,2,1,0:T(1,128)} custom-call(s32[4]{0:T(128)S(1)} %get-tuple-element.16.live_ref, bf16[4,2,2,256,128]{4,3,2,1,0:T(8,128)(2,1)S(1)} %all-to-all-done.qg_ref, bf16[2,2,256,128]{3,2,1,0:T(8,128)(2,1)S(1)} %get-tuple-element.18.mine_ref, bf16[2,2,256,128]{3,2,1,0:T(8,128)(2,1)S(1)} %collective-permute-done.1.mate_ref, ...), custom_call_target="tpu_custom_call" | custom-call | flops 1000000000 | bytes 2097152 | tf_op jit(solution)/shard_map/stats/pallas_call | solution.py:221
  44.1 4.5 %all-to-all-start.1 = ((f32[8,4,2,1,512]{4,3,2,1,0:T(1,128)}), f32[8,4,2,1,512]{4,3,2,1,0:T(1,128)S(1)}, u32[]{:S(2)}, u32[]{:S(2)}) async-start(f32[8,4,2,1,512]{4,3,2,1,0:T(1,128)} %stats.1), calls=%async_computation.1 | async-start | bytes 262144 | tf_op jit(solution)/shard_map/all_to_all | solution.py:302
  48.6 0.1 copy.15
  48.7 0.1 copy.16.work_ref
  48.8 5.4 %all-to-all-done.1.stats_ref = f32[8,4,2,1,512]{4,3,2,1,0:T(1,128)S(1)} async-done(((f32[8,4,2,1,512]{4,3,2,1,0:T(1,128)}), f32[8,4,2,1,512]{4,3,2,1,0:T(1,128)S(1)}, u32[]{:S(2)}, u32[]{:S(2)}) %all-to-all-start.1) | async-done | bytes 131104 | tf_op jit(solution)/shard_map/all_to_all | solution.py:302
  54.2 4.7 %grads.1 = (f32[2,2,256,128]{3,2,1,0:T(8,128)S(1)}, bf16[2,2,256,128]{3,2,1,0:T(8,128)(2,1)S(1)}, bf16[4,4,128,128]{3,2,1,0:T(8,128)(2,1)}) custom-call(s32[4]{0:T(128)S(1)} %get-tuple-element.16.live_ref, s32[16,64]{1,0:T(8,128)S(1)} %copy.16.work_ref, bf16[4,2,2,256,128]{4,3,2,1,0:T(8,128)(2,1)S(1)} %all-to-all-done.qg_ref, ...), custom_call_target="tpu_custom_call" | custom-call | flops 2000000000 | bytes 2097152 | tf_op jit(solution)/shard_map/grads/pallas_call | solution.py:233
  58.9 5.8 %collective-permute-start.2 = (bf16[2,2,256,128]{3,2,1,0:T(8,128)(2,1)S(1)}, bf16[2,2,256,128]{3,2,1,0:T(8,128)(2,1)S(1)}, u32[]{:S(2)}, u32[]{:S(2)}) collective-permute-start(bf16[2,2,256,128]{3,2,1,0:T(8,128)(2,1)S(1)} %get-tuple-element.21), channel_id=1, source_target_pairs={{0,32},{32,0},{1,33},{33,1},{2,34},{34,2},{3,35},{35,3},{4,36},{36... | collective-permute-start | bytes 786440 | tf_op jit(solution)/shard_map/ppermute | solution.py:196
  64.7 1.1 %collective-permute-done.2 = bf16[2,2,256,128]{3,2,1,0:T(8,128)(2,1)S(1)} collective-permute-done((bf16[2,2,256,128]{3,2,1,0:T(8,128)(2,1)S(1)}, bf16[2,2,256,128]{3,2,1,0:T(8,128)(2,1)S(1)}, u32[]{:S(2)}, u32[]{:S(2)}) %collective-permute-start.2) | collective-permute-done | bytes 262176 | tf_op jit(solution)/shard_map/ppermute | solution.py:196
  66.0 8.8 %collective-permute-start.3 = (bf16[2,256,128]{2,1,0:T(8,128)(2,1)S(1)}, bf16[2,256,128]{2,1,0:T(8,128)(2,1)S(1)}, u32[]{:S(2)}, u32[]{:S(2)}) collective-permute-start(bf16[2,256,128]{2,1,0:T(8,128)(2,1)S(1)} %fusion), channel_id=1, source_target_pairs={{0,65},{1,64},{64,1},{65,0},{2,67},{3,66},{66,3},{67,2},{4,69},{5,... | collective-permute-start | bytes 393224 | tf_op jit(solution)/shard_map/ppermute | solution.py:200
  74.8 5.9 %all-to-all-start.2 = ((bf16[8,256,128]{2,1,0:T(8,128)(2,1)}), bf16[8,256,128]{2,1,0:T(8,128)(2,1)S(1)}, u32[]{:S(2)}, u32[]{:S(2)}) async-start(bf16[8,256,128]{2,1,0:T(8,128)(2,1)} %bitcast.7), calls=%async_computation.2 | async-start | bytes 1048576 | tf_op jit(solution)/shard_map/all_to_all | solution.py:310
  80.7 8.1 %collective-permute-done.3.arrived_ref = bf16[2,256,128]{2,1,0:T(8,128)(2,1)S(1)} collective-permute-done((bf16[2,256,128]{2,1,0:T(8,128)(2,1)S(1)}, bf16[2,256,128]{2,1,0:T(8,128)(2,1)S(1)}, u32[]{:S(2)}, u32[]{:S(2)}) %collective-permute-start.3) | collective-permute-done | bytes 131104 | tf_op jit(solution)/shard_map/ppermute | solution.py:200
  88.8 0.7 finish.1
  89.5 4.1 %all-to-all-done.2.parts_ref = bf16[8,256,128]{2,1,0:T(8,128)(2,1)S(1)} async-done(((bf16[8,256,128]{2,1,0:T(8,128)(2,1)}), bf16[8,256,128]{2,1,0:T(8,128)(2,1)S(1)}, u32[]{:S(2)}, u32[]{:S(2)}) %all-to-all-start.2) | async-done | bytes 524320 | tf_op jit(solution)/shard_map/all_to_all | solution.py:310
  93.6 0.7 sum.1
  (12 shorter events, 0.1 us)
Async XLA Ops:
  1.5 5.6 %copy-start = (bf16[1,1,256,128]{3,2,1,0:T(8,128)(2,1)S(1)}, bf16[1,1,256,128]{3,2,1,0:T(8,128)(2,1)}, u32[]{:S(2)}) copy-start(bf16[1,1,256,128]{3,2,1,0:T(8,128)(2,1)} %param.8) | copy-start | bytes 196612
  1.5 5.6 %copy-start.1 = (bf16[1,1,256,128]{3,2,1,0:T(8,128)(2,1)S(1)}, bf16[1,1,256,128]{3,2,1,0:T(8,128)(2,1)}, u32[]{:S(2)}) copy-start(bf16[1,1,256,128]{3,2,1,0:T(8,128)(2,1)} %param.7) | copy-start | bytes 196612
  7.2 20.8 %collective-permute-start = (bf16[2,256,128]{2,1,0:T(8,128)(2,1)S(1)}, bf16[2,256,128]{2,1,0:T(8,128)(2,1)S(1)}, u32[]{:S(2)}, u32[]{:S(2)}) collective-permute-start(bf16[2,256,128]{2,1,0:T(8,128)(2,1)S(1)} %pad_maximum_fusion.own_ref), channel_id=1, source_target_pairs={{0,65},{1,64},{64,1},{65,0},{2,67},{3,66},{66,3},{67,2},{4,69},{5,... | collective-permute-start | bytes 393224 | tf_op jit(solution)/shard_map/ppermute | solution.py:200
  23.8 4.1 %copy-start.2 = (s32[64,32]{0,1:T(8,128)S(1)}, s32[64,32]{0,1:T(8,128)}, u32[]{:S(2)}) copy-start(s32[64,32]{0,1:T(8,128)} %param.10) | copy-start | bytes 24580
  23.8 17.2 %all-to-all-start = ((bf16[4,2,2,256,128]{4,3,2,1,0:T(8,128)(2,1)}), bf16[4,2,2,256,128]{4,3,2,1,0:T(8,128)(2,1)S(1)}, u32[]{:S(2)}, u32[]{:S(2)}) async-start(bf16[4,2,2,256,128]{4,3,2,1,0:T(8,128)(2,1)} %broadcast_in_dim.15), calls=%async_computation | async-start | bytes 2097152 | tf_op jit(solution)/shard_map/all_to_all | solution.py:296
  28.9 9.4 %collective-permute-start.1 = (bf16[2,2,256,128]{3,2,1,0:T(8,128)(2,1)S(1)}, bf16[2,2,256,128]{3,2,1,0:T(8,128)(2,1)S(1)}, u32[]{:S(2)}, u32[]{:S(2)}) collective-permute-start(bf16[2,2,256,128]{3,2,1,0:T(8,128)(2,1)S(1)} %get-tuple-element.18.mine_ref), channel_id=1, source_target_pairs={{0,32},{32,0},{1,33},{33,1},{2,34},{34,2},{3,35},{35,3},{4,36},{36... | collective-permute-start | bytes 786440 | tf_op jit(solution)/shard_map/ppermute | solution.py:196
  44.1 4.5 %copy-start.3 = (s32[16,32,2]{1,2,0:T(2,128)S(1)}, s32[16,32,2]{1,2,0:T(2,128)}, u32[]{:S(2)}) copy-start(s32[16,32,2]{1,2,0:T(2,128)} %param.11) | copy-start | bytes 12292
  44.1 10.1 %all-to-all-start.1 = ((f32[8,4,2,1,512]{4,3,2,1,0:T(1,128)}), f32[8,4,2,1,512]{4,3,2,1,0:T(1,128)S(1)}, u32[]{:S(2)}, u32[]{:S(2)}) async-start(f32[8,4,2,1,512]{4,3,2,1,0:T(1,128)} %stats.1), calls=%async_computation.1 | async-start | bytes 262144 | tf_op jit(solution)/shard_map/all_to_all | solution.py:302
  58.9 7.0 %collective-permute-start.2 = (bf16[2,2,256,128]{3,2,1,0:T(8,128)(2,1)S(1)}, bf16[2,2,256,128]{3,2,1,0:T(8,128)(2,1)S(1)}, u32[]{:S(2)}, u32[]{:S(2)}) collective-permute-start(bf16[2,2,256,128]{3,2,1,0:T(8,128)(2,1)S(1)} %get-tuple-element.21), channel_id=1, source_target_pairs={{0,32},{32,0},{1,33},{33,1},{2,34},{34,2},{3,35},{35,3},{4,36},{36... | collective-permute-start | bytes 786440 | tf_op jit(solution)/shard_map/ppermute | solution.py:196
  66.0 22.8 %collective-permute-start.3 = (bf16[2,256,128]{2,1,0:T(8,128)(2,1)S(1)}, bf16[2,256,128]{2,1,0:T(8,128)(2,1)S(1)}, u32[]{:S(2)}, u32[]{:S(2)}) collective-permute-start(bf16[2,256,128]{2,1,0:T(8,128)(2,1)S(1)} %fusion), channel_id=1, source_target_pairs={{0,65},{1,64},{64,1},{65,0},{2,67},{3,66},{66,3},{67,2},{4,69},{5,... | collective-permute-start | bytes 393224 | tf_op jit(solution)/shard_map/ppermute | solution.py:200
  74.8 18.8 %all-to-all-start.2 = ((bf16[8,256,128]{2,1,0:T(8,128)(2,1)}), bf16[8,256,128]{2,1,0:T(8,128)(2,1)S(1)}, u32[]{:S(2)}, u32[]{:S(2)}) async-start(bf16[8,256,128]{2,1,0:T(8,128)(2,1)} %bitcast.7), calls=%async_computation.2 | async-start | bytes 1048576 | tf_op jit(solution)/shard_map/all_to_all | solution.py:310

commit v3 on v2

--- a/solution.py
+++ b/solution.py
@@ -25,6 +25,13 @@
 
 def dot_n(a, b):
     return jnp.dot(a, b, preferred_element_type=jnp.float32)
+
+
+def spread_kernel(own_ref, mate_ref, out_ref):
+    half = lax.axis_index("p")
+    for j in range(NX):
+        out_ref[j, half] = own_ref[...]
+        out_ref[j, 1 - half] = mate_ref[...]
 
 
 def mask_kernel(tiles_ref, own_ref, across_ref, far_ref, live_ref, mine_ref, table_ref):
@@ -200,6 +207,17 @@
     return lax.ppermute(value, ("zh", "p"), [(0, 3), (1, 2), (2, 1), (3, 0)])
 
 
+def run_spread(own, mate):
+    return pl.pallas_call(
+        spread_kernel,
+        out_shape=jax.ShapeDtypeStruct((NX, 2) + own.shape, own.dtype),
+        in_specs=[VMEM] * 2,
+        out_specs=VMEM,
+        compiler_params=pltpu.CompilerParams(vmem_limit_bytes=8 * 1024 * 1024),
+        name="spread",
+    )(own, mate)
+
+
 def run_masks(tiles, own, arrived):
     return pl.pallas_call(
         mask_kernel,
@@ -288,11 +306,10 @@
 
 def on_device(queries, keys, values, grad_out, key_tiles, work_lists):
     own_qg = jnp.stack([queries[0, 0], grad_out[0, 0]])
-    both_qg = lax.all_gather(own_qg, "p")
+    mate_qg = flipped(own_qg, "p")
     own_kv = jnp.stack([keys[0, 0], values[0, 0]])
-    own_kv, both_qg = lax.optimization_barrier((own_kv, both_qg))
     across_kv = across(own_kv)
-    spread = jnp.broadcast_to(both_qg[None], (NX,) + both_qg.shape)
+    spread = run_spread(own_qg, mate_qg)
     all_qg = lax.all_to_all(spread, "x", 0, 0)
     far, live, mine = run_masks(key_tiles, own_kv, across_kv)
     kv = (mine, flipped(mine, "c"))

time: 94.9 us -> 90.5 us (0.954)
  blocking collectives: 5.61 us -> 0 us
  starting transfers between devices: 52.8 us -> 56.2 us
  waiting for transfers between devices: 22.5 us -> 20.4 us
  local copies, waits for them, and re-layouts: 1.45 us -> 0.27 us
  Pallas kernels: 10.2 us -> 11.3 us
    all_gather x1 -> x0, blocking collectives: 5.61 us -> none  [on_device(): both_qg = lax.all_gather(own_qg, 'p')]
    ppermute x2 -> x3, starting transfers between devices: 14 us -> 18.5 us  [flipped(): return lax.ppermute(value, axis, [(0, 1), (1, 0)])]
    ppermute x2, waiting for transfers between devices: 8.11 us -> 6.41 us  [across(): return lax.ppermute(value, ('zh', 'p'), [(0, 3), (1, 2), (2, 1), (3, 0)])]
    broadcast_in_dim x1 -> x0, local copies, waits for them, and re-layouts: 1.18 us -> none  [on_device(): spread = jnp.broadcast_to(both_qg[None], (NX,) + both_qg.shape)]
    pallas_call x0 -> x1, Pallas kernels: none -> 1.15 us  [run_spread(): pl.pallas_call(spread_kernel, out_shape=jax.ShapeDtypeStruct((NX, 2) + ow...]
    ppermute x2 -> x3, waiting for transfers between devices: 2.28 us -> 2.28 us  [flipped(): return lax.ppermute(value, axis, [(0, 1), (1, 0)])]
  transfers between devices with their start and end apart: 7 -> 8, of which waited for: 6 -> 6; matrix products, arithmetic and copies ran while one was open for 1% -> 0% of each run, Pallas kernels for 2% -> 3%
where the time goes in v3:
time: 90.5 us; the launch traced here: 89.9 us
  starting transfers between devices  56.2 us (62%)
  waiting for transfers between devices  20.4 us (23%)
  Pallas kernels  11.3 us (12%)
  other arithmetic  1 us (1%)
    ppermute x2, starting transfers between devices, across(): return lax.ppermute(value, ('zh', 'p'), [(0, 3), (1, 2), (2, 1), (3, 0)])  23.4 us
    ppermute x3, starting transfers between devices, flipped(): return lax.ppermute(value, axis, [(0, 1), (1, 0)])  18.5 us
    ppermute x2, waiting for transfers between devices, across(): return lax.ppermute(value, ('zh', 'p'), [(0, 3), (1, 2), (2, 1), (3, 0)])  6.41 us
    all_to_all x1, starting transfers between devices, on_device(): dq_parts = lax.all_to_all(dq, ('x', 'p'), 0, 0)  5.92 us
    all_to_all x1, waiting for transfers between devices, on_device(): stats = lax.all_to_all(stats, ('x', 'p'), 0, 0)  5.39 us
    pallas_call x1, Pallas kernels, run_grads(): pl.pallas_call(grads_kernel, out_shape=[jax.ShapeDtypeStruct((2, 2, HALF,...  4.75 us
    all_to_all x1, starting transfers between devices, on_device(): stats = lax.all_to_all(stats, ('x', 'p'), 0, 0)  4.42 us
    all_to_all x1, starting transfers between devices, on_device(): all_qg = lax.all_to_all(spread, 'x', 0, 0)  4.01 us
  transfers between devices with their start and end apart: 8, of which 6 were waited for; matrix products, arithmetic and copies ran while one was open for 0% of the time, Pallas kernels for 3%

profile of v3, /device:TPU:1, one launch (start us, length us, event | category | flops | bytes accessed | tf_op | source)
XLA Modules:
  0.0 89.9 jit_solution(3812545710100083934)
XLA Ops:
  0.7 0.9 %pad_maximum_fusion.1.own_ref = bf16[2,256,128]{2,1,0:T(8,128)(2,1)S(1)} fusion(bf16[1,256,128]{2,1,0:T(8,128)(2,1)} %bitcast.13, bf16[1,256,128]{2,1,0:T(8,128)(2,1)} %bitcast.14), kind=kLoop, calls=%fused_computation.4 | loop fusion | flops 65536 | bytes 262144 | tf_op jit(solution)/shard_map/stack | solution.py:308
  1.6 4.4 %collective-permute-start.1 = (bf16[2,256,128]{2,1,0:T(8,128)(2,1)S(1)}, bf16[2,256,128]{2,1,0:T(8,128)(2,1)S(1)}, u32[]{:S(2)}, u32[]{:S(2)}) collective-permute-start(bf16[2,256,128]{2,1,0:T(8,128)(2,1)S(1)} %pad_maximum_fusion.1.own_ref), channel_id=1, source_target_pairs={{0,1},{1,0},{2,3},{3,2},{4,5},{5,4},{6,7},{7,6},{8,9},{9,8},{10,11... | collective-permute-start | bytes 393224 | tf_op jit(solution)/shard_map/ppermute | solution.py:203
  6.0 14.1 %collective-permute-start = (bf16[2,256,128]{2,1,0:T(8,128)(2,1)S(1)}, bf16[2,256,128]{2,1,0:T(8,128)(2,1)S(1)}, u32[]{:S(2)}, u32[]{:S(2)}) collective-permute-start(bf16[2,256,128]{2,1,0:T(8,128)(2,1)S(1)} %pad_maximum_fusion.own_ref), channel_id=1, source_target_pairs={{0,65},{1,64},{64,1},{65,0},{2,67},{3,66},{66,3},{67,2},{4,69},{5,... | collective-permute-start | bytes 393224 | tf_op jit(solution)/shard_map/ppermute | solution.py:207
  20.1 0.1 copy.11.tiles_ref
  20.2 1.1 %spread.1 = bf16[4,2,2,256,128]{4,3,2,1,0:T(8,128)(2,1)} custom-call(bf16[2,256,128]{2,1,0:T(8,128)(2,1)S(1)} %pad_maximum_fusion.1.own_ref, bf16[2,256,128]{2,1,0:T(8,128)(2,1)S(1)} %collective-permute-done.1.mate_ref), custom_call_target="tpu_custom_call" | custom-call | tf_op jit(solution)/shard_map/spread/pallas_call | solution.py:211
  21.4 4.0 %all-to-all-start = ((bf16[4,2,2,256,128]{4,3,2,1,0:T(8,128)(2,1)}), bf16[4,2,2,256,128]{4,3,2,1,0:T(8,128)(2,1)S(1)}, u32[]{:S(2)}, u32[]{:S(2)}) async-start(bf16[4,2,2,256,128]{4,3,2,1,0:T(8,128)(2,1)} %spread.1), calls=%async_computation | async-start | bytes 2097152 | tf_op jit(solution)/shard_map/all_to_all | solution.py:313
  25.4 0.9 %masks.1 = (f32[4,2,8,256]{3,2,1,0:T(8,128)S(1)}, s32[4]{0:T(128)S(1)}, bf16[2,2,256,128]{3,2,1,0:T(8,128)(2,1)S(1)}) custom-call(s32[64,32]{1,0:T(8,128)S(1)} %copy.11.tiles_ref, bf16[2,256,128]{2,1,0:T(8,128)(2,1)S(1)} %pad_maximum_fusion.own_ref, bf16[2,256,128]{2,1,0:T(8,128)(2,1)S(1)} %collective-permute-done.across_ref), custom_call_target="tpu_custom_call" | custom-call | flops 99999997952 | bytes 1048576 | tf_op jit(solution)/shard_map/masks/pallas_call | solution.py:222
  26.3 8.8 %collective-permute-start.2 = (bf16[2,2,256,128]{3,2,1,0:T(8,128)(2,1)S(1)}, bf16[2,2,256,128]{3,2,1,0:T(8,128)(2,1)S(1)}, u32[]{:S(2)}, u32[]{:S(2)}) collective-permute-start(bf16[2,2,256,128]{3,2,1,0:T(8,128)(2,1)S(1)} %get-tuple-element.14.mine_ref), channel_id=1, source_target_pairs={{0,32},{32,0},{1,33},{33,1},{2,34},{34,2},{3,35},{35,3},{4,36},{36... | collective-permute-start | bytes 786440 | tf_op jit(solution)/shard_map/ppermute | solution.py:203
  35.1 1.1 %collective-permute-done.2.mate_ref = bf16[2,2,256,128]{3,2,1,0:T(8,128)(2,1)S(1)} collective-permute-done((bf16[2,2,256,128]{3,2,1,0:T(8,128)(2,1)S(1)}, bf16[2,2,256,128]{3,2,1,0:T(8,128)(2,1)S(1)}, u32[]{:S(2)}, u32[]{:S(2)}) %collective-permute-start.2) | collective-permute-done | bytes 262176 | tf_op jit(solution)/shard_map/ppermute | solution.py:203
  36.2 2.8 %all-to-all-done.qg_ref = bf16[4,2,2,256,128]{4,3,2,1,0:T(8,128)(2,1)S(1)} async-done(((bf16[4,2,2,256,128]{4,3,2,1,0:T(8,128)(2,1)}), bf16[4,2,2,256,128]{4,3,2,1,0:T(8,128)(2,1)S(1)}, u32[]{:S(2)}, u32[]{:S(2)}) %all-to-all-start) | async-done | bytes 1048608 | tf_op jit(solution)/shard_map/all_to_all | solution.py:313
  39.0 3.2 %stats.1 = f32[8,4,2,1,512]{4,3,2,1,0:T(1,128)} custom-call(s32[4]{0:T(128)S(1)} %get-tuple-element.13.live_ref, bf16[4,2,2,256,128]{4,3,2,1,0:T(8,128)(2,1)S(1)} %all-to-all-done.qg_ref, bf16[2,2,256,128]{3,2,1,0:T(8,128)(2,1)S(1)} %get-tuple-element.14.mine_ref, bf16[2,2,256,128]{3,2,1,0:T(8,128)(2,1)S(1)} %collective-permute-done.2.mate_ref, ...), custom_call_target="tpu_custom_call" | custom-call | flops 1000000000 | bytes 2097152 | tf_op jit(solution)/shard_map/stats/pallas_call | solution.py:239
  42.1 4.4 %all-to-all-start.1 = ((f32[8,4,2,1,512]{4,3,2,1,0:T(1,128)}), f32[8,4,2,1,512]{4,3,2,1,0:T(1,128)S(1)}, u32[]{:S(2)}, u32[]{:S(2)}) async-start(f32[8,4,2,1,512]{4,3,2,1,0:T(1,128)} %stats.1), calls=%async_computation.1 | async-start | bytes 262144 | tf_op jit(solution)/shard_map/all_to_all | solution.py:319
  46.6 0.1 copy.12
  46.6 0.1 copy.13.work_ref
  46.7 5.4 %all-to-all-done.1.stats_ref = f32[8,4,2,1,512]{4,3,2,1,0:T(1,128)S(1)} async-done(((f32[8,4,2,1,512]{4,3,2,1,0:T(1,128)}), f32[8,4,2,1,512]{4,3,2,1,0:T(1,128)S(1)}, u32[]{:S(2)}, u32[]{:S(2)}) %all-to-all-start.1) | async-done | bytes 131104 | tf_op jit(solution)/shard_map/all_to_all | solution.py:319
  52.1 4.7 %grads.1 = (f32[2,2,256,128]{3,2,1,0:T(8,128)S(1)}, bf16[2,2,256,128]{3,2,1,0:T(8,128)(2,1)S(1)}, bf16[4,4,128,128]{3,2,1,0:T(8,128)(2,1)}) custom-call(s32[4]{0:T(128)S(1)} %get-tuple-element.13.live_ref, s32[16,64]{1,0:T(8,128)S(1)} %copy.13.work_ref, bf16[4,2,2,256,128]{4,3,2,1,0:T(8,128)(2,1)S(1)} %all-to-all-done.qg_ref, ...), custom_call_target="tpu_custom_call" | custom-call | flops 2000000000 | bytes 2097152 | tf_op jit(solution)/shard_map/grads/pallas_call | solution.py:251
  56.8 5.3 %collective-permute-start.3 = (bf16[2,2,256,128]{3,2,1,0:T(8,128)(2,1)S(1)}, bf16[2,2,256,128]{3,2,1,0:T(8,128)(2,1)S(1)}, u32[]{:S(2)}, u32[]{:S(2)}) collective-permute-start(bf16[2,2,256,128]{3,2,1,0:T(8,128)(2,1)S(1)} %get-tuple-element.17), channel_id=1, source_target_pairs={{0,32},{32,0},{1,33},{33,1},{2,34},{34,2},{3,35},{35,3},{4,36},{36... | collective-permute-start | bytes 786440 | tf_op jit(solution)/shard_map/ppermute | solution.py:203
  62.2 1.1 %collective-permute-done.3 = bf16[2,2,256,128]{3,2,1,0:T(8,128)(2,1)S(1)} collective-permute-done((bf16[2,2,256,128]{3,2,1,0:T(8,128)(2,1)S(1)}, bf16[2,2,256,128]{3,2,1,0:T(8,128)(2,1)S(1)}, u32[]{:S(2)}, u32[]{:S(2)}) %collective-permute-start.3) | collective-permute-done | bytes 262176 | tf_op jit(solution)/shard_map/ppermute | solution.py:203
  63.4 9.3 %collective-permute-start.4 = (bf16[2,256,128]{2,1,0:T(8,128)(2,1)S(1)}, bf16[2,256,128]{2,1,0:T(8,128)(2,1)S(1)}, u32[]{:S(2)}, u32[]{:S(2)}) collective-permute-start(bf16[2,256,128]{2,1,0:T(8,128)(2,1)S(1)} %fusion), channel_id=1, source_target_pairs={{0,65},{1,64},{64,1},{65,0},{2,67},{3,66},{66,3},{67,2},{4,69},{5,... | collective-permute-start | bytes 393224 | tf_op jit(solution)/shard_map/ppermute | solution.py:207
  72.7 5.9 %all-to-all-start.2 = ((bf16[8,256,128]{2,1,0:T(8,128)(2,1)}), bf16[8,256,128]{2,1,0:T(8,128)(2,1)S(1)}, u32[]{:S(2)}, u32[]{:S(2)}) async-start(bf16[8,256,128]{2,1,0:T(8,128)(2,1)} %bitcast.6), calls=%async_computation.2 | async-start | bytes 1048576 | tf_op jit(solution)/shard_map/all_to_all | solution.py:327
  78.6 6.4 %collective-permute-done.4.arrived_ref = bf16[2,256,128]{2,1,0:T(8,128)(2,1)S(1)} collective-permute-done((bf16[2,256,128]{2,1,0:T(8,128)(2,1)S(1)}, bf16[2,256,128]{2,1,0:T(8,128)(2,1)S(1)}, u32[]{:S(2)}, u32[]{:S(2)}) %collective-permute-start.4) | collective-permute-done | bytes 131104 | tf_op jit(solution)/shard_map/ppermute | solution.py:207
  85.0 0.7 finish.1
  85.7 3.5 %all-to-all-done.2.parts_ref = bf16[8,256,128]{2,1,0:T(8,128)(2,1)S(1)} async-done(((bf16[8,256,128]{2,1,0:T(8,128)(2,1)}), bf16[8,256,128]{2,1,0:T(8,128)(2,1)S(1)}, u32[]{:S(2)}, u32[]{:S(2)}) %all-to-all-start.2) | async-done | bytes 524320 | tf_op jit(solution)/shard_map/all_to_all | solution.py:327
  89.2 0.7 sum.1
  (13 shorter events, 0.1 us)
Async XLA Ops:
  0.6 5.3 %copy-start = (bf16[1,1,256,128]{3,2,1,0:T(8,128)(2,1)S(1)}, bf16[1,1,256,128]{3,2,1,0:T(8,128)(2,1)}, u32[]{:S(2)}) copy-start(bf16[1,1,256,128]{3,2,1,0:T(8,128)(2,1)} %param.8) | copy-start | bytes 196612
  0.6 5.3 %copy-start.1 = (bf16[1,1,256,128]{3,2,1,0:T(8,128)(2,1)S(1)}, bf16[1,1,256,128]{3,2,1,0:T(8,128)(2,1)}, u32[]{:S(2)}) copy-start(bf16[1,1,256,128]{3,2,1,0:T(8,128)(2,1)} %param.7) | copy-start | bytes 196612
  1.6 18.6 %collective-permute-start.1 = (bf16[2,256,128]{2,1,0:T(8,128)(2,1)S(1)}, bf16[2,256,128]{2,1,0:T(8,128)(2,1)S(1)}, u32[]{:S(2)}, u32[]{:S(2)}) collective-permute-start(bf16[2,256,128]{2,1,0:T(8,128)(2,1)S(1)} %pad_maximum_fusion.1.own_ref), channel_id=1, source_target_pairs={{0,1},{1,0},{2,3},{3,2},{4,5},{5,4},{6,7},{7,6},{8,9},{9,8},{10,11... | collective-permute-start | bytes 393224 | tf_op jit(solution)/shard_map/ppermute | solution.py:203
  6.0 14.1 %copy-start.2 = (s32[64,32]{0,1:T(8,128)S(1)}, s32[64,32]{0,1:T(8,128)}, u32[]{:S(2)}) copy-start(s32[64,32]{0,1:T(8,128)} %param.10) | copy-start | bytes 24580
  6.0 19.4 %collective-permute-start = (bf16[2,256,128]{2,1,0:T(8,128)(2,1)S(1)}, bf16[2,256,128]{2,1,0:T(8,128)(2,1)S(1)}, u32[]{:S(2)}, u32[]{:S(2)}) collective-permute-start(bf16[2,256,128]{2,1,0:T(8,128)(2,1)S(1)} %pad_maximum_fusion.own_ref), channel_id=1, source_target_pairs={{0,65},{1,64},{64,1},{65,0},{2,67},{3,66},{66,3},{67,2},{4,69},{5,... | collective-permute-start | bytes 393224 | tf_op jit(solution)/shard_map/ppermute | solution.py:207
  21.4 17.6 %all-to-all-start = ((bf16[4,2,2,256,128]{4,3,2,1,0:T(8,128)(2,1)}), bf16[4,2,2,256,128]{4,3,2,1,0:T(8,128)(2,1)S(1)}, u32[]{:S(2)}, u32[]{:S(2)}) async-start(bf16[4,2,2,256,128]{4,3,2,1,0:T(8,128)(2,1)} %spread.1), calls=%async_computation | async-start | bytes 2097152 | tf_op jit(solution)/shard_map/all_to_all | solution.py:313
  26.3 9.9 %collective-permute-start.2 = (bf16[2,2,256,128]{3,2,1,0:T(8,128)(2,1)S(1)}, bf16[2,2,256,128]{3,2,1,0:T(8,128)(2,1)S(1)}, u32[]{:S(2)}, u32[]{:S(2)}) collective-permute-start(bf16[2,2,256,128]{3,2,1,0:T(8,128)(2,1)S(1)} %get-tuple-element.14.mine_ref), channel_id=1, source_target_pairs={{0,32},{32,0},{1,33},{33,1},{2,34},{34,2},{3,35},{35,3},{4,36},{36... | collective-permute-start | bytes 786440 | tf_op jit(solution)/shard_map/ppermute | solution.py:203
  42.1 4.4 %copy-start.3 = (s32[16,32,2]{1,2,0:T(2,128)S(1)}, s32[16,32,2]{1,2,0:T(2,128)}, u32[]{:S(2)}) copy-start(s32[16,32,2]{1,2,0:T(2,128)} %param.11) | copy-start | bytes 12292
  42.1 10.0 %all-to-all-start.1 = ((f32[8,4,2,1,512]{4,3,2,1,0:T(1,128)}), f32[8,4,2,1,512]{4,3,2,1,0:T(1,128)S(1)}, u32[]{:S(2)}, u32[]{:S(2)}) async-start(f32[8,4,2,1,512]{4,3,2,1,0:T(1,128)} %stats.1), calls=%async_computation.1 | async-start | bytes 262144 | tf_op jit(solution)/shard_map/all_to_all | solution.py:319
  56.8 6.5 %collective-permute-start.3 = (bf16[2,2,256,128]{3,2,1,0:T(8,128)(2,1)S(1)}, bf16[2,2,256,128]{3,2,1,0:T(8,128)(2,1)S(1)}, u32[]{:S(2)}, u32[]{:S(2)}) collective-permute-start(bf16[2,2,256,128]{3,2,1,0:T(8,128)(2,1)S(1)} %get-tuple-element.17), channel_id=1, source_target_pairs={{0,32},{32,0},{1,33},{33,1},{2,34},{34,2},{3,35},{35,3},{4,36},{36... | collective-permute-start | bytes 786440 | tf_op jit(solution)/shard_map/ppermute | solution.py:203
  63.4 21.6 %collective-permute-start.4 = (bf16[2,256,128]{2,1,0:T(8,128)(2,1)S(1)}, bf16[2,256,128]{2,1,0:T(8,128)(2,1)S(1)}, u32[]{:S(2)}, u32[]{:S(2)}) collective-permute-start(bf16[2,256,128]{2,1,0:T(8,128)(2,1)S(1)} %fusion), channel_id=1, source_target_pairs={{0,65},{1,64},{64,1},{65,0},{2,67},{3,66},{66,3},{67,2},{4,69},{5,... | collective-permute-start | bytes 393224 | tf_op jit(solution)/shard_map/ppermute | solution.py:207
  72.7 16.5 %all-to-all-start.2 = ((bf16[8,256,128]{2,1,0:T(8,128)(2,1)}), bf16[8,256,128]{2,1,0:T(8,128)(2,1)S(1)}, u32[]{:S(2)}, u32[]{:S(2)}) async-start(bf16[8,256,128]{2,1,0:T(8,128)(2,1)} %bitcast.6), calls=%async_computation.2 | async-start | bytes 1048576 | tf_op jit(solution)/shard_map/all_to_all | solution.py:327

commit v4 on v3

--- a/solution.py
+++ b/solution.py
@@ -34,55 +34,59 @@
         out_ref[j, 1 - half] = mate_ref[...]
 
 
-def mask_kernel(tiles_ref, own_ref, across_ref, far_ref, live_ref, mine_ref, table_ref):
-    mine_ref[0] = own_ref[...]
-    mine_ref[1] = across_ref[...]
+def mask_kernel(tiles_ref, after_ref, far_ref, live_ref, table_ref):
     x, zh, core, half = (lax.axis_index(name) for name in ("x", "zh", "c", "p"))
     tiles = tiles_ref[...]
     for k in range(2 * NCHUNK):
-        chunk_zh = zh if k // 2 % 2 == 0 else 1 - zh
-        chunk_core = core if k // 4 == 0 else 1 - core
-        chunk_half = half if k // 2 % 2 == 0 else 1 - half
-        key_id = (4 * x + 2 * chunk_zh + chunk_core) * 4 + 2 * chunk_half + k % 2
+        chunk_zh = zh if k // 4 == 0 else 1 - zh
+        chunk_half = half if k // 4 == 0 else 1 - half
+        key_id = (4 * x + 2 * chunk_zh + k // 2 % 2) * 4 + 2 * chunk_half + k % 2
         hit = jnp.where(tiles == key_id, 0.0, FAR)
         table_ref[k] = jnp.broadcast_to(jnp.min(hit, axis=1, keepdims=True), (64, TILE))
     for n in range(NX):
         first = (4 * n + 2 * zh + core) * 4
-        nearest = jnp.full((4, TILE), FAR, jnp.float32)
-        for k in range(2 * NCHUNK):
-            four = table_ref[k, pl.ds(first, 4), :]
-            nearest = jnp.minimum(nearest, four)
-            for h in range(2):
-                far_ref[n, h, k : k + 1, :TILE] = four[2 * h : 2 * h + 1]
-                far_ref[n, h, k : k + 1, TILE:] = four[2 * h + 1 : 2 * h + 2]
-        live_ref[n] = (jnp.min(nearest) < 1.0).astype(jnp.int32)
-
-
-def stats_kernel(live_ref, qg_ref, mine_ref, mate_ref, far_ref, out_ref):
-    chunks = (mine_ref.at[0], mine_ref.at[1], mate_ref.at[0], mate_ref.at[1])
+        for side in range(2):
+            nearest = jnp.full((4, TILE), FAR, jnp.float32)
+            for k in range(NCHUNK * side, NCHUNK * (side + 1)):
+                four = table_ref[k, pl.ds(first, 4), :]
+                nearest = jnp.minimum(nearest, four)
+                for h in range(2):
+                    far_ref[n, h, k : k + 1, :TILE] = four[2 * h : 2 * h + 1]
+                    far_ref[n, h, k : k + 1, TILE:] = four[2 * h + 1 : 2 * h + 2]
+            live_ref[2 * n + side] = (jnp.min(nearest) < 1.0).astype(jnp.int32)
+
+
+def by_sides(live_ref, n, work, nothing):
+    here, there = live_ref[2 * n], live_ref[2 * n + 1]
+    pl.when((here > 0) & (there > 0))(lambda: work((0, 1, 2, 3)))
+    pl.when((here > 0) & (there == 0))(lambda: work((0, 1)))
+    pl.when((here == 0) & (there > 0))(lambda: work((2, 3)))
+    pl.when((here == 0) & (there == 0))(nothing)
+
+
+def stats_kernel(live_ref, qg_ref, here_ref, there_ref, far_ref, out_ref):
+    chunks = (here_ref.at[0], here_ref.at[1], there_ref.at[0], there_ref.at[1])
 
     def group(n, carry):
-        @pl.when(live_ref[n] > 0)
-        def _():
+        def work(subset):
             for h in range(2):
                 q = qg_ref[n, h, 0]
                 g = qg_ref[n, h, 1]
                 far = far_ref[n, h]
-                scores = []
+                scores = {}
                 top = jnp.full((1, HALF), -FAR, jnp.float32)
-                for i, chunk in enumerate(chunks):
-                    s = dot_t(chunk[0], q)
+                for i in subset:
+                    s = dot_t(chunks[i][0], q)
                     for t in range(2):
-                        st = s[t * TILE : (t + 1) * TILE]
-                        scores.append(st)
                         k = 2 * i + t
-                        near = jnp.max(st, axis=0, keepdims=True) - far[k : k + 1]
+                        scores[k] = s[t * TILE : (t + 1) * TILE]
+                        near = jnp.max(scores[k], axis=0, keepdims=True) - far[k : k + 1]
                         top = jnp.maximum(top, near)
                 top = top * SCALE2
                 total = jnp.zeros((1, HALF), jnp.float32)
                 weighted = jnp.zeros((1, HALF), jnp.float32)
-                for i, chunk in enumerate(chunks):
-                    gp = dot_t(chunk[1], g)
+                for i in subset:
+                    gp = dot_t(chunks[i][1], g)
                     for t in range(2):
                         k = 2 * i + t
                         e = jnp.exp2(scores[k] * SCALE2 - (top + 4.0 * far[k : k + 1]))
@@ -98,13 +102,13 @@
                     out_ref[j, n, h, :, :HALF] = lse
                     out_ref[j, n, h, :, HALF:] = mean
 
-        @pl.when(live_ref[n] == 0)
-        def _():
+        def nothing():
             for j in range(BLOCKS):
                 for h in range(2):
                     out_ref[j, n, h, :, :HALF] = jnp.full((1, HALF), -FAR, jnp.float32)
                     out_ref[j, n, h, :, HALF:] = jnp.zeros((1, HALF), jnp.float32)
 
+        by_sides(live_ref, n, work, nothing)
         return carry
 
     lax.fori_loop(0, NX, group, 0)
@@ -114,8 +118,8 @@
     live_ref,
     work_ref,
     qg_ref,
-    mine_ref,
-    mate_ref,
+    here_ref,
+    there_ref,
     far_ref,
     stats_ref,
     keep_ref,
@@ -125,17 +129,18 @@
     dv_acc,
     kt_ref,
     ds_ref,
+    dq_buf,
+    sems,
 ):
     zh, core, head = (lax.axis_index(name) for name in ("zh", "c", "n"))
-    chunks = (mine_ref.at[0], mine_ref.at[1], mate_ref.at[0], mate_ref.at[1])
+    chunks = (here_ref.at[0], here_ref.at[1], there_ref.at[0], there_ref.at[1])
     dk_acc[...] = jnp.zeros_like(dk_acc)
     dv_acc[...] = jnp.zeros_like(dv_acc)
     for i, chunk in enumerate(chunks):
         kt_ref[:, i * HALF : (i + 1) * HALF] = chunk[0].T
 
     def group(n, carry):
-        @pl.when(live_ref[n] > 0)
-        def _():
+        def work(subset):
             q_all = qg_ref[n, :, 0].reshape(2 * HALF, HD)
             g_all = qg_ref[n, :, 1].reshape(2 * HALF, HD)
             rows_stats = []
@@ -149,13 +154,13 @@
                     total = total + w
                     weighted = weighted + w * stats_ref[j, n, h, :, HALF:]
                 rows_stats.append((top + jnp.log2(total), weighted / total))
-            for i, chunk in enumerate(chunks):
+            for i in subset:
                 rows = slice(i * HALF, (i + 1) * HALF)
                 ps, ds = [], []
                 for h in range(2):
                     lse, delta = rows_stats[h]
-                    s = dot_t(chunk[0], qg_ref[n, h, 0])
-                    gp = dot_t(chunk[1], qg_ref[n, h, 1])
+                    s = dot_t(chunks[i][0], qg_ref[n, h, 0])
+                    gp = dot_t(chunks[i][1], qg_ref[n, h, 1])
                     p_parts, d_parts = [], []
                     for t in range(2):
                         k = 2 * i + t
@@ -170,29 +175,33 @@
                     ds_ref[h, rows] = d
                 dv_acc[rows] += dot_n(jnp.concatenate(ps, axis=1), g_all)
                 dk_acc[rows] += dot_n(jnp.concatenate(ds, axis=1), q_all)
+            used = slice(subset[0] * HALF, (subset[-1] + 1) * HALF)
             for h in range(2):
-                dq = (dot_n(kt_ref[...], ds_ref[h]) * SCALE).T.astype(jnp.bfloat16)
+                dq = (dot_n(kt_ref[:, used], ds_ref[h, used]) * SCALE).T.astype(jnp.bfloat16)
                 for t in range(2):
                     slot = jnp.int32(3)
                     for w in range(3):
                         listed = work_ref[4 * n + 2 * zh + core, 4 * head + w]
                         slot = jnp.where(listed == 2 * h + t, w, slot)
-                    dq_ref[n, slot] = dq[t * TILE : (t + 1) * TILE]
-
-        @pl.when(live_ref[n] == 0)
-        def _():
-            dq_ref[n] = jnp.zeros((4, TILE, HD), jnp.bfloat16)
-
+                    dq_buf[n, slot] = dq[t * TILE : (t + 1) * TILE]
+
+        def nothing():
+            dq_buf[n] = jnp.zeros((4, TILE, HD), jnp.bfloat16)
+
+        by_sides(live_ref, n, work, nothing)
+        pltpu.make_async_copy(dq_buf.at[n], dq_ref.at[n], sems.at[n]).start()
         return carry
 
     lax.fori_loop(0, NX, group, 0)
     for i in range(2):
-        rows = slice(i * HALF, (i + 1) * HALF)
+        rows = pl.ds((2 * i + core) * HALF, HALF)
         keep_ref[i, 0] = dk_acc[rows] * SCALE
         keep_ref[i, 1] = dv_acc[rows]
-        rows = slice((i + 2) * HALF, (i + 3) * HALF)
+        rows = pl.ds((2 * i + 1 - core) * HALF, HALF)
         send_ref[i, 0] = (dk_acc[rows] * SCALE).astype(jnp.bfloat16)
         send_ref[i, 1] = dv_acc[rows].astype(jnp.bfloat16)
+    for n in range(NX):
+        pltpu.make_async_copy(dq_buf.at[n], dq_ref.at[n], sems.at[n]).wait()
 
 
 VMEM = pl.BlockSpec(memory_space=pltpu.VMEM)
@@ -218,21 +227,20 @@
     )(own, mate)
 
 
-def run_masks(tiles, own, arrived):
+def run_masks(tiles, after):
     return pl.pallas_call(
         mask_kernel,
         out_shape=[
             jax.ShapeDtypeStruct((NX, 2, 2 * NCHUNK, HALF), jnp.float32),
-            jax.ShapeDtypeStruct((NX,), jnp.int32),
-            jax.ShapeDtypeStruct((2,) + own.shape, own.dtype),
+            jax.ShapeDtypeStruct((2 * NX,), jnp.int32),
         ],
-        in_specs=[VMEM] * 3,
-        out_specs=[VMEM, SMEM, VMEM],
+        in_specs=[VMEM, pl.BlockSpec(memory_space=pl.ANY)],
+        out_specs=[VMEM, SMEM],
         scratch_shapes=[pltpu.VMEM((2 * NCHUNK, 64, TILE), jnp.float32)],
         compiler_params=pltpu.CompilerParams(vmem_limit_bytes=8 * 1024 * 1024),
-        cost_estimate=pl.CostEstimate(flops=10**11, bytes_accessed=2**20, transcendentals=0),
+        cost_estimate=pl.CostEstimate(flops=10**10, bytes_accessed=2**20, transcendentals=0),
         name="masks",
-    )(tiles, own, arrived)
+    )(tiles, after)
 
 
 def run_stats(live, qg, kv, far):
@@ -256,12 +264,14 @@
             jax.ShapeDtypeStruct((NX, 4, TILE, HD), jnp.bfloat16),
         ],
         in_specs=[SMEM, SMEM] + [VMEM] * 5,
-        out_specs=[VMEM] * 3,
+        out_specs=[VMEM, VMEM, pl.BlockSpec(memory_space=pl.ANY)],
         scratch_shapes=[
             pltpu.VMEM((NCHUNK * HALF, HD), jnp.float32),
             pltpu.VMEM((NCHUNK * HALF, HD), jnp.float32),
             pltpu.VMEM((HD, NCHUNK * HALF), jnp.bfloat16),
             pltpu.VMEM((2, NCHUNK * HALF, HALF), jnp.bfloat16),
+            pltpu.VMEM((NX, 4, TILE, HD), jnp.bfloat16),
+            pltpu.SemaphoreType.DMA((NX,)),
         ],
         compiler_params=pltpu.CompilerParams(vmem_limit_bytes=24 * 1024 * 1024),
         cost_estimate=pl.CostEstimate(flops=2 * 10**9, bytes_accessed=2**21, transcendentals=2**21),
@@ -311,8 +321,9 @@
     across_kv = across(own_kv)
     spread = run_spread(own_qg, mate_qg)
     all_qg = lax.all_to_all(spread, "x", 0, 0)
-    far, live, mine = run_masks(key_tiles, own_kv, across_kv)
-    kv = (mine, flipped(mine, "c"))
+    far, live = run_masks(key_tiles, spread)
+    own_kv, _ = lax.optimization_barrier((own_kv, far))
+    kv = (lax.all_gather(own_kv, "c"), lax.all_gather(across_kv, "c"))
     work = work_lists.reshape(16, 64)
 
     stats = run_stats(live, all_qg, kv, far)

time: 90.5 us -> 87.9 us (0.971)
  starting transfers between devices: 56.2 us -> 45 us
  blocking collectives: 0 us -> 7.57 us
  waiting for transfers between devices: 20.4 us -> 21.4 us
    ppermute x3 -> x2, starting transfers between devices: 18.5 us -> 10.2 us  [flipped(): return lax.ppermute(value, axis, [(0, 1), (1, 0)])]
    all_gather x0 -> x2, blocking collectives: none -> 7.57 us  [on_device(): kv = (lax.all_gather(own_kv, 'c'), lax.all_gather(across_kv, 'c'))]
    all_to_all x1, waiting for transfers between devices: 3.53 us -> 0.01 us  [on_device(): dq_parts = lax.all_to_all(dq, ('x', 'p'), 0, 0)]
    ppermute x2, waiting for transfers between devices: 6.41 us -> 9.78 us  [across(): return lax.ppermute(value, ('zh', 'p'), [(0, 3), (1, 2), (2, 1), (3, 0)])]
    all_to_all x1, waiting for transfers between devices: 2.78 us -> 5.12 us  [on_device(): all_qg = lax.all_to_all(spread, 'x', 0, 0)]
    ppermute x2, starting transfers between devices: 23.4 us -> 21.9 us  [across(): return lax.ppermute(value, ('zh', 'p'), [(0, 3), (1, 2), (2, 1), (3, 0)])]
    ppermute x3 -> x2, waiting for transfers between devices: 2.28 us -> 1.14 us  [flipped(): return lax.ppermute(value, axis, [(0, 1), (1, 0)])]
  transfers between devices with their start and end apart: 8 -> 7, of which waited for: 6 -> 4; matrix products, arithmetic and copies ran while one was open for 0% -> 0% of each run, Pallas kernels for 3% -> 3%
where the time goes in v4:
time: 87.9 us; the launch traced here: 87.3 us
  starting transfers between devices  45 us (51%)
  waiting for transfers between devices  21.4 us (24%)
  Pallas kernels  11.3 us (13%)
  blocking collectives  7.57 us (9%)
  other arithmetic  1 us (1%)
    ppermute x2, starting transfers between devices, across(): return lax.ppermute(value, ('zh', 'p'), [(0, 3), (1, 2), (2, 1), (3, 0)])  21.9 us
    ppermute x2, starting transfers between devices, flipped(): return lax.ppermute(value, axis, [(0, 1), (1, 0)])  10.2 us
    ppermute x2, waiting for transfers between devices, across(): return lax.ppermute(value, ('zh', 'p'), [(0, 3), (1, 2), (2, 1), (3, 0)])  9.78 us
    all_gather x2, blocking collectives, on_device(): kv = (lax.all_gather(own_kv, 'c'), lax.all_gather(across_kv, 'c'))  7.57 us
    all_to_all x1, waiting for transfers between devices, on_device(): stats = lax.all_to_all(stats, ('x', 'p'), 0, 0)  5.39 us
    all_to_all x1, starting transfers between devices, on_device(): dq_parts = lax.all_to_all(dq, ('x', 'p'), 0, 0)  5.32 us
    all_to_all x1, waiting for transfers between devices, on_device(): all_qg = lax.all_to_all(spread, 'x', 0, 0)  5.12 us
    pallas_call x1, Pallas kernels, run_grads(): pl.pallas_call(grads_kernel, out_shape=[jax.ShapeDtypeStruct((2, 2, HALF,...  4.68 us
  transfers between devices with their start and end apart: 7, of which 4 were waited for; matrix products, arithmetic and copies ran while one was open for 0% of the time, Pallas kernels for 3%

profile of v4, /device:TPU:1, one launch (start us, length us, event | category | flops | bytes accessed | tf_op | source)
XLA Modules:
  0.0 87.3 jit_solution(18392782896811931219)
XLA Ops:
  0.7 0.9 %pad_maximum_fusion.own_ref = bf16[2,256,128]{2,1,0:T(8,128)(2,1)S(1)} fusion(bf16[1,256,128]{2,1,0:T(8,128)(2,1)} %bitcast.19, bf16[1,256,128]{2,1,0:T(8,128)(2,1)} %bitcast.20), kind=kLoop, calls=%fused_computation.3 | loop fusion | flops 65536 | bytes 262144 | tf_op jit(solution)/shard_map/stack | solution.py:318
  1.6 4.4 %collective-permute-start = (bf16[2,256,128]{2,1,0:T(8,128)(2,1)S(1)}, bf16[2,256,128]{2,1,0:T(8,128)(2,1)S(1)}, u32[]{:S(2)}, u32[]{:S(2)}) collective-permute-start(bf16[2,256,128]{2,1,0:T(8,128)(2,1)S(1)} %pad_maximum_fusion.own_ref), channel_id=1, source_target_pairs={{0,1},{1,0},{2,3},{3,2},{4,5},{5,4},{6,7},{7,6},{8,9},{9,8},{10,11... | collective-permute-start | bytes 393224 | tf_op jit(solution)/shard_map/ppermute | solution.py:212
  6.0 14.1 %collective-permute-start.1 = (bf16[2,256,128]{2,1,0:T(8,128)(2,1)S(1)}, bf16[2,256,128]{2,1,0:T(8,128)(2,1)S(1)}, u32[]{:S(2)}, u32[]{:S(2)}) collective-permute-start(bf16[2,256,128]{2,1,0:T(8,128)(2,1)S(1)} %pad_maximum_fusion.1), channel_id=1, source_target_pairs={{0,65},{1,64},{64,1},{65,0},{2,67},{3,66},{66,3},{67,2},{4,69},{5,... | collective-permute-start | bytes 393224 | tf_op jit(solution)/shard_map/ppermute | solution.py:216
  20.1 0.1 copy.14.tiles_ref
  20.2 1.1 %spread.1.after_ref = bf16[4,2,2,256,128]{4,3,2,1,0:T(8,128)(2,1)} custom-call(bf16[2,256,128]{2,1,0:T(8,128)(2,1)S(1)} %pad_maximum_fusion.own_ref, bf16[2,256,128]{2,1,0:T(8,128)(2,1)S(1)} %collective-permute-done.mate_ref), custom_call_target="tpu_custom_call" | custom-call | tf_op jit(solution)/shard_map/spread/pallas_call | solution.py:220
  21.3 4.0 %all-to-all-start = ((bf16[4,2,2,256,128]{4,3,2,1,0:T(8,128)(2,1)}), bf16[4,2,2,256,128]{4,3,2,1,0:T(8,128)(2,1)S(1)}, u32[]{:S(2)}, u32[]{:S(2)}) async-start(bf16[4,2,2,256,128]{4,3,2,1,0:T(8,128)(2,1)} %spread.1.after_ref), calls=%async_computation | async-start | bytes 2097152 | tf_op jit(solution)/shard_map/all_to_all | solution.py:323
  25.4 0.9 %masks.1 = (f32[4,2,8,256]{3,2,1,0:T(8,128)S(1)}, s32[8]{0:T(128)S(1)}) custom-call(s32[64,32]{1,0:T(8,128)S(1)} %copy.14.tiles_ref, bf16[4,2,2,256,128]{4,3,2,1,0:T(8,128)(2,1)} %spread.1.after_ref), custom_call_target="tpu_custom_call" | custom-call | flops 10000000000 | bytes 1048576 | tf_op jit(solution)/shard_map/masks/pallas_call | solution.py:231
  26.3 3.1 %all-gather = bf16[4,256,128]{2,1,0:T(8,128)(2,1)S(1)} all-gather(bf16[2,256,128]{2,1,0:T(8,128)(2,1)S(1)} %pad_maximum_fusion.1), channel_id=2, replica_groups=mesh['x'=4,'zh'=2,'c'=2,'n'=16,'p'=2] {'c'}, dimensions={0}, use_global_device_ids=true | all-gather | bytes 393216 | tf_op jit(solution)/shard_map/all_gather | solution.py:326
  29.4 4.4 %all-gather.1 = bf16[4,256,128]{2,1,0:T(8,128)(2,1)S(1)} all-gather(bf16[2,256,128]{2,1,0:T(8,128)(2,1)S(1)} %collective-permute-done.1), channel_id=3, replica_groups=mesh['x'=4,'zh'=2,'c'=2,'n'=16,'p'=2] {'c'}, dimensions={0}, use_global_device_ids=true | all-gather | bytes 393216 | tf_op jit(solution)/shard_map/all_gather | solution.py:326
  33.8 5.1 %all-to-all-done.qg_ref = bf16[4,2,2,256,128]{4,3,2,1,0:T(8,128)(2,1)S(1)} async-done(((bf16[4,2,2,256,128]{4,3,2,1,0:T(8,128)(2,1)}), bf16[4,2,2,256,128]{4,3,2,1,0:T(8,128)(2,1)S(1)}, u32[]{:S(2)}, u32[]{:S(2)}) %all-to-all-start) | async-done | bytes 1048608 | tf_op jit(solution)/shard_map/all_to_all | solution.py:323
  39.0 3.2 %stats.1 = f32[8,4,2,1,512]{4,3,2,1,0:T(1,128)} custom-call(s32[8]{0:T(128)S(1)} %get-tuple-element.13.live_ref, bf16[4,2,2,256,128]{4,3,2,1,0:T(8,128)(2,1)S(1)} %all-to-all-done.qg_ref, bf16[2,2,256,128]{3,2,1,0:T(8,128)(2,1)S(1)} %bitcast.13, bf16[2,2,256,128]{3,2,1,0:T(8,128)(2,1)S(1)} %bitcast.15, f32[4,2,8,256]{3,2,1,0:T(8,128)S(1)} %get-tuple-element.14.far_ref), custom_call_target="tpu_custom_call" | custom-call | flops 1000000000 | bytes 2097152 | tf_op jit(solution)/shard_map/stats/pallas_call | solution.py:247
  42.1 3.6 %all-to-all-start.1 = ((f32[8,4,2,1,512]{4,3,2,1,0:T(1,128)}), f32[8,4,2,1,512]{4,3,2,1,0:T(1,128)S(1)}, u32[]{:S(2)}, u32[]{:S(2)}) async-start(f32[8,4,2,1,512]{4,3,2,1,0:T(1,128)} %stats.1), calls=%async_computation.1 | async-start | bytes 262144 | tf_op jit(solution)/shard_map/all_to_all | solution.py:330
  45.8 0.1 copy.15
  45.8 0.1 copy.16.work_ref
  45.9 5.4 %all-to-all-done.1.stats_ref = f32[8,4,2,1,512]{4,3,2,1,0:T(1,128)S(1)} async-done(((f32[8,4,2,1,512]{4,3,2,1,0:T(1,128)}), f32[8,4,2,1,512]{4,3,2,1,0:T(1,128)S(1)}, u32[]{:S(2)}, u32[]{:S(2)}) %all-to-all-start.1) | async-done | bytes 131104 | tf_op jit(solution)/shard_map/all_to_all | solution.py:330
  51.3 4.7 %grads.1 = (f32[2,2,256,128]{3,2,1,0:T(8,128)S(1)}, bf16[2,2,256,128]{3,2,1,0:T(8,128)(2,1)S(1)}, bf16[4,4,128,128]{3,2,1,0:T(8,128)(2,1)}) custom-call(s32[8]{0:T(128)S(1)} %get-tuple-element.13.live_ref, s32[16,64]{1,0:T(8,128)S(1)} %copy.16.work_ref, bf16[4,2,2,256,128]{4,3,2,1,0:T(8,128)(2,1)S(1)} %all-to-all-done.qg_ref, ...), custom_call_target="tpu_custom_call" | custom-call | flops 2000000000 | bytes 2097152 | tf_op jit(solution)/shard_map/grads/pallas_call | solution.py:259
  56.0 5.8 %collective-permute-start.2 = (bf16[2,2,256,128]{3,2,1,0:T(8,128)(2,1)S(1)}, bf16[2,2,256,128]{3,2,1,0:T(8,128)(2,1)S(1)}, u32[]{:S(2)}, u32[]{:S(2)}) collective-permute-start(bf16[2,2,256,128]{3,2,1,0:T(8,128)(2,1)S(1)} %get-tuple-element.17), channel_id=1, source_target_pairs={{0,32},{32,0},{1,33},{33,1},{2,34},{34,2},{3,35},{35,3},{4,36},{36... | collective-permute-start | bytes 786440 | tf_op jit(solution)/shard_map/ppermute | solution.py:212
  61.8 1.1 %collective-permute-done.2 = bf16[2,2,256,128]{3,2,1,0:T(8,128)(2,1)S(1)} collective-permute-done((bf16[2,2,256,128]{3,2,1,0:T(8,128)(2,1)S(1)}, bf16[2,2,256,128]{3,2,1,0:T(8,128)(2,1)S(1)}, u32[]{:S(2)}, u32[]{:S(2)}) %collective-permute-start.2) | collective-permute-done | bytes 262176 | tf_op jit(solution)/shard_map/ppermute | solution.py:212
  62.9 0.1 convert_add_fusion.total_ref
  63.0 7.8 %collective-permute-start.3 = (bf16[2,256,128]{2,1,0:T(8,128)(2,1)S(1)}, bf16[2,256,128]{2,1,0:T(8,128)(2,1)S(1)}, u32[]{:S(2)}, u32[]{:S(2)}) collective-permute-start(bf16[2,256,128]{2,1,0:T(8,128)(2,1)S(1)} %fusion), channel_id=1, source_target_pairs={{0,65},{1,64},{64,1},{65,0},{2,67},{3,66},{66,3},{67,2},{4,69},{5,... | collective-permute-start | bytes 393224 | tf_op jit(solution)/shard_map/ppermute | solution.py:216
  70.8 5.3 %all-to-all-start.2 = ((bf16[8,256,128]{2,1,0:T(8,128)(2,1)}), bf16[8,256,128]{2,1,0:T(8,128)(2,1)S(1)}, u32[]{:S(2)}, u32[]{:S(2)}) async-start(bf16[8,256,128]{2,1,0:T(8,128)(2,1)} %bitcast.8), calls=%async_computation.2 | async-start | bytes 1048576 | tf_op jit(solution)/shard_map/all_to_all | solution.py:338
  76.2 9.8 %collective-permute-done.3.arrived_ref = bf16[2,256,128]{2,1,0:T(8,128)(2,1)S(1)} collective-permute-done((bf16[2,256,128]{2,1,0:T(8,128)(2,1)S(1)}, bf16[2,256,128]{2,1,0:T(8,128)(2,1)S(1)}, u32[]{:S(2)}, u32[]{:S(2)}) %collective-permute-start.3) | collective-permute-done | bytes 131104 | tf_op jit(solution)/shard_map/ppermute | solution.py:216
  85.9 0.7 finish.1
  86.6 0.7 sum.1
  (13 shorter events, 0.1 us)
Async XLA Ops:
  0.6 5.3 %copy-start = (bf16[1,1,256,128]{3,2,1,0:T(8,128)(2,1)S(1)}, bf16[1,1,256,128]{3,2,1,0:T(8,128)(2,1)}, u32[]{:S(2)}) copy-start(bf16[1,1,256,128]{3,2,1,0:T(8,128)(2,1)} %param.8) | copy-start | bytes 196612
  0.6 5.3 %copy-start.1 = (bf16[1,1,256,128]{3,2,1,0:T(8,128)(2,1)S(1)}, bf16[1,1,256,128]{3,2,1,0:T(8,128)(2,1)}, u32[]{:S(2)}) copy-start(bf16[1,1,256,128]{3,2,1,0:T(8,128)(2,1)} %param.7) | copy-start | bytes 196612
  1.6 18.6 %collective-permute-start = (bf16[2,256,128]{2,1,0:T(8,128)(2,1)S(1)}, bf16[2,256,128]{2,1,0:T(8,128)(2,1)S(1)}, u32[]{:S(2)}, u32[]{:S(2)}) collective-permute-start(bf16[2,256,128]{2,1,0:T(8,128)(2,1)S(1)} %pad_maximum_fusion.own_ref), channel_id=1, source_target_pairs={{0,1},{1,0},{2,3},{3,2},{4,5},{5,4},{6,7},{7,6},{8,9},{9,8},{10,11... | collective-permute-start | bytes 393224 | tf_op jit(solution)/shard_map/ppermute | solution.py:212
  6.0 14.1 %copy-start.2 = (s32[64,32]{0,1:T(8,128)S(1)}, s32[64,32]{0,1:T(8,128)}, u32[]{:S(2)}) copy-start(s32[64,32]{0,1:T(8,128)} %param.10) | copy-start | bytes 24580
  6.0 23.4 %collective-permute-start.1 = (bf16[2,256,128]{2,1,0:T(8,128)(2,1)S(1)}, bf16[2,256,128]{2,1,0:T(8,128)(2,1)S(1)}, u32[]{:S(2)}, u32[]{:S(2)}) collective-permute-start(bf16[2,256,128]{2,1,0:T(8,128)(2,1)S(1)} %pad_maximum_fusion.1), channel_id=1, source_target_pairs={{0,65},{1,64},{64,1},{65,0},{2,67},{3,66},{66,3},{67,2},{4,69},{5,... | collective-permute-start | bytes 393224 | tf_op jit(solution)/shard_map/ppermute | solution.py:216
  21.3 17.6 %all-to-all-start = ((bf16[4,2,2,256,128]{4,3,2,1,0:T(8,128)(2,1)}), bf16[4,2,2,256,128]{4,3,2,1,0:T(8,128)(2,1)S(1)}, u32[]{:S(2)}, u32[]{:S(2)}) async-start(bf16[4,2,2,256,128]{4,3,2,1,0:T(8,128)(2,1)} %spread.1.after_ref), calls=%async_computation | async-start | bytes 2097152 | tf_op jit(solution)/shard_map/all_to_all | solution.py:323
  42.1 3.6 %copy-start.3 = (s32[16,32,2]{1,2,0:T(2,128)S(1)}, s32[16,32,2]{1,2,0:T(2,128)}, u32[]{:S(2)}) copy-start(s32[16,32,2]{1,2,0:T(2,128)} %param.11) | copy-start | bytes 12292
  42.1 9.2 %all-to-all-start.1 = ((f32[8,4,2,1,512]{4,3,2,1,0:T(1,128)}), f32[8,4,2,1,512]{4,3,2,1,0:T(1,128)S(1)}, u32[]{:S(2)}, u32[]{:S(2)}) async-start(f32[8,4,2,1,512]{4,3,2,1,0:T(1,128)} %stats.1), calls=%async_computation.1 | async-start | bytes 262144 | tf_op jit(solution)/shard_map/all_to_all | solution.py:330
  56.0 6.9 %collective-permute-start.2 = (bf16[2,2,256,128]{3,2,1,0:T(8,128)(2,1)S(1)}, bf16[2,2,256,128]{3,2,1,0:T(8,128)(2,1)S(1)}, u32[]{:S(2)}, u32[]{:S(2)}) collective-permute-start(bf16[2,2,256,128]{3,2,1,0:T(8,128)(2,1)S(1)} %get-tuple-element.17), channel_id=1, source_target_pairs={{0,32},{32,0},{1,33},{33,1},{2,34},{34,2},{3,35},{35,3},{4,36},{36... | collective-permute-start | bytes 786440 | tf_op jit(solution)/shard_map/ppermute | solution.py:212
  63.0 22.9 %collective-permute-start.3 = (bf16[2,256,128]{2,1,0:T(8,128)(2,1)S(1)}, bf16[2,256,128]{2,1,0:T(8,128)(2,1)S(1)}, u32[]{:S(2)}, u32[]{:S(2)}) collective-permute-start(bf16[2,256,128]{2,1,0:T(8,128)(2,1)S(1)} %fusion), channel_id=1, source_target_pairs={{0,65},{1,64},{64,1},{65,0},{2,67},{3,66},{66,3},{67,2},{4,69},{5,... | collective-permute-start | bytes 393224 | tf_op jit(solution)/shard_map/ppermute | solution.py:216
  70.8 15.8 %all-to-all-start.2 = ((bf16[8,256,128]{2,1,0:T(8,128)(2,1)}), bf16[8,256,128]{2,1,0:T(8,128)(2,1)S(1)}, u32[]{:S(2)}, u32[]{:S(2)}) async-start(bf16[8,256,128]{2,1,0:T(8,128)(2,1)} %bitcast.8), calls=%async_computation.2 | async-start | bytes 1048576 | tf_op jit(solution)/shard_map/all_to_all | solution.py:338

commit v5 on v4

--- a/solution.py
+++ b/solution.py
@@ -114,6 +114,12 @@
     lax.fori_loop(0, NX, group, 0)
 
 
+def turn_kernel(here_ref, there_ref, after_ref, kt_ref):
+    chunks = (here_ref.at[0], here_ref.at[1], there_ref.at[0], there_ref.at[1])
+    for i, chunk in enumerate(chunks):
+        kt_ref[:, i * HALF : (i + 1) * HALF] = chunk[0].T
+
+
 def grads_kernel(
     live_ref,
     work_ref,
@@ -122,12 +128,13 @@
     there_ref,
     far_ref,
     stats_ref,
+    kt_ref,
     keep_ref,
-    send_ref,
+    send_here_ref,
+    send_there_ref,
     dq_ref,
     dk_acc,
     dv_acc,
-    kt_ref,
     ds_ref,
     dq_buf,
     sems,
@@ -136,8 +143,6 @@
     chunks = (here_ref.at[0], here_ref.at[1], there_ref.at[0], there_ref.at[1])
     dk_acc[...] = jnp.zeros_like(dk_acc)
     dv_acc[...] = jnp.zeros_like(dv_acc)
-    for i, chunk in enumerate(chunks):
-        kt_ref[:, i * HALF : (i + 1) * HALF] = chunk[0].T
 
     def group(n, carry):
         def work(subset):
@@ -193,13 +198,13 @@
         return carry
 
     lax.fori_loop(0, NX, group, 0)
-    for i in range(2):
+    for i, send_ref in enumerate((send_here_ref, send_there_ref)):
         rows = pl.ds((2 * i + core) * HALF, HALF)
         keep_ref[i, 0] = dk_acc[rows] * SCALE
         keep_ref[i, 1] = dv_acc[rows]
         rows = pl.ds((2 * i + 1 - core) * HALF, HALF)
-        send_ref[i, 0] = (dk_acc[rows] * SCALE).astype(jnp.bfloat16)
-        send_ref[i, 1] = dv_acc[rows].astype(jnp.bfloat16)
+        send_ref[0] = (dk_acc[rows] * SCALE).astype(jnp.bfloat16)
+        send_ref[1] = dv_acc[rows].astype(jnp.bfloat16)
     for n in range(NX):
         pltpu.make_async_copy(dq_buf.at[n], dq_ref.at[n], sems.at[n]).wait()
 
@@ -255,20 +260,32 @@
     )(live, qg, *kv, far)
 
 
-def run_grads(live, work, qg, kv, far, stats):
+def run_turn(kv, after):
+    return pl.pallas_call(
+        turn_kernel,
+        out_shape=jax.ShapeDtypeStruct((HD, NCHUNK * HALF), jnp.bfloat16),
+        in_specs=[VMEM, VMEM, pl.BlockSpec(memory_space=pl.ANY)],
+        out_specs=VMEM,
+        compiler_params=pltpu.CompilerParams(vmem_limit_bytes=8 * 1024 * 1024),
+        cost_estimate=pl.CostEstimate(flops=10**9, bytes_accessed=2**20, transcendentals=0),
+        name="turn",
+    )(*kv, after)
+
+
+def run_grads(live, work, qg, kv, far, stats, kt):
     return pl.pallas_call(
         grads_kernel,
         out_shape=[
             jax.ShapeDtypeStruct((2, 2, HALF, HD), jnp.float32),
-            jax.ShapeDtypeStruct((2, 2, HALF, HD), jnp.bfloat16),
+            jax.ShapeDtypeStruct((2, HALF, HD), jnp.bfloat16),
+            jax.ShapeDtypeStruct((2, HALF, HD), jnp.bfloat16),
             jax.ShapeDtypeStruct((NX, 4, TILE, HD), jnp.bfloat16),
         ],
-        in_specs=[SMEM, SMEM] + [VMEM] * 5,
-        out_specs=[VMEM, VMEM, pl.BlockSpec(memory_space=pl.ANY)],
+        in_specs=[SMEM, SMEM] + [VMEM] * 6,
+        out_specs=[VMEM, VMEM, VMEM, pl.BlockSpec(memory_space=pl.ANY)],
         scratch_shapes=[
             pltpu.VMEM((NCHUNK * HALF, HD), jnp.float32),
             pltpu.VMEM((NCHUNK * HALF, HD), jnp.float32),
-            pltpu.VMEM((HD, NCHUNK * HALF), jnp.bfloat16),
             pltpu.VMEM((2, NCHUNK * HALF, HALF), jnp.bfloat16),
             pltpu.VMEM((NX, 4, TILE, HD), jnp.bfloat16),
             pltpu.SemaphoreType.DMA((NX,)),
@@ -276,24 +293,25 @@
         compiler_params=pltpu.CompilerParams(vmem_limit_bytes=24 * 1024 * 1024),
         cost_estimate=pl.CostEstimate(flops=2 * 10**9, bytes_accessed=2**21, transcendentals=2**21),
         name="grads",
-    )(live, work, qg, *kv, far, stats)
-
-
-def finish_kernel(total_ref, arrived_ref, dk_ref, dv_ref):
-    dk_ref[...] = (total_ref[0, 0] + arrived_ref[0].astype(jnp.float32)).astype(jnp.bfloat16)
-    dv_ref[...] = (total_ref[0, 1] + arrived_ref[1].astype(jnp.float32)).astype(jnp.bfloat16)
-
-
-def run_finish(total, arrived):
+    )(live, work, qg, *kv, far, stats, kt)
+
+
+def finish_kernel(keep_ref, sibling_ref, arrived_ref, dk_ref, dv_ref):
+    for i, out_ref in enumerate((dk_ref, dv_ref)):
+        total = keep_ref[0, i] + sibling_ref[i].astype(jnp.float32)
+        out_ref[...] = (total + arrived_ref[i].astype(jnp.float32)).astype(jnp.bfloat16)
+
+
+def run_finish(keep, sibling, arrived):
     return pl.pallas_call(
         finish_kernel,
         out_shape=[jax.ShapeDtypeStruct((HALF, HD), jnp.bfloat16)] * 2,
-        in_specs=[VMEM] * 2,
+        in_specs=[VMEM] * 3,
         out_specs=[VMEM] * 2,
         compiler_params=pltpu.CompilerParams(vmem_limit_bytes=8 * 1024 * 1024),
         cost_estimate=pl.CostEstimate(flops=10**11, bytes_accessed=2**20, transcendentals=0),
         name="finish",
-    )(total, arrived)
+    )(keep, sibling, arrived)
 
 
 def sum_kernel(parts_ref, dq_ref):
@@ -326,17 +344,19 @@
     kv = (lax.all_gather(own_kv, "c"), lax.all_gather(across_kv, "c"))
     work = work_lists.reshape(16, 64)
 
-    stats = run_stats(live, all_qg, kv, far)
-    stats = lax.all_to_all(stats, ("x", "p"), 0, 0)
-    keep, send, dq = run_grads(live, work, all_qg, kv, far, stats)
-
-    total = keep + flipped(send, "c").astype(jnp.float32)
-    dkv_out = total[1].astype(jnp.bfloat16)
-    dkv_out, dq = lax.optimization_barrier((dkv_out, dq))
+    own_stats = run_stats(live, all_qg, kv, far)
+    kt = run_turn(kv, own_stats)
+    stats = lax.all_to_all(own_stats, ("x", "p"), 0, 0)
+    keep, send_here, send_there, dq = run_grads(live, work, all_qg, kv, far, stats, kt)
+
+    sibling = 1 - lax.axis_index("c")
+    there = lax.dynamic_index_in_dim(lax.all_gather(send_there, "c"), sibling, 0, False)
+    dkv_out = (keep[1] + there.astype(jnp.float32)).astype(jnp.bfloat16)
+    dkv_out, dq, send_here = lax.optimization_barrier((dkv_out, dq, send_here))
     from_across = across(dkv_out)
-    dq = dq.reshape(BLOCKS, HALF, HD)
-    dq_parts = lax.all_to_all(dq, ("x", "p"), 0, 0)
-    grad_keys, grad_values = run_finish(total, from_across)
+    dq_parts = lax.all_to_all(dq.reshape(BLOCKS, HALF, HD), ("x", "p"), 0, 0)
+    here = lax.dynamic_index_in_dim(lax.all_gather(send_here, "c"), sibling, 0, False)
+    grad_keys, grad_values = run_finish(keep, here, from_across)
     outs = (run_sum(dq_parts), grad_keys, grad_values)
     return tuple(out[None, None] for out in outs)
 

time: 87.9 us -> 87.8 us (level)
  blocking collectives: 7.57 us -> 16.3 us
  starting transfers between devices: 45 us -> 38.2 us
  waiting for transfers between devices: 21.4 us -> 18.9 us
    all_gather x0 -> x2, blocking collectives: none -> 8.76 us  [the longest x1 6.49 us: on_device(): lax.all_gather(send_there, 'c')]
    ppermute x2 -> x1, starting transfers between devices: 10.2 us -> 4.38 us  [flipped(): return lax.ppermute(value, axis, [(0, 1), (1, 0)])]
    ppermute x2, waiting for transfers between devices: 9.78 us -> 6.87 us  [across(): return lax.ppermute(value, ('zh', 'p'), [(0, 3), (1, 2), (2, 1), (3, 0)])]
    ppermute x2, starting transfers between devices: 21.9 us -> 20.3 us  [across(): return lax.ppermute(value, ('zh', 'p'), [(0, 3), (1, 2), (2, 1), (3, 0)])]
    all_to_all x2, waiting for transfers between devices: 5.39 us -> 6.93 us  [the longest x1 5.26 us: on_device(): stats = lax.all_to_all(own_stats, ('x', 'p'), 0, 0)]
    ppermute x2 -> x1, waiting for transfers between devices: 1.14 us -> 0.01 us  [flipped(): return lax.ppermute(value, axis, [(0, 1), (1, 0)])]
  transfers between devices with their start and end apart: 7 -> 6, of which waited for: 4 -> 4; matrix products, arithmetic and copies ran while one was open for 0% -> 0% of each run, Pallas kernels for 3% -> 3%
where the time goes in v5:
time: 87.8 us; the launch traced here: 86.9 us
  starting transfers between devices  38.2 us (44%)
  waiting for transfers between devices  18.9 us (22%)
  blocking collectives  16.3 us (19%)
  Pallas kernels  11.4 us (13%)
  other arithmetic  0.97 us (1%)
    ppermute x2, starting transfers between devices, across(): return lax.ppermute(value, ('zh', 'p'), [(0, 3), (1, 2), (2, 1), (3, 0)])  20.3 us
    all_gather x2, blocking collectives, on_device(): kv = (lax.all_gather(own_kv, 'c'), lax.all_gather(across_kv, 'c'))  7.56 us
    ppermute x2, waiting for transfers between devices, across(): return lax.ppermute(value, ('zh', 'p'), [(0, 3), (1, 2), (2, 1), (3, 0)])  6.87 us
    all_gather x1, blocking collectives, on_device(): lax.all_gather(send_there, 'c')  6.49 us
    all_to_all x1, starting transfers between devices, on_device(): dq_parts = lax.all_to_all(dq.reshape(BLOCKS, HALF, HD), ('x', 'p'), 0, 0)  5.95 us
    all_to_all x1, waiting for transfers between devices, on_device(): stats = lax.all_to_all(own_stats, ('x', 'p'), 0, 0)  5.26 us
    all_to_all x1, waiting for transfers between devices, on_device(): all_qg = lax.all_to_all(spread, 'x', 0, 0)  5.12 us
    pallas_call x1, Pallas kernels, run_grads(): pl.pallas_call(grads_kernel, out_shape=[jax.ShapeDtypeStruct((2, 2, HALF,...  4.67 us
  transfers between devices with their start and end apart: 6, of which 4 were waited for; matrix products, arithmetic and copies ran while one was open for 0% of the time, Pallas kernels for 3%

profile of v5, /device:TPU:1, one launch (start us, length us, event | category | flops | bytes accessed | tf_op | source)
XLA Modules:
  0.0 86.9 jit_solution(13522294710864292216)
XLA Ops:
  0.7 0.9 %pad_maximum_fusion.own_ref = bf16[2,256,128]{2,1,0:T(8,128)(2,1)S(1)} fusion(bf16[1,256,128]{2,1,0:T(8,128)(2,1)} %bitcast.27, bf16[1,256,128]{2,1,0:T(8,128)(2,1)} %bitcast.28), kind=kLoop, calls=%fused_computation.2 | loop fusion | flops 65536 | bytes 262144 | tf_op jit(solution)/shard_map/stack | solution.py:336
  1.6 4.4 %collective-permute-start = (bf16[2,256,128]{2,1,0:T(8,128)(2,1)S(1)}, bf16[2,256,128]{2,1,0:T(8,128)(2,1)S(1)}, u32[]{:S(2)}, u32[]{:S(2)}) collective-permute-start(bf16[2,256,128]{2,1,0:T(8,128)(2,1)S(1)} %pad_maximum_fusion.own_ref), channel_id=1, source_target_pairs={{0,1},{1,0},{2,3},{3,2},{4,5},{5,4},{6,7},{7,6},{8,9},{9,8},{10,11... | collective-permute-start | bytes 393224 | tf_op jit(solution)/shard_map/ppermute | solution.py:217
  6.0 14.1 %collective-permute-start.1 = (bf16[2,256,128]{2,1,0:T(8,128)(2,1)S(1)}, bf16[2,256,128]{2,1,0:T(8,128)(2,1)S(1)}, u32[]{:S(2)}, u32[]{:S(2)}) collective-permute-start(bf16[2,256,128]{2,1,0:T(8,128)(2,1)S(1)} %pad_maximum_fusion.1), channel_id=1, source_target_pairs={{0,65},{1,64},{64,1},{65,0},{2,67},{3,66},{66,3},{67,2},{4,69},{5,... | collective-permute-start | bytes 393224 | tf_op jit(solution)/shard_map/ppermute | solution.py:221
  20.1 0.1 copy.14.tiles_ref
  20.2 1.1 %spread.1.after_ref = bf16[4,2,2,256,128]{4,3,2,1,0:T(8,128)(2,1)} custom-call(bf16[2,256,128]{2,1,0:T(8,128)(2,1)S(1)} %pad_maximum_fusion.own_ref, bf16[2,256,128]{2,1,0:T(8,128)(2,1)S(1)} %collective-permute-done.mate_ref), custom_call_target="tpu_custom_call" | custom-call | tf_op jit(solution)/shard_map/spread/pallas_call | solution.py:225
  21.3 4.0 %all-to-all-start = ((bf16[4,2,2,256,128]{4,3,2,1,0:T(8,128)(2,1)}), bf16[4,2,2,256,128]{4,3,2,1,0:T(8,128)(2,1)S(1)}, u32[]{:S(2)}, u32[]{:S(2)}) async-start(bf16[4,2,2,256,128]{4,3,2,1,0:T(8,128)(2,1)} %spread.1.after_ref), calls=%async_computation | async-start | bytes 2097152 | tf_op jit(solution)/shard_map/all_to_all | solution.py:341
  25.4 0.9 %masks.1 = (f32[4,2,8,256]{3,2,1,0:T(8,128)S(1)}, s32[8]{0:T(128)S(1)}) custom-call(s32[64,32]{1,0:T(8,128)S(1)} %copy.14.tiles_ref, bf16[4,2,2,256,128]{4,3,2,1,0:T(8,128)(2,1)} %spread.1.after_ref), custom_call_target="tpu_custom_call" | custom-call | flops 10000000000 | bytes 1048576 | tf_op jit(solution)/shard_map/masks/pallas_call | solution.py:236
  26.3 3.1 %all-gather = bf16[4,256,128]{2,1,0:T(8,128)(2,1)S(1)} all-gather(bf16[2,256,128]{2,1,0:T(8,128)(2,1)S(1)} %pad_maximum_fusion.1), channel_id=2, replica_groups=mesh['x'=4,'zh'=2,'c'=2,'n'=16,'p'=2] {'c'}, dimensions={0}, use_global_device_ids=true | all-gather | bytes 393216 | tf_op jit(solution)/shard_map/all_gather | solution.py:344
  29.4 4.4 %all-gather.1 = bf16[4,256,128]{2,1,0:T(8,128)(2,1)S(1)} all-gather(bf16[2,256,128]{2,1,0:T(8,128)(2,1)S(1)} %collective-permute-done.1), channel_id=3, replica_groups=mesh['x'=4,'zh'=2,'c'=2,'n'=16,'p'=2] {'c'}, dimensions={0}, use_global_device_ids=true | all-gather | bytes 393216 | tf_op jit(solution)/shard_map/all_gather | solution.py:344
  33.8 5.1 %all-to-all-done.qg_ref = bf16[4,2,2,256,128]{4,3,2,1,0:T(8,128)(2,1)S(1)} async-done(((bf16[4,2,2,256,128]{4,3,2,1,0:T(8,128)(2,1)}), bf16[4,2,2,256,128]{4,3,2,1,0:T(8,128)(2,1)S(1)}, u32[]{:S(2)}, u32[]{:S(2)}) %all-to-all-start) | async-done | bytes 1048608 | tf_op jit(solution)/shard_map/all_to_all | solution.py:341
  39.0 3.2 %stats.1.after_ref = f32[8,4,2,1,512]{4,3,2,1,0:T(1,128)} custom-call(s32[8]{0:T(128)S(1)} %get-tuple-element.15.live_ref, bf16[4,2,2,256,128]{4,3,2,1,0:T(8,128)(2,1)S(1)} %all-to-all-done.qg_ref, bf16[2,2,256,128]{3,2,1,0:T(8,128)(2,1)S(1)} %bitcast.17, bf16[2,2,256,128]{3,2,1,0:T(8,128)(2,1)S(1)} %bitcast.20, f32[4,2,8,256]{3,2,1,0:T(8,128)S(1)} %get-tuple-element.16.far_ref), custom_call_target="tpu_custom_call" | custom-call | flops 1000000000 | bytes 2097152 | tf_op jit(solution)/shard_map/stats/pallas_call | solution.py:252
  42.2 3.6 %all-to-all-start.1 = ((f32[8,4,2,1,512]{4,3,2,1,0:T(1,128)}), f32[8,4,2,1,512]{4,3,2,1,0:T(1,128)S(1)}, u32[]{:S(2)}, u32[]{:S(2)}) async-start(f32[8,4,2,1,512]{4,3,2,1,0:T(1,128)} %stats.1.after_ref), calls=%async_computation.1 | async-start | bytes 262144 | tf_op jit(solution)/shard_map/all_to_all | solution.py:349
  45.8 0.1 copy.15
  45.9 0.1 turn.1.kt_ref
  46.1 5.3 %all-to-all-done.1.stats_ref = f32[8,4,2,1,512]{4,3,2,1,0:T(1,128)S(1)} async-done(((f32[8,4,2,1,512]{4,3,2,1,0:T(1,128)}), f32[8,4,2,1,512]{4,3,2,1,0:T(1,128)S(1)}, u32[]{:S(2)}, u32[]{:S(2)}) %all-to-all-start.1) | async-done | bytes 131104 | tf_op jit(solution)/shard_map/all_to_all | solution.py:349
  51.3 4.7 %grads.1 = (f32[2,2,256,128]{3,2,1,0:T(8,128)S(1)}, bf16[2,256,128]{2,1,0:T(8,128)(2,1)S(1)}, bf16[2,256,128]{2,1,0:T(8,128)(2,1)S(1)}, bf16[4,4,128,128]{3,2,1,0:T(8,128)(2,1)}) custom-call(s32[8]{0:T(128)S(1)} %get-tuple-element.15.live_ref, s32[16,64]{1,0:T(8,128)S(1)} %copy.16.work_ref, bf16[4,2,2,256,128]{4,3,2,1,0:T(8,128)(2,1)S(1)} %all-to-all-done.qg_ref, ...), custom_call_target="tpu_custom_call" | custom-call | flops 2000000000 | bytes 2097152 | tf_op jit(solution)/shard_map/grads/pallas_call | solution.py:276
  56.0 6.5 %all-gather.2 = bf16[4,256,128]{2,1,0:T(8,128)(2,1)S(1)} all-gather(bf16[2,256,128]{2,1,0:T(8,128)(2,1)S(1)} %get-tuple-element.19), channel_id=4, replica_groups=mesh['x'=4,'zh'=2,'c'=2,'n'=16,'p'=2] {'c'}, dimensions={0}, use_global_device_ids=true | all-gather | bytes 393216 | tf_op jit(solution)/shard_map/all_gather | solution.py:353
  62.5 6.2 %collective-permute-start.2 = (bf16[2,256,128]{2,1,0:T(8,128)(2,1)S(1)}, bf16[2,256,128]{2,1,0:T(8,128)(2,1)S(1)}, u32[]{:S(2)}, u32[]{:S(2)}) collective-permute-start(bf16[2,256,128]{2,1,0:T(8,128)(2,1)S(1)} %fusion), channel_id=1, source_target_pairs={{0,65},{1,64},{64,1},{65,0},{2,67},{3,66},{66,3},{67,2},{4,69},{5,... | collective-permute-start | bytes 393224 | tf_op jit(solution)/shard_map/ppermute | solution.py:221
  68.7 2.3 %all-gather.3 = bf16[4,256,128]{2,1,0:T(8,128)(2,1)S(1)} all-gather(bf16[2,256,128]{2,1,0:T(8,128)(2,1)S(1)} %get-tuple-element.23), channel_id=5, replica_groups=mesh['x'=4,'zh'=2,'c'=2,'n'=16,'p'=2] {'c'}, dimensions={0}, use_global_device_ids=true | all-gather | bytes 393216 | tf_op jit(solution)/shard_map/all_gather | solution.py:358
  71.0 6.0 %all-to-all-start.2 = ((bf16[8,256,128]{2,1,0:T(8,128)(2,1)}), bf16[8,256,128]{2,1,0:T(8,128)(2,1)S(1)}, u32[]{:S(2)}, u32[]{:S(2)}) async-start(bf16[8,256,128]{2,1,0:T(8,128)(2,1)} %bitcast.9), calls=%async_computation.2 | async-start | bytes 1048576 | tf_op jit(solution)/shard_map/all_to_all | solution.py:357
  77.0 6.9 %collective-permute-done.2.arrived_ref = bf16[2,256,128]{2,1,0:T(8,128)(2,1)S(1)} collective-permute-done((bf16[2,256,128]{2,1,0:T(8,128)(2,1)S(1)}, bf16[2,256,128]{2,1,0:T(8,128)(2,1)S(1)}, u32[]{:S(2)}, u32[]{:S(2)}) %collective-permute-start.2) | collective-permute-done | bytes 131104 | tf_op jit(solution)/shard_map/ppermute | solution.py:221
  83.8 0.7 finish.1
  84.5 1.7 %all-to-all-done.2.parts_ref = bf16[8,256,128]{2,1,0:T(8,128)(2,1)S(1)} async-done(((bf16[8,256,128]{2,1,0:T(8,128)(2,1)}), bf16[8,256,128]{2,1,0:T(8,128)(2,1)S(1)}, u32[]{:S(2)}, u32[]{:S(2)}) %all-to-all-start.2) | async-done | bytes 524320 | tf_op jit(solution)/shard_map/all_to_all | solution.py:357
  86.2 0.7 sum.1
  (14 shorter events, 0.1 us)
Async XLA Ops:
  0.6 5.3 %copy-start = (bf16[1,1,256,128]{3,2,1,0:T(8,128)(2,1)S(1)}, bf16[1,1,256,128]{3,2,1,0:T(8,128)(2,1)}, u32[]{:S(2)}) copy-start(bf16[1,1,256,128]{3,2,1,0:T(8,128)(2,1)} %param.8) | copy-start | bytes 196612
  0.6 5.3 %copy-start.1 = (bf16[1,1,256,128]{3,2,1,0:T(8,128)(2,1)S(1)}, bf16[1,1,256,128]{3,2,1,0:T(8,128)(2,1)}, u32[]{:S(2)}) copy-start(bf16[1,1,256,128]{3,2,1,0:T(8,128)(2,1)} %param.7) | copy-start | bytes 196612
  1.6 18.6 %collective-permute-start = (bf16[2,256,128]{2,1,0:T(8,128)(2,1)S(1)}, bf16[2,256,128]{2,1,0:T(8,128)(2,1)S(1)}, u32[]{:S(2)}, u32[]{:S(2)}) collective-permute-start(bf16[2,256,128]{2,1,0:T(8,128)(2,1)S(1)} %pad_maximum_fusion.own_ref), channel_id=1, source_target_pairs={{0,1},{1,0},{2,3},{3,2},{4,5},{5,4},{6,7},{7,6},{8,9},{9,8},{10,11... | collective-permute-start | bytes 393224 | tf_op jit(solution)/shard_map/ppermute | solution.py:217
  6.0 14.1 %copy-start.2 = (s32[64,32]{0,1:T(8,128)S(1)}, s32[64,32]{0,1:T(8,128)}, u32[]{:S(2)}) copy-start(s32[64,32]{0,1:T(8,128)} %param.10) | copy-start | bytes 24580
  6.0 23.4 %collective-permute-start.1 = (bf16[2,256,128]{2,1,0:T(8,128)(2,1)S(1)}, bf16[2,256,128]{2,1,0:T(8,128)(2,1)S(1)}, u32[]{:S(2)}, u32[]{:S(2)}) collective-permute-start(bf16[2,256,128]{2,1,0:T(8,128)(2,1)S(1)} %pad_maximum_fusion.1), channel_id=1, source_target_pairs={{0,65},{1,64},{64,1},{65,0},{2,67},{3,66},{66,3},{67,2},{4,69},{5,... | collective-permute-start | bytes 393224 | tf_op jit(solution)/shard_map/ppermute | solution.py:221
  21.3 17.6 %all-to-all-start = ((bf16[4,2,2,256,128]{4,3,2,1,0:T(8,128)(2,1)}), bf16[4,2,2,256,128]{4,3,2,1,0:T(8,128)(2,1)S(1)}, u32[]{:S(2)}, u32[]{:S(2)}) async-start(bf16[4,2,2,256,128]{4,3,2,1,0:T(8,128)(2,1)} %spread.1.after_ref), calls=%async_computation | async-start | bytes 2097152 | tf_op jit(solution)/shard_map/all_to_all | solution.py:341
  42.2 3.6 %copy-start.3 = (s32[16,32,2]{1,2,0:T(2,128)S(1)}, s32[16,32,2]{1,2,0:T(2,128)}, u32[]{:S(2)}) copy-start(s32[16,32,2]{1,2,0:T(2,128)} %param.11) | copy-start | bytes 12292
  42.2 9.1 %all-to-all-start.1 = ((f32[8,4,2,1,512]{4,3,2,1,0:T(1,128)}), f32[8,4,2,1,512]{4,3,2,1,0:T(1,128)S(1)}, u32[]{:S(2)}, u32[]{:S(2)}) async-start(f32[8,4,2,1,512]{4,3,2,1,0:T(1,128)} %stats.1.after_ref), calls=%async_computation.1 | async-start | bytes 262144 | tf_op jit(solution)/shard_map/all_to_all | solution.py:349
  62.5 21.3 %collective-permute-start.2 = (bf16[2,256,128]{2,1,0:T(8,128)(2,1)S(1)}, bf16[2,256,128]{2,1,0:T(8,128)(2,1)S(1)}, u32[]{:S(2)}, u32[]{:S(2)}) collective-permute-start(bf16[2,256,128]{2,1,0:T(8,128)(2,1)S(1)} %fusion), channel_id=1, source_target_pairs={{0,65},{1,64},{64,1},{65,0},{2,67},{3,66},{66,3},{67,2},{4,69},{5,... | collective-permute-start | bytes 393224 | tf_op jit(solution)/shard_map/ppermute | solution.py:221
  71.0 15.2 %all-to-all-start.2 = ((bf16[8,256,128]{2,1,0:T(8,128)(2,1)}), bf16[8,256,128]{2,1,0:T(8,128)(2,1)S(1)}, u32[]{:S(2)}, u32[]{:S(2)}) async-start(bf16[8,256,128]{2,1,0:T(8,128)(2,1)} %bitcast.9), calls=%async_computation.2 | async-start | bytes 1048576 | tf_op jit(solution)/shard_map/all_to_all | solution.py:357

commit v6 on v5

--- a/solution.py
+++ b/solution.py
@@ -120,18 +120,102 @@
         kt_ref[:, i * HALF : (i + 1) * HALF] = chunk[0].T
 
 
-def grads_kernel(
+def side_grads(side, n, qg_ref, keys_ref, far_ref, stats_ref, kt_ref, dk_acc, dv_acc, ds_ref):
+    q_all = qg_ref[n, :, 0].reshape(2 * HALF, HD)
+    g_all = qg_ref[n, :, 1].reshape(2 * HALF, HD)
+    rows_stats = []
+    for h in range(2):
+        lse_parts = [stats_ref[j, n, h, :, :HALF] for j in range(BLOCKS)]
+        top = functools.reduce(jnp.maximum, lse_parts)
+        total = jnp.zeros((1, HALF), jnp.float32)
+        weighted = jnp.zeros((1, HALF), jnp.float32)
+        for j in range(BLOCKS):
+            w = jnp.exp2(lse_parts[j] - top)
+            total = total + w
+            weighted = weighted + w * stats_ref[j, n, h, :, HALF:]
+        rows_stats.append((top + jnp.log2(total), weighted / total))
+    for i in range(2):
+        rows = slice(i * HALF, (i + 1) * HALF)
+        ps, ds = [], []
+        for h in range(2):
+            lse, delta = rows_stats[h]
+            s = dot_t(keys_ref[i, 0], qg_ref[n, h, 0])
+            gp = dot_t(keys_ref[i, 1], qg_ref[n, h, 1])
+            p_parts, d_parts = [], []
+            for t in range(2):
+                k = NCHUNK * side + 2 * i + t
+                part = slice(t * TILE, (t + 1) * TILE)
+                shift = lse + 4.0 * far_ref[n, h, k : k + 1, :]
+                p = jnp.exp2(s[part] * SCALE2 - shift)
+                p_parts.append(p.astype(jnp.bfloat16))
+                d_parts.append((p * (gp[part] - delta)).astype(jnp.bfloat16))
+            ps.append(jnp.concatenate(p_parts, axis=0))
+            d = jnp.concatenate(d_parts, axis=0)
+            ds.append(d)
+            ds_ref[h, rows] = d
+        dv_acc[rows] += dot_n(jnp.concatenate(ps, axis=1), g_all)
+        dk_acc[rows] += dot_n(jnp.concatenate(ds, axis=1), q_all)
+    used = slice(2 * side * HALF, 2 * (side + 1) * HALF)
+    return [dot_n(kt_ref[:, used], ds_ref[h]) for h in range(2)]
+
+
+def split_keys(core, dk_acc, dv_acc, keep_ref, send_ref):
+    rows = pl.ds(core * HALF, HALF)
+    keep_ref[0] = dk_acc[rows] * SCALE
+    keep_ref[1] = dv_acc[rows]
+    rows = pl.ds((1 - core) * HALF, HALF)
+    send_ref[0] = (dk_acc[rows] * SCALE).astype(jnp.bfloat16)
+    send_ref[1] = dv_acc[rows].astype(jnp.bfloat16)
+
+
+def there_kernel(
     live_ref,
-    work_ref,
     qg_ref,
-    here_ref,
     there_ref,
     far_ref,
     stats_ref,
     kt_ref,
     keep_ref,
-    send_here_ref,
-    send_there_ref,
+    send_ref,
+    dqt_ref,
+    dk_acc,
+    dv_acc,
+    ds_ref,
+):
+    dk_acc[...] = jnp.zeros_like(dk_acc)
+    dv_acc[...] = jnp.zeros_like(dv_acc)
+
+    def group(n, carry):
+        @pl.when(live_ref[2 * n + 1] > 0)
+        def _():
+            parts = side_grads(
+                1, n, qg_ref, there_ref, far_ref, stats_ref, kt_ref, dk_acc, dv_acc, ds_ref
+            )
+            for h in range(2):
+                dqt_ref[n, h] = parts[h]
+
+        @pl.when(live_ref[2 * n + 1] == 0)
+        def _():
+            dqt_ref[n] = jnp.zeros((2, HD, HALF), jnp.float32)
+
+        return carry
+
+    lax.fori_loop(0, NX, group, 0)
+    split_keys(lax.axis_index("c"), dk_acc, dv_acc, keep_ref, send_ref)
+
+
+def here_kernel(
+    live_ref,
+    work_ref,
+    qg_ref,
+    here_ref,
+    far_ref,
+    stats_ref,
+    kt_ref,
+    dqt_ref,
+    after_ref,
+    keep_ref,
+    send_ref,
     dq_ref,
     dk_acc,
     dv_acc,
@@ -140,49 +224,13 @@
     sems,
 ):
     zh, core, head = (lax.axis_index(name) for name in ("zh", "c", "n"))
-    chunks = (here_ref.at[0], here_ref.at[1], there_ref.at[0], there_ref.at[1])
     dk_acc[...] = jnp.zeros_like(dk_acc)
     dv_acc[...] = jnp.zeros_like(dv_acc)
 
     def group(n, carry):
-        def work(subset):
-            q_all = qg_ref[n, :, 0].reshape(2 * HALF, HD)
-            g_all = qg_ref[n, :, 1].reshape(2 * HALF, HD)
-            rows_stats = []
+        def deliver(parts):
             for h in range(2):
-                lse_parts = [stats_ref[j, n, h, :, :HALF] for j in range(BLOCKS)]
-                top = functools.reduce(jnp.maximum, lse_parts)
-                total = jnp.zeros((1, HALF), jnp.float32)
-                weighted = jnp.zeros((1, HALF), jnp.float32)
-                for j in range(BLOCKS):
-                    w = jnp.exp2(lse_parts[j] - top)
-                    total = total + w
-                    weighted = weighted + w * stats_ref[j, n, h, :, HALF:]
-                rows_stats.append((top + jnp.log2(total), weighted / total))
-            for i in subset:
-                rows = slice(i * HALF, (i + 1) * HALF)
-                ps, ds = [], []
-                for h in range(2):
-                    lse, delta = rows_stats[h]
-                    s = dot_t(chunks[i][0], qg_ref[n, h, 0])
-                    gp = dot_t(chunks[i][1], qg_ref[n, h, 1])
-                    p_parts, d_parts = [], []
-                    for t in range(2):
-                        k = 2 * i + t
-                        part = slice(t * TILE, (t + 1) * TILE)
-                        shift = lse + 4.0 * far_ref[n, h, k : k + 1, :]
-                        p = jnp.exp2(s[part] * SCALE2 - shift)
-                        p_parts.append(p.astype(jnp.bfloat16))
-                        d_parts.append((p * (gp[part] - delta)).astype(jnp.bfloat16))
-                    ps.append(jnp.concatenate(p_parts, axis=0))
-                    d = jnp.concatenate(d_parts, axis=0)
-                    ds.append(d)
-                    ds_ref[h, rows] = d
-                dv_acc[rows] += dot_n(jnp.concatenate(ps, axis=1), g_all)
-                dk_acc[rows] += dot_n(jnp.concatenate(ds, axis=1), q_all)
-            used = slice(subset[0] * HALF, (subset[-1] + 1) * HALF)
-            for h in range(2):
-                dq = (dot_n(kt_ref[:, used], ds_ref[h, used]) * SCALE).T.astype(jnp.bfloat16)
+                dq = (parts[h] * SCALE).T.astype(jnp.bfloat16)
                 for t in range(2):
                     slot = jnp.int32(3)
                     for w in range(3):
@@ -190,21 +238,22 @@
                         slot = jnp.where(listed == 2 * h + t, w, slot)
                     dq_buf[n, slot] = dq[t * TILE : (t + 1) * TILE]
 
-        def nothing():
-            dq_buf[n] = jnp.zeros((4, TILE, HD), jnp.bfloat16)
-
-        by_sides(live_ref, n, work, nothing)
+        @pl.when(live_ref[2 * n] > 0)
+        def _():
+            parts = side_grads(
+                0, n, qg_ref, here_ref, far_ref, stats_ref, kt_ref, dk_acc, dv_acc, ds_ref
+            )
+            deliver([parts[h] + dqt_ref[n, h] for h in range(2)])
+
+        @pl.when(live_ref[2 * n] == 0)
+        def _():
+            deliver([dqt_ref[n, h] for h in range(2)])
+
         pltpu.make_async_copy(dq_buf.at[n], dq_ref.at[n], sems.at[n]).start()
         return carry
 
     lax.fori_loop(0, NX, group, 0)
-    for i, send_ref in enumerate((send_here_ref, send_there_ref)):
-        rows = pl.ds((2 * i + core) * HALF, HALF)
-        keep_ref[i, 0] = dk_acc[rows] * SCALE
-        keep_ref[i, 1] = dv_acc[rows]
-        rows = pl.ds((2 * i + 1 - core) * HALF, HALF)
-        send_ref[0] = (dk_acc[rows] * SCALE).astype(jnp.bfloat16)
-        send_ref[1] = dv_acc[rows].astype(jnp.bfloat16)
+    split_keys(core, dk_acc, dv_acc, keep_ref, send_ref)
     for n in range(NX):
         pltpu.make_async_copy(dq_buf.at[n], dq_ref.at[n], sems.at[n]).wait()
 
@@ -272,33 +321,52 @@
     )(*kv, after)
 
 
-def run_grads(live, work, qg, kv, far, stats, kt):
-    return pl.pallas_call(
-        grads_kernel,
+ACCUMULATORS = [
+    pltpu.VMEM((2 * HALF, HD), jnp.float32),
+    pltpu.VMEM((2 * HALF, HD), jnp.float32),
+    pltpu.VMEM((2, 2 * HALF, HALF), jnp.bfloat16),
+]
+
+
+def run_there(live, qg, there, far, stats, kt):
+    return pl.pallas_call(
+        there_kernel,
         out_shape=[
-            jax.ShapeDtypeStruct((2, 2, HALF, HD), jnp.float32),
+            jax.ShapeDtypeStruct((2, HALF, HD), jnp.float32),
             jax.ShapeDtypeStruct((2, HALF, HD), jnp.bfloat16),
+            jax.ShapeDtypeStruct((NX, 2, HD, HALF), jnp.float32),
+        ],
+        in_specs=[SMEM] + [VMEM] * 5,
+        out_specs=[VMEM] * 3,
+        scratch_shapes=ACCUMULATORS,
+        compiler_params=pltpu.CompilerParams(vmem_limit_bytes=24 * 1024 * 1024),
+        cost_estimate=pl.CostEstimate(flops=10**9, bytes_accessed=2**21, transcendentals=2**20),
+        name="there",
+    )(live, qg, there, far, stats, kt)
+
+
+def run_here(live, work, qg, here, far, stats, kt, dqt, after):
+    anywhere = pl.BlockSpec(memory_space=pl.ANY)
+    return pl.pallas_call(
+        here_kernel,
+        out_shape=[
+            jax.ShapeDtypeStruct((2, HALF, HD), jnp.float32),
             jax.ShapeDtypeStruct((2, HALF, HD), jnp.bfloat16),
             jax.ShapeDtypeStruct((NX, 4, TILE, HD), jnp.bfloat16),
         ],
-        in_specs=[SMEM, SMEM] + [VMEM] * 6,
-        out_specs=[VMEM, VMEM, VMEM, pl.BlockSpec(memory_space=pl.ANY)],
-        scratch_shapes=[
-            pltpu.VMEM((NCHUNK * HALF, HD), jnp.float32),
-            pltpu.VMEM((NCHUNK * HALF, HD), jnp.float32),
-            pltpu.VMEM((2, NCHUNK * HALF, HALF), jnp.bfloat16),
-            pltpu.VMEM((NX, 4, TILE, HD), jnp.bfloat16),
-            pltpu.SemaphoreType.DMA((NX,)),
-        ],
+        in_specs=[SMEM, SMEM] + [VMEM] * 6 + [anywhere],
+        out_specs=[VMEM, VMEM, anywhere],
+        scratch_shapes=ACCUMULATORS
+        + [pltpu.VMEM((NX, 4, TILE, HD), jnp.bfloat16), pltpu.SemaphoreType.DMA((NX,))],
         compiler_params=pltpu.CompilerParams(vmem_limit_bytes=24 * 1024 * 1024),
-        cost_estimate=pl.CostEstimate(flops=2 * 10**9, bytes_accessed=2**21, transcendentals=2**21),
-        name="grads",
-    )(live, work, qg, *kv, far, stats, kt)
+        cost_estimate=pl.CostEstimate(flops=10**11, bytes_accessed=2**21, transcendentals=2**20),
+        name="here",
+    )(live, work, qg, here, far, stats, kt, dqt, after)
 
 
 def finish_kernel(keep_ref, sibling_ref, arrived_ref, dk_ref, dv_ref):
     for i, out_ref in enumerate((dk_ref, dv_ref)):
-        total = keep_ref[0, i] + sibling_ref[i].astype(jnp.float32)
+        total = keep_ref[i] + sibling_ref[i].astype(jnp.float32)
         out_ref[...] = (total + arrived_ref[i].astype(jnp.float32)).astype(jnp.bfloat16)
 
 
@@ -347,15 +415,14 @@
     own_stats = run_stats(live, all_qg, kv, far)
     kt = run_turn(kv, own_stats)
     stats = lax.all_to_all(own_stats, ("x", "p"), 0, 0)
-    keep, send_here, send_there, dq = run_grads(live, work, all_qg, kv, far, stats, kt)
-
     sibling = 1 - lax.axis_index("c")
+    keep_there, send_there, dqt = run_there(live, all_qg, kv[1], far, stats, kt)
     there = lax.dynamic_index_in_dim(lax.all_gather(send_there, "c"), sibling, 0, False)
-    dkv_out = (keep[1] + there.astype(jnp.float32)).astype(jnp.bfloat16)
-    dkv_out, dq, send_here = lax.optimization_barrier((dkv_out, dq, send_here))
+    dkv_out = (keep_there + there.astype(jnp.float32)).astype(jnp.bfloat16)
     from_across = across(dkv_out)
+    keep, send, dq = run_here(live, work, all_qg, kv[0], far, stats, kt, dqt, dkv_out)
     dq_parts = lax.all_to_all(dq.reshape(BLOCKS, HALF, HD), ("x", "p"), 0, 0)
-    here = lax.dynamic_index_in_dim(lax.all_gather(send_here, "c"), sibling, 0, False)
+    here = lax.dynamic_index_in_dim(lax.all_gather(send, "c"), sibling, 0, False)
     grad_keys, grad_values = run_finish(keep, here, from_across)
     outs = (run_sum(dq_parts), grad_keys, grad_values)
     return tuple(out[None, None] for out in outs)

time: 87.8 us -> 86.8 us (0.989)
  waiting for transfers between devices: 18.9 us -> 16.4 us
  Pallas kernels: 11.4 us -> 12.7 us
    ppermute x2, waiting for transfers between devices: 6.87 us -> 3.4 us  [across(): return lax.ppermute(value, ('zh', 'p'), [(0, 3), (1, 2), (2, 1), (3, 0)])]
    pallas_call x1 -> x2, Pallas kernels: 4.67 us -> 5.94 us  [the longest x1 3.53 us: run_here(): pl.pallas_call(here_kernel, out_shape=[jax.ShapeDtypeStruct((2, HALF, HD)...]
    all_to_all x1, waiting for transfers between devices: 1.67 us -> 2.57 us  [on_device(): dq_parts = lax.all_to_all(dq.reshape(BLOCKS, HALF, HD), ('x', 'p'), 0, 0)]
  transfers between devices with their start and end apart: 6 -> 6, of which waited for: 4 -> 4; matrix products, arithmetic and copies ran while one was open for 0% -> 0% of each run, Pallas kernels for 3% -> 7%
where the time goes in v6:
time: 86.8 us; the launch traced here: 85.9 us
  starting transfers between devices  38.4 us (44%)
  blocking collectives  16.5 us (19%)
  waiting for transfers between devices  16.4 us (19%)
  Pallas kernels  12.7 us (15%)
  other arithmetic  0.97 us (1%)
    ppermute x2, starting transfers between devices, across(): return lax.ppermute(value, ('zh', 'p'), [(0, 3), (1, 2), (2, 1), (3, 0)])  20.2 us
    all_gather x2, blocking collectives, on_device(): kv = (lax.all_gather(own_kv, 'c'), lax.all_gather(across_kv, 'c'))  7.57 us
    all_gather x1, blocking collectives, on_device(): lax.all_gather(send_there, 'c')  6.36 us
    all_to_all x1, starting transfers between devices, on_device(): dq_parts = lax.all_to_all(dq.reshape(BLOCKS, HALF, HD), ('x', 'p'), 0, 0)  6.19 us
    all_to_all x1, waiting for transfers between devices, on_device(): stats = lax.all_to_all(own_stats, ('x', 'p'), 0, 0)  5.26 us
    all_to_all x1, waiting for transfers between devices, on_device(): all_qg = lax.all_to_all(spread, 'x', 0, 0)  5.12 us
    ppermute x1, starting transfers between devices, flipped(): return lax.ppermute(value, axis, [(0, 1), (1, 0)])  4.38 us
    all_to_all x1, starting transfers between devices, on_device(): all_qg = lax.all_to_all(spread, 'x', 0, 0)  4.01 us
  transfers between devices with their start and end apart: 6, of which 4 were waited for; matrix products, arithmetic and copies ran while one was open for 0% of the time, Pallas kernels for 7%

profile of v6, /device:TPU:1, one launch (start us, length us, event | category | flops | bytes accessed | tf_op | source)
XLA Modules:
  0.0 85.9 jit_solution(12716021689502844851)
XLA Ops:
  0.7 0.9 %pad_maximum_fusion.own_ref = bf16[2,256,128]{2,1,0:T(8,128)(2,1)S(1)} fusion(bf16[1,256,128]{2,1,0:T(8,128)(2,1)} %bitcast.28, bf16[1,256,128]{2,1,0:T(8,128)(2,1)} %bitcast.29), kind=kLoop, calls=%fused_computation.2 | loop fusion | flops 65536 | bytes 262144 | tf_op jit(solution)/shard_map/stack | solution.py:404
  1.6 4.4 %collective-permute-start = (bf16[2,256,128]{2,1,0:T(8,128)(2,1)S(1)}, bf16[2,256,128]{2,1,0:T(8,128)(2,1)S(1)}, u32[]{:S(2)}, u32[]{:S(2)}) collective-permute-start(bf16[2,256,128]{2,1,0:T(8,128)(2,1)S(1)} %pad_maximum_fusion.own_ref), channel_id=1, source_target_pairs={{0,1},{1,0},{2,3},{3,2},{4,5},{5,4},{6,7},{7,6},{8,9},{9,8},{10,11... | collective-permute-start | bytes 393224 | tf_op jit(solution)/shard_map/ppermute | solution.py:266
  6.0 14.1 %collective-permute-start.1 = (bf16[2,256,128]{2,1,0:T(8,128)(2,1)S(1)}, bf16[2,256,128]{2,1,0:T(8,128)(2,1)S(1)}, u32[]{:S(2)}, u32[]{:S(2)}) collective-permute-start(bf16[2,256,128]{2,1,0:T(8,128)(2,1)S(1)} %pad_maximum_fusion.1), channel_id=1, source_target_pairs={{0,65},{1,64},{64,1},{65,0},{2,67},{3,66},{66,3},{67,2},{4,69},{5,... | collective-permute-start | bytes 393224 | tf_op jit(solution)/shard_map/ppermute | solution.py:270
  20.2 1.1 %spread.1.after_ref = bf16[4,2,2,256,128]{4,3,2,1,0:T(8,128)(2,1)} custom-call(bf16[2,256,128]{2,1,0:T(8,128)(2,1)S(1)} %pad_maximum_fusion.own_ref, bf16[2,256,128]{2,1,0:T(8,128)(2,1)S(1)} %collective-permute-done.mate_ref), custom_call_target="tpu_custom_call" | custom-call | tf_op jit(solution)/shard_map/spread/pallas_call | solution.py:274
  21.3 4.0 %all-to-all-start = ((bf16[4,2,2,256,128]{4,3,2,1,0:T(8,128)(2,1)}), bf16[4,2,2,256,128]{4,3,2,1,0:T(8,128)(2,1)S(1)}, u32[]{:S(2)}, u32[]{:S(2)}) async-start(bf16[4,2,2,256,128]{4,3,2,1,0:T(8,128)(2,1)} %spread.1.after_ref), calls=%async_computation | async-start | bytes 2097152 | tf_op jit(solution)/shard_map/all_to_all | solution.py:409
  25.4 0.9 %masks.1 = (f32[4,2,8,256]{3,2,1,0:T(8,128)S(1)}, s32[8]{0:T(128)S(1)}) custom-call(s32[64,32]{1,0:T(8,128)S(1)} %copy.14.tiles_ref, bf16[4,2,2,256,128]{4,3,2,1,0:T(8,128)(2,1)} %spread.1.after_ref), custom_call_target="tpu_custom_call" | custom-call | flops 10000000000 | bytes 1048576 | tf_op jit(solution)/shard_map/masks/pallas_call | solution.py:285
  26.3 3.1 %all-gather = bf16[4,256,128]{2,1,0:T(8,128)(2,1)S(1)} all-gather(bf16[2,256,128]{2,1,0:T(8,128)(2,1)S(1)} %pad_maximum_fusion.1), channel_id=2, replica_groups=mesh['x'=4,'zh'=2,'c'=2,'n'=16,'p'=2] {'c'}, dimensions={0}, use_global_device_ids=true | all-gather | bytes 393216 | tf_op jit(solution)/shard_map/all_gather | solution.py:412
  29.4 4.4 %all-gather.1 = bf16[4,256,128]{2,1,0:T(8,128)(2,1)S(1)} all-gather(bf16[2,256,128]{2,1,0:T(8,128)(2,1)S(1)} %collective-permute-done.1), channel_id=3, replica_groups=mesh['x'=4,'zh'=2,'c'=2,'n'=16,'p'=2] {'c'}, dimensions={0}, use_global_device_ids=true | all-gather | bytes 393216 | tf_op jit(solution)/shard_map/all_gather | solution.py:412
  33.8 5.1 %all-to-all-done.qg_ref = bf16[4,2,2,256,128]{4,3,2,1,0:T(8,128)(2,1)S(1)} async-done(((bf16[4,2,2,256,128]{4,3,2,1,0:T(8,128)(2,1)}), bf16[4,2,2,256,128]{4,3,2,1,0:T(8,128)(2,1)S(1)}, u32[]{:S(2)}, u32[]{:S(2)}) %all-to-all-start) | async-done | bytes 1048608 | tf_op jit(solution)/shard_map/all_to_all | solution.py:409
  39.0 3.2 %stats.1.after_ref = f32[8,4,2,1,512]{4,3,2,1,0:T(1,128)} custom-call(s32[8]{0:T(128)S(1)} %get-tuple-element.14.live_ref, bf16[4,2,2,256,128]{4,3,2,1,0:T(8,128)(2,1)S(1)} %all-to-all-done.qg_ref, bf16[2,2,256,128]{3,2,1,0:T(8,128)(2,1)S(1)} %bitcast.18, bf16[2,2,256,128]{3,2,1,0:T(8,128)(2,1)S(1)} %bitcast.21, f32[4,2,8,256]{3,2,1,0:T(8,128)S(1)} %get-tuple-element.15.far_ref), custom_call_target="tpu_custom_call" | custom-call | flops 1000000000 | bytes 2097152 | tf_op jit(solution)/shard_map/stats/pallas_call | solution.py:301
  42.1 3.6 %all-to-all-start.1 = ((f32[8,4,2,1,512]{4,3,2,1,0:T(1,128)}), f32[8,4,2,1,512]{4,3,2,1,0:T(1,128)S(1)}, u32[]{:S(2)}, u32[]{:S(2)}) async-start(f32[8,4,2,1,512]{4,3,2,1,0:T(1,128)} %stats.1.after_ref), calls=%async_computation.1 | async-start | bytes 262144 | tf_op jit(solution)/shard_map/all_to_all | solution.py:417
  45.8 0.1 copy.15
  46.0 0.1 turn.1.kt_ref
  46.1 5.3 %all-to-all-done.1.stats_ref = f32[8,4,2,1,512]{4,3,2,1,0:T(1,128)S(1)} async-done(((f32[8,4,2,1,512]{4,3,2,1,0:T(1,128)}), f32[8,4,2,1,512]{4,3,2,1,0:T(1,128)S(1)}, u32[]{:S(2)}, u32[]{:S(2)}) %all-to-all-start.1) | async-done | bytes 131104 | tf_op jit(solution)/shard_map/all_to_all | solution.py:417
  51.3 2.4 %there.1 = (f32[2,256,128]{2,1,0:T(8,128)S(1)}, bf16[2,256,128]{2,1,0:T(8,128)(2,1)S(1)}, f32[4,2,128,256]{3,2,1,0:T(8,128)S(1)}) custom-call(s32[8]{0:T(128)S(1)} %get-tuple-element.14.live_ref, bf16[4,2,2,256,128]{4,3,2,1,0:T(8,128)(2,1)S(1)} %all-to-all-done.qg_ref, bf16[2,2,256,128]{3,2,1,0:T(8,128)(2,1)S(1)} %bitcast.23, ...), custom_call_target="tpu_custom_call" | custom-call | flops 1000000000 | bytes 2097152 | tf_op jit(solution)/shard_map/there/pallas_call | solution.py:332
  53.8 6.4 %all-gather.2 = bf16[4,256,128]{2,1,0:T(8,128)(2,1)S(1)} all-gather(bf16[2,256,128]{2,1,0:T(8,128)(2,1)S(1)} %get-tuple-element.19), channel_id=4, replica_groups=mesh['x'=4,'zh'=2,'c'=2,'n'=16,'p'=2] {'c'}, dimensions={0}, use_global_device_ids=true | all-gather | bytes 393216 | tf_op jit(solution)/shard_map/all_gather | solution.py:420
  60.2 6.1 %collective-permute-start.2 = (bf16[2,256,128]{2,1,0:T(8,128)(2,1)S(1)}, bf16[2,256,128]{2,1,0:T(8,128)(2,1)S(1)}, u32[]{:S(2)}, u32[]{:S(2)}) collective-permute-start(bf16[2,256,128]{2,1,0:T(8,128)(2,1)S(1)} %fusion.after_ref), channel_id=1, source_target_pairs={{0,65},{1,64},{64,1},{65,0},{2,67},{3,66},{66,3},{67,2},{4,69},{5,... | collective-permute-start | bytes 393224 | tf_op jit(solution)/shard_map/ppermute | solution.py:270
  66.3 3.5 %here.1 = (f32[2,256,128]{2,1,0:T(8,128)S(1)}, bf16[2,256,128]{2,1,0:T(8,128)(2,1)S(1)}, bf16[4,4,128,128]{3,2,1,0:T(8,128)(2,1)}) custom-call(s32[8]{0:T(128)S(1)} %get-tuple-element.14.live_ref, s32[16,64]{1,0:T(8,128)S(1)} %copy.16.work_ref, bf16[4,2,2,256,128]{4,3,2,1,0:T(8,128)(2,1)S(1)} %all-to-all-done.qg_ref, bf16[2,2,256,128]{3,2,1,0:T(8,128)(2,1)S(1)} %bitcast.20, ...), custom_call_target="tpu_custom_call" | custom-call | flops 99999997952 | bytes 2097152 | tf_op jit(solution)/shard_map/here/pallas_call | solution.py:350
  69.8 6.2 %all-to-all-start.2 = ((bf16[8,256,128]{2,1,0:T(8,128)(2,1)}), bf16[8,256,128]{2,1,0:T(8,128)(2,1)S(1)}, u32[]{:S(2)}, u32[]{:S(2)}) async-start(bf16[8,256,128]{2,1,0:T(8,128)(2,1)} %bitcast.9), calls=%async_computation.2 | async-start | bytes 1048576 | tf_op jit(solution)/shard_map/all_to_all | solution.py:424
  76.0 2.5 %all-gather.3 = bf16[4,256,128]{2,1,0:T(8,128)(2,1)S(1)} all-gather(bf16[2,256,128]{2,1,0:T(8,128)(2,1)S(1)} %get-tuple-element.22), channel_id=5, replica_groups=mesh['x'=4,'zh'=2,'c'=2,'n'=16,'p'=2] {'c'}, dimensions={0}, use_global_device_ids=true | all-gather | bytes 393216 | tf_op jit(solution)/shard_map/all_gather | solution.py:425
  78.6 3.4 %collective-permute-done.2.arrived_ref = bf16[2,256,128]{2,1,0:T(8,128)(2,1)S(1)} collective-permute-done((bf16[2,256,128]{2,1,0:T(8,128)(2,1)S(1)}, bf16[2,256,128]{2,1,0:T(8,128)(2,1)S(1)}, u32[]{:S(2)}, u32[]{:S(2)}) %collective-permute-start.2) | collective-permute-done | bytes 131104 | tf_op jit(solution)/shard_map/ppermute | solution.py:270
  82.0 0.7 finish.1
  82.6 2.6 %all-to-all-done.2.parts_ref = bf16[8,256,128]{2,1,0:T(8,128)(2,1)S(1)} async-done(((bf16[8,256,128]{2,1,0:T(8,128)(2,1)}), bf16[8,256,128]{2,1,0:T(8,128)(2,1)S(1)}, u32[]{:S(2)}, u32[]{:S(2)}) %all-to-all-start.2) | async-done | bytes 524320 | tf_op jit(solution)/shard_map/all_to_all | solution.py:424
  85.2 0.7 sum.1
  (15 shorter events, 0.2 us)
Async XLA Ops:
  0.6 5.3 %copy-start = (bf16[1,1,256,128]{3,2,1,0:T(8,128)(2,1)S(1)}, bf16[1,1,256,128]{3,2,1,0:T(8,128)(2,1)}, u32[]{:S(2)}) copy-start(bf16[1,1,256,128]{3,2,1,0:T(8,128)(2,1)} %param.8) | copy-start | bytes 196612
  0.6 5.3 %copy-start.1 = (bf16[1,1,256,128]{3,2,1,0:T(8,128)(2,1)S(1)}, bf16[1,1,256,128]{3,2,1,0:T(8,128)(2,1)}, u32[]{:S(2)}) copy-start(bf16[1,1,256,128]{3,2,1,0:T(8,128)(2,1)} %param.7) | copy-start | bytes 196612
  1.6 18.6 %collective-permute-start = (bf16[2,256,128]{2,1,0:T(8,128)(2,1)S(1)}, bf16[2,256,128]{2,1,0:T(8,128)(2,1)S(1)}, u32[]{:S(2)}, u32[]{:S(2)}) collective-permute-start(bf16[2,256,128]{2,1,0:T(8,128)(2,1)S(1)} %pad_maximum_fusion.own_ref), channel_id=1, source_target_pairs={{0,1},{1,0},{2,3},{3,2},{4,5},{5,4},{6,7},{7,6},{8,9},{9,8},{10,11... | collective-permute-start | bytes 393224 | tf_op jit(solution)/shard_map/ppermute | solution.py:266
  6.0 14.1 %copy-start.2 = (s32[64,32]{0,1:T(8,128)S(1)}, s32[64,32]{0,1:T(8,128)}, u32[]{:S(2)}) copy-start(s32[64,32]{0,1:T(8,128)} %param.10) | copy-start | bytes 24580
  6.0 23.4 %collective-permute-start.1 = (bf16[2,256,128]{2,1,0:T(8,128)(2,1)S(1)}, bf16[2,256,128]{2,1,0:T(8,128)(2,1)S(1)}, u32[]{:S(2)}, u32[]{:S(2)}) collective-permute-start(bf16[2,256,128]{2,1,0:T(8,128)(2,1)S(1)} %pad_maximum_fusion.1), channel_id=1, source_target_pairs={{0,65},{1,64},{64,1},{65,0},{2,67},{3,66},{66,3},{67,2},{4,69},{5,... | collective-permute-start | bytes 393224 | tf_op jit(solution)/shard_map/ppermute | solution.py:270
  21.3 17.6 %all-to-all-start = ((bf16[4,2,2,256,128]{4,3,2,1,0:T(8,128)(2,1)}), bf16[4,2,2,256,128]{4,3,2,1,0:T(8,128)(2,1)S(1)}, u32[]{:S(2)}, u32[]{:S(2)}) async-start(bf16[4,2,2,256,128]{4,3,2,1,0:T(8,128)(2,1)} %spread.1.after_ref), calls=%async_computation | async-start | bytes 2097152 | tf_op jit(solution)/shard_map/all_to_all | solution.py:409
  42.1 3.7 %copy-start.3 = (s32[16,32,2]{1,2,0:T(2,128)S(1)}, s32[16,32,2]{1,2,0:T(2,128)}, u32[]{:S(2)}) copy-start(s32[16,32,2]{1,2,0:T(2,128)} %param.11) | copy-start | bytes 12292
  42.1 9.2 %all-to-all-start.1 = ((f32[8,4,2,1,512]{4,3,2,1,0:T(1,128)}), f32[8,4,2,1,512]{4,3,2,1,0:T(1,128)S(1)}, u32[]{:S(2)}, u32[]{:S(2)}) async-start(f32[8,4,2,1,512]{4,3,2,1,0:T(1,128)} %stats.1.after_ref), calls=%async_computation.1 | async-start | bytes 262144 | tf_op jit(solution)/shard_map/all_to_all | solution.py:417
  60.2 21.8 %collective-permute-start.2 = (bf16[2,256,128]{2,1,0:T(8,128)(2,1)S(1)}, bf16[2,256,128]{2,1,0:T(8,128)(2,1)S(1)}, u32[]{:S(2)}, u32[]{:S(2)}) collective-permute-start(bf16[2,256,128]{2,1,0:T(8,128)(2,1)S(1)} %fusion.after_ref), channel_id=1, source_target_pairs={{0,65},{1,64},{64,1},{65,0},{2,67},{3,66},{66,3},{67,2},{4,69},{5,... | collective-permute-start | bytes 393224 | tf_op jit(solution)/shard_map/ppermute | solution.py:270
  69.8 15.4 %all-to-all-start.2 = ((bf16[8,256,128]{2,1,0:T(8,128)(2,1)}), bf16[8,256,128]{2,1,0:T(8,128)(2,1)S(1)}, u32[]{:S(2)}, u32[]{:S(2)}) async-start(bf16[8,256,128]{2,1,0:T(8,128)(2,1)} %bitcast.9), calls=%async_computation.2 | async-start | bytes 1048576 | tf_op jit(solution)/shard_map/all_to_all | solution.py:424

commit v7 on v6

--- a/solution.py
+++ b/solution.py
@@ -27,11 +27,17 @@
     return jnp.dot(a, b, preferred_element_type=jnp.float32)
 
 
-def spread_kernel(own_ref, mate_ref, out_ref):
+def spread_kernel(own_ref, mate_ref, out_ref, sems):
     half = lax.axis_index("p")
+    copies = []
     for j in range(NX):
-        out_ref[j, half] = own_ref[...]
-        out_ref[j, 1 - half] = mate_ref[...]
+        for i, (source, index) in enumerate(((own_ref, half), (mate_ref, 1 - half))):
+            target = out_ref.at[j, index]
+            copies.append(pltpu.make_async_copy(source, target, sems.at[2 * j + i]))
+    for copy in copies:
+        copy.start()
+    for copy in copies:
+        copy.wait()
 
 
 def mask_kernel(tiles_ref, after_ref, far_ref, live_ref, table_ref):
@@ -275,7 +281,8 @@
         spread_kernel,
         out_shape=jax.ShapeDtypeStruct((NX, 2) + own.shape, own.dtype),
         in_specs=[VMEM] * 2,
-        out_specs=VMEM,
+        out_specs=pl.BlockSpec(memory_space=pl.ANY),
+        scratch_shapes=[pltpu.SemaphoreType.DMA((2 * NX,))],
         compiler_params=pltpu.CompilerParams(vmem_limit_bytes=8 * 1024 * 1024),
         name="spread",
     )(own, mate)

time: 86.8 us -> 87.2 us (level)
  the two profiles are of different devices: /device:TPU:1 before, /device:TPU:8 now
where the time goes in v7:
time: 87.2 us; the launch traced here: 86.2 us
  starting transfers between devices  40.9 us (47%)
  waiting for transfers between devices  22.7 us (26%)
  Pallas kernels  12.6 us (14%)
  blocking collectives  7.95 us (9%)
  other arithmetic  0.97 us (1%)
    ppermute x2, starting transfers between devices, across(): return lax.ppermute(value, ('zh', 'p'), [(0, 3), (1, 2), (2, 1), (3, 0)])  22.5 us
    all_to_all x1, waiting for transfers between devices, on_device(): all_qg = lax.all_to_all(spread, 'x', 0, 0)  7.14 us
    all_to_all x1, starting transfers between devices, on_device(): dq_parts = lax.all_to_all(dq.reshape(BLOCKS, HALF, HD), ('x', 'p'), 0, 0)  6.47 us
    all_to_all x1, waiting for transfers between devices, on_device(): stats = lax.all_to_all(own_stats, ('x', 'p'), 0, 0)  6.41 us
    ppermute x2, waiting for transfers between devices, across(): return lax.ppermute(value, ('zh', 'p'), [(0, 3), (1, 2), (2, 1), (3, 0)])  5.66 us
    all_to_all x1, starting transfers between devices, on_device(): all_qg = lax.all_to_all(spread, 'x', 0, 0)  4.3 us
    all_gather x2, blocking collectives, on_device(): kv = (lax.all_gather(own_kv, 'c'), lax.all_gather(across_kv, 'c'))  3.98 us
    all_to_all x1, starting transfers between devices, on_device(): stats = lax.all_to_all(own_stats, ('x', 'p'), 0, 0)  3.89 us
  transfers between devices with their start and end apart: 6, of which 5 were waited for; matrix products, arithmetic and copies ran while one was open for 0% of the time, Pallas kernels for 7%

profile of v7, /device:TPU:8, one launch (start us, length us, event | category | flops | bytes accessed | tf_op | source)
XLA Modules:
  0.0 86.2 jit_solution(5410008405397957673)
XLA Ops:
  0.7 0.9 %pad_maximum_fusion.own_ref = bf16[2,256,128]{2,1,0:T(8,128)(2,1)S(1)} fusion(bf16[1,256,128]{2,1,0:T(8,128)(2,1)} %bitcast.28, bf16[1,256,128]{2,1,0:T(8,128)(2,1)} %bitcast.29), kind=kLoop, calls=%fused_computation.2 | loop fusion | flops 65536 | bytes 262144 | tf_op jit(solution)/shard_map/stack | solution.py:411
  1.6 3.8 %collective-permute-start = (bf16[2,256,128]{2,1,0:T(8,128)(2,1)S(1)}, bf16[2,256,128]{2,1,0:T(8,128)(2,1)S(1)}, u32[]{:S(2)}, u32[]{:S(2)}) collective-permute-start(bf16[2,256,128]{2,1,0:T(8,128)(2,1)S(1)} %pad_maximum_fusion.own_ref), channel_id=1, source_target_pairs={{0,1},{1,0},{2,3},{3,2},{4,5},{5,4},{6,7},{7,6},{8,9},{9,8},{10,11... | collective-permute-start | bytes 393224 | tf_op jit(solution)/shard_map/ppermute | solution.py:272
  5.5 14.4 %collective-permute-start.1 = (bf16[2,256,128]{2,1,0:T(8,128)(2,1)S(1)}, bf16[2,256,128]{2,1,0:T(8,128)(2,1)S(1)}, u32[]{:S(2)}, u32[]{:S(2)}) collective-permute-start(bf16[2,256,128]{2,1,0:T(8,128)(2,1)S(1)} %pad_maximum_fusion.1), channel_id=1, source_target_pairs={{0,65},{1,64},{64,1},{65,0},{2,67},{3,66},{66,3},{67,2},{4,69},{5,... | collective-permute-start | bytes 393224 | tf_op jit(solution)/shard_map/ppermute | solution.py:276
  19.9 1.1 %spread.1.after_ref = bf16[4,2,2,256,128]{4,3,2,1,0:T(8,128)(2,1)} custom-call(bf16[2,256,128]{2,1,0:T(8,128)(2,1)S(1)} %pad_maximum_fusion.own_ref, bf16[2,256,128]{2,1,0:T(8,128)(2,1)S(1)} %collective-permute-done.mate_ref), custom_call_target="tpu_custom_call" | custom-call | tf_op jit(solution)/shard_map/spread/pallas_call | solution.py:280
  21.0 4.3 %all-to-all-start = ((bf16[4,2,2,256,128]{4,3,2,1,0:T(8,128)(2,1)}), bf16[4,2,2,256,128]{4,3,2,1,0:T(8,128)(2,1)S(1)}, u32[]{:S(2)}, u32[]{:S(2)}) async-start(bf16[4,2,2,256,128]{4,3,2,1,0:T(8,128)(2,1)} %spread.1.after_ref), calls=%async_computation | async-start | bytes 2097152 | tf_op jit(solution)/shard_map/all_to_all | solution.py:416
  25.3 0.9 %masks.1 = (f32[4,2,8,256]{3,2,1,0:T(8,128)S(1)}, s32[8]{0:T(128)S(1)}) custom-call(s32[64,32]{1,0:T(8,128)S(1)} %copy.14.tiles_ref, bf16[4,2,2,256,128]{4,3,2,1,0:T(8,128)(2,1)} %spread.1.after_ref), custom_call_target="tpu_custom_call" | custom-call | flops 10000000000 | bytes 1048576 | tf_op jit(solution)/shard_map/masks/pallas_call | solution.py:292
  26.2 2.0 %all-gather = bf16[4,256,128]{2,1,0:T(8,128)(2,1)S(1)} all-gather(bf16[2,256,128]{2,1,0:T(8,128)(2,1)S(1)} %pad_maximum_fusion.1), channel_id=2, replica_groups=mesh['x'=4,'zh'=2,'c'=2,'n'=16,'p'=2] {'c'}, dimensions={0}, use_global_device_ids=true | all-gather | bytes 393216 | tf_op jit(solution)/shard_map/all_gather | solution.py:419
  28.2 2.5 %collective-permute-done.1 = bf16[2,256,128]{2,1,0:T(8,128)(2,1)S(1)} collective-permute-done((bf16[2,256,128]{2,1,0:T(8,128)(2,1)S(1)}, bf16[2,256,128]{2,1,0:T(8,128)(2,1)S(1)}, u32[]{:S(2)}, u32[]{:S(2)}) %collective-permute-start.1) | collective-permute-done | bytes 131104 | tf_op jit(solution)/shard_map/ppermute | solution.py:276
  30.7 2.0 %all-gather.1 = bf16[4,256,128]{2,1,0:T(8,128)(2,1)S(1)} all-gather(bf16[2,256,128]{2,1,0:T(8,128)(2,1)S(1)} %collective-permute-done.1), channel_id=3, replica_groups=mesh['x'=4,'zh'=2,'c'=2,'n'=16,'p'=2] {'c'}, dimensions={0}, use_global_device_ids=true | all-gather | bytes 393216 | tf_op jit(solution)/shard_map/all_gather | solution.py:419
  32.7 7.1 %all-to-all-done.qg_ref = bf16[4,2,2,256,128]{4,3,2,1,0:T(8,128)(2,1)S(1)} async-done(((bf16[4,2,2,256,128]{4,3,2,1,0:T(8,128)(2,1)}), bf16[4,2,2,256,128]{4,3,2,1,0:T(8,128)(2,1)S(1)}, u32[]{:S(2)}, u32[]{:S(2)}) %all-to-all-start) | async-done | bytes 1048608 | tf_op jit(solution)/shard_map/all_to_all | solution.py:416
  39.8 3.2 %stats.1.after_ref = f32[8,4,2,1,512]{4,3,2,1,0:T(1,128)} custom-call(s32[8]{0:T(128)S(1)} %get-tuple-element.14.live_ref, bf16[4,2,2,256,128]{4,3,2,1,0:T(8,128)(2,1)S(1)} %all-to-all-done.qg_ref, bf16[2,2,256,128]{3,2,1,0:T(8,128)(2,1)S(1)} %bitcast.18, bf16[2,2,256,128]{3,2,1,0:T(8,128)(2,1)S(1)} %bitcast.21, f32[4,2,8,256]{3,2,1,0:T(8,128)S(1)} %get-tuple-element.15.far_ref), custom_call_target="tpu_custom_call" | custom-call | flops 1000000000 | bytes 2097152 | tf_op jit(solution)/shard_map/stats/pallas_call | solution.py:308
  43.0 3.9 %all-to-all-start.1 = ((f32[8,4,2,1,512]{4,3,2,1,0:T(1,128)}), f32[8,4,2,1,512]{4,3,2,1,0:T(1,128)S(1)}, u32[]{:S(2)}, u32[]{:S(2)}) async-start(f32[8,4,2,1,512]{4,3,2,1,0:T(1,128)} %stats.1.after_ref), calls=%async_computation.1 | async-start | bytes 262144 | tf_op jit(solution)/shard_map/all_to_all | solution.py:424
  47.1 0.1 turn.1.kt_ref
  47.2 6.4 %all-to-all-done.1.stats_ref = f32[8,4,2,1,512]{4,3,2,1,0:T(1,128)S(1)} async-done(((f32[8,4,2,1,512]{4,3,2,1,0:T(1,128)}), f32[8,4,2,1,512]{4,3,2,1,0:T(1,128)S(1)}, u32[]{:S(2)}, u32[]{:S(2)}) %all-to-all-start.1) | async-done | bytes 131104 | tf_op jit(solution)/shard_map/all_to_all | solution.py:424
  53.6 2.4 %there.1 = (f32[2,256,128]{2,1,0:T(8,128)S(1)}, bf16[2,256,128]{2,1,0:T(8,128)(2,1)S(1)}, f32[4,2,128,256]{3,2,1,0:T(8,128)S(1)}) custom-call(s32[8]{0:T(128)S(1)} %get-tuple-element.14.live_ref, bf16[4,2,2,256,128]{4,3,2,1,0:T(8,128)(2,1)S(1)} %all-to-all-done.qg_ref, bf16[2,2,256,128]{3,2,1,0:T(8,128)(2,1)S(1)} %bitcast.23, ...), custom_call_target="tpu_custom_call" | custom-call | flops 1000000000 | bytes 2097152 | tf_op jit(solution)/shard_map/there/pallas_call | solution.py:339
  56.0 2.0 %all-gather.2 = bf16[4,256,128]{2,1,0:T(8,128)(2,1)S(1)} all-gather(bf16[2,256,128]{2,1,0:T(8,128)(2,1)S(1)} %get-tuple-element.19), channel_id=4, replica_groups=mesh['x'=4,'zh'=2,'c'=2,'n'=16,'p'=2] {'c'}, dimensions={0}, use_global_device_ids=true | all-gather | bytes 393216 | tf_op jit(solution)/shard_map/all_gather | solution.py:427
  58.1 8.1 %collective-permute-start.2 = (bf16[2,256,128]{2,1,0:T(8,128)(2,1)S(1)}, bf16[2,256,128]{2,1,0:T(8,128)(2,1)S(1)}, u32[]{:S(2)}, u32[]{:S(2)}) collective-permute-start(bf16[2,256,128]{2,1,0:T(8,128)(2,1)S(1)} %fusion.after_ref), channel_id=1, source_target_pairs={{0,65},{1,64},{64,1},{65,0},{2,67},{3,66},{66,3},{67,2},{4,69},{5,... | collective-permute-start | bytes 393224 | tf_op jit(solution)/shard_map/ppermute | solution.py:276
  66.2 3.5 %here.1 = (f32[2,256,128]{2,1,0:T(8,128)S(1)}, bf16[2,256,128]{2,1,0:T(8,128)(2,1)S(1)}, bf16[4,4,128,128]{3,2,1,0:T(8,128)(2,1)}) custom-call(s32[8]{0:T(128)S(1)} %get-tuple-element.14.live_ref, s32[16,64]{1,0:T(8,128)S(1)} %copy.16.work_ref, bf16[4,2,2,256,128]{4,3,2,1,0:T(8,128)(2,1)S(1)} %all-to-all-done.qg_ref, bf16[2,2,256,128]{3,2,1,0:T(8,128)(2,1)S(1)} %bitcast.20, ...), custom_call_target="tpu_custom_call" | custom-call | flops 99999997952 | bytes 2097152 | tf_op jit(solution)/shard_map/here/pallas_call | solution.py:357
  69.7 6.5 %all-to-all-start.2 = ((bf16[8,256,128]{2,1,0:T(8,128)(2,1)}), bf16[8,256,128]{2,1,0:T(8,128)(2,1)S(1)}, u32[]{:S(2)}, u32[]{:S(2)}) async-start(bf16[8,256,128]{2,1,0:T(8,128)(2,1)} %bitcast.9), calls=%async_computation.2 | async-start | bytes 1048576 | tf_op jit(solution)/shard_map/all_to_all | solution.py:431
  76.2 2.0 %all-gather.3 = bf16[4,256,128]{2,1,0:T(8,128)(2,1)S(1)} all-gather(bf16[2,256,128]{2,1,0:T(8,128)(2,1)S(1)} %get-tuple-element.22), channel_id=5, replica_groups=mesh['x'=4,'zh'=2,'c'=2,'n'=16,'p'=2] {'c'}, dimensions={0}, use_global_device_ids=true | all-gather | bytes 393216 | tf_op jit(solution)/shard_map/all_gather | solution.py:432
  78.2 3.2 %collective-permute-done.2.arrived_ref = bf16[2,256,128]{2,1,0:T(8,128)(2,1)S(1)} collective-permute-done((bf16[2,256,128]{2,1,0:T(8,128)(2,1)S(1)}, bf16[2,256,128]{2,1,0:T(8,128)(2,1)S(1)}, u32[]{:S(2)}, u32[]{:S(2)}) %collective-permute-start.2) | collective-permute-done | bytes 131104 | tf_op jit(solution)/shard_map/ppermute | solution.py:276
  81.3 0.7 finish.1
  82.0 3.5 %all-to-all-done.2.parts_ref = bf16[8,256,128]{2,1,0:T(8,128)(2,1)S(1)} async-done(((bf16[8,256,128]{2,1,0:T(8,128)(2,1)}), bf16[8,256,128]{2,1,0:T(8,128)(2,1)S(1)}, u32[]{:S(2)}, u32[]{:S(2)}) %all-to-all-start.2) | async-done | bytes 524320 | tf_op jit(solution)/shard_map/all_to_all | solution.py:431
  85.5 0.7 sum.1
  (15 shorter events, 0.3 us)
Async XLA Ops:
  0.6 4.8 %copy-start = (bf16[1,1,256,128]{3,2,1,0:T(8,128)(2,1)S(1)}, bf16[1,1,256,128]{3,2,1,0:T(8,128)(2,1)}, u32[]{:S(2)}) copy-start(bf16[1,1,256,128]{3,2,1,0:T(8,128)(2,1)} %param.8) | copy-start | bytes 196612
  0.6 4.8 %copy-start.1 = (bf16[1,1,256,128]{3,2,1,0:T(8,128)(2,1)S(1)}, bf16[1,1,256,128]{3,2,1,0:T(8,128)(2,1)}, u32[]{:S(2)}) copy-start(bf16[1,1,256,128]{3,2,1,0:T(8,128)(2,1)} %param.7) | copy-start | bytes 196612
  1.6 18.4 %collective-permute-start = (bf16[2,256,128]{2,1,0:T(8,128)(2,1)S(1)}, bf16[2,256,128]{2,1,0:T(8,128)(2,1)S(1)}, u32[]{:S(2)}, u32[]{:S(2)}) collective-permute-start(bf16[2,256,128]{2,1,0:T(8,128)(2,1)S(1)} %pad_maximum_fusion.own_ref), channel_id=1, source_target_pairs={{0,1},{1,0},{2,3},{3,2},{4,5},{5,4},{6,7},{7,6},{8,9},{9,8},{10,11... | collective-permute-start | bytes 393224 | tf_op jit(solution)/shard_map/ppermute | solution.py:272
  5.4 14.4 %copy-start.2 = (s32[64,32]{0,1:T(8,128)S(1)}, s32[64,32]{0,1:T(8,128)}, u32[]{:S(2)}) copy-start(s32[64,32]{0,1:T(8,128)} %param.10) | copy-start | bytes 24580
  5.5 25.3 %collective-permute-start.1 = (bf16[2,256,128]{2,1,0:T(8,128)(2,1)S(1)}, bf16[2,256,128]{2,1,0:T(8,128)(2,1)S(1)}, u32[]{:S(2)}, u32[]{:S(2)}) collective-permute-start(bf16[2,256,128]{2,1,0:T(8,128)(2,1)S(1)} %pad_maximum_fusion.1), channel_id=1, source_target_pairs={{0,65},{1,64},{64,1},{65,0},{2,67},{3,66},{66,3},{67,2},{4,69},{5,... | collective-permute-start | bytes 393224 | tf_op jit(solution)/shard_map/ppermute | solution.py:276
  21.0 18.8 %all-to-all-start = ((bf16[4,2,2,256,128]{4,3,2,1,0:T(8,128)(2,1)}), bf16[4,2,2,256,128]{4,3,2,1,0:T(8,128)(2,1)S(1)}, u32[]{:S(2)}, u32[]{:S(2)}) async-start(bf16[4,2,2,256,128]{4,3,2,1,0:T(8,128)(2,1)} %spread.1.after_ref), calls=%async_computation | async-start | bytes 2097152 | tf_op jit(solution)/shard_map/all_to_all | solution.py:416
  43.0 3.9 %copy-start.3 = (s32[16,32,2]{1,2,0:T(2,128)S(1)}, s32[16,32,2]{1,2,0:T(2,128)}, u32[]{:S(2)}) copy-start(s32[16,32,2]{1,2,0:T(2,128)} %param.11) | copy-start | bytes 12292
  43.0 10.6 %all-to-all-start.1 = ((f32[8,4,2,1,512]{4,3,2,1,0:T(1,128)}), f32[8,4,2,1,512]{4,3,2,1,0:T(1,128)S(1)}, u32[]{:S(2)}, u32[]{:S(2)}) async-start(f32[8,4,2,1,512]{4,3,2,1,0:T(1,128)} %stats.1.after_ref), calls=%async_computation.1 | async-start | bytes 262144 | tf_op jit(solution)/shard_map/all_to_all | solution.py:424
  58.1 23.3 %collective-permute-start.2 = (bf16[2,256,128]{2,1,0:T(8,128)(2,1)S(1)}, bf16[2,256,128]{2,1,0:T(8,128)(2,1)S(1)}, u32[]{:S(2)}, u32[]{:S(2)}) collective-permute-start(bf16[2,256,128]{2,1,0:T(8,128)(2,1)S(1)} %fusion.after_ref), channel_id=1, source_target_pairs={{0,65},{1,64},{64,1},{65,0},{2,67},{3,66},{66,3},{67,2},{4,69},{5,... | collective-permute-start | bytes 393224 | tf_op jit(solution)/shard_map/ppermute | solution.py:276
  69.7 15.8 %all-to-all-start.2 = ((bf16[8,256,128]{2,1,0:T(8,128)(2,1)}), bf16[8,256,128]{2,1,0:T(8,128)(2,1)S(1)}, u32[]{:S(2)}, u32[]{:S(2)}) async-start(bf16[8,256,128]{2,1,0:T(8,128)(2,1)} %bitcast.9), calls=%async_computation.2 | async-start | bytes 1048576 | tf_op jit(solution)/shard_map/all_to_all | solution.py:431

commit v8 on v7

--- a/solution.py
+++ b/solution.py
@@ -70,7 +70,7 @@
     pl.when((here == 0) & (there == 0))(nothing)
 
 
-def stats_kernel(live_ref, qg_ref, here_ref, there_ref, far_ref, out_ref):
+def stats_kernel(live_ref, qg_ref, here_ref, there_ref, far_ref, out_ref, buf, sems):
     chunks = (here_ref.at[0], here_ref.at[1], there_ref.at[0], there_ref.at[1])
 
     def group(n, carry):
@@ -104,20 +104,23 @@
                 safe = jnp.where(some, total, 1.0)
                 lse = jnp.where(some, top + jnp.log2(safe), -FAR)
                 mean = jnp.where(some, weighted / safe, 0.0)
-                for j in range(BLOCKS):
-                    out_ref[j, n, h, :, :HALF] = lse
-                    out_ref[j, n, h, :, HALF:] = mean
+                buf[n, h, :, :HALF] = lse
+                buf[n, h, :, HALF:] = mean
 
         def nothing():
-            for j in range(BLOCKS):
-                for h in range(2):
-                    out_ref[j, n, h, :, :HALF] = jnp.full((1, HALF), -FAR, jnp.float32)
-                    out_ref[j, n, h, :, HALF:] = jnp.zeros((1, HALF), jnp.float32)
+            for h in range(2):
+                buf[n, h, :, :HALF] = jnp.full((1, HALF), -FAR, jnp.float32)
+                buf[n, h, :, HALF:] = jnp.zeros((1, HALF), jnp.float32)
 
         by_sides(live_ref, n, work, nothing)
+        for j in range(BLOCKS):
+            pltpu.make_async_copy(buf.at[n], out_ref.at[j, n], sems.at[n, j]).start()
         return carry
 
     lax.fori_loop(0, NX, group, 0)
+    for n in range(NX):
+        for j in range(BLOCKS):
+            pltpu.make_async_copy(buf.at[n], out_ref.at[j, n], sems.at[n, j]).wait()
 
 
 def turn_kernel(here_ref, there_ref, after_ref, kt_ref):
@@ -309,7 +312,11 @@
         stats_kernel,
         out_shape=jax.ShapeDtypeStruct((BLOCKS, NX, 2, 1, 2 * HALF), jnp.float32),
         in_specs=[SMEM] + [VMEM] * 4,
-        out_specs=VMEM,
+        out_specs=pl.BlockSpec(memory_space=pl.ANY),
+        scratch_shapes=[
+            pltpu.VMEM((NX, 2, 1, 2 * HALF), jnp.float32),
+            pltpu.SemaphoreType.DMA((NX, BLOCKS)),
+        ],
         compiler_params=pltpu.CompilerParams(vmem_limit_bytes=32 * 1024 * 1024),
         cost_estimate=pl.CostEstimate(flops=10**9, bytes_accessed=2**21, transcendentals=2**21),
         name="stats",

time: 87.2 us -> 87.7 us (level)
  the two profiles are of different devices: /device:TPU:8 before, /device:TPU:1 now
where the time goes in v8:
time: 87.7 us; the launch traced here: 86.8 us
  starting transfers between devices  39.1 us (45%)
  blocking collectives  16.5 us (19%)
  waiting for transfers between devices  16.3 us (19%)
  Pallas kernels  12.9 us (15%)
  other arithmetic  0.97 us (1%)
    ppermute x2, starting transfers between devices, across(): return lax.ppermute(value, ('zh', 'p'), [(0, 3), (1, 2), (2, 1), (3, 0)])  20.2 us
    all_gather x2, blocking collectives, on_device(): kv = (lax.all_gather(own_kv, 'c'), lax.all_gather(across_kv, 'c'))  7.63 us
    all_to_all x1, starting transfers between devices, on_device(): dq_parts = lax.all_to_all(dq.reshape(BLOCKS, HALF, HD), ('x', 'p'), 0, 0)  7.01 us
    all_gather x1, blocking collectives, on_device(): lax.all_gather(send_there, 'c')  6.34 us
    all_to_all x1, waiting for transfers between devices, on_device(): stats = lax.all_to_all(own_stats, ('x', 'p'), 0, 0)  5.26 us
    all_to_all x1, waiting for transfers between devices, on_device(): all_qg = lax.all_to_all(spread, 'x', 0, 0)  5.06 us
    ppermute x1, starting transfers between devices, flipped(): return lax.ppermute(value, axis, [(0, 1), (1, 0)])  4.38 us
    all_to_all x1, starting transfers between devices, on_device(): all_qg = lax.all_to_all(spread, 'x', 0, 0)  4.02 us
  transfers between devices with their start and end apart: 6, of which 4 were waited for; matrix products, arithmetic and copies ran while one was open for 0% of the time, Pallas kernels for 7%

profile of v8, /device:TPU:1, one launch (start us, length us, event | category | flops | bytes accessed | tf_op | source)
XLA Modules:
  0.0 86.8 jit_solution(16530660037254810524)
XLA Ops:
  0.7 0.9 %pad_maximum_fusion.own_ref = bf16[2,256,128]{2,1,0:T(8,128)(2,1)S(1)} fusion(bf16[1,256,128]{2,1,0:T(8,128)(2,1)} %bitcast.28, bf16[1,256,128]{2,1,0:T(8,128)(2,1)} %bitcast.29), kind=kLoop, calls=%fused_computation.2 | loop fusion | flops 65536 | bytes 262144 | tf_op jit(solution)/shard_map/stack | solution.py:418
  1.6 4.4 %collective-permute-start = (bf16[2,256,128]{2,1,0:T(8,128)(2,1)S(1)}, bf16[2,256,128]{2,1,0:T(8,128)(2,1)S(1)}, u32[]{:S(2)}, u32[]{:S(2)}) collective-permute-start(bf16[2,256,128]{2,1,0:T(8,128)(2,1)S(1)} %pad_maximum_fusion.own_ref), channel_id=1, source_target_pairs={{0,1},{1,0},{2,3},{3,2},{4,5},{5,4},{6,7},{7,6},{8,9},{9,8},{10,11... | collective-permute-start | bytes 393224 | tf_op jit(solution)/shard_map/ppermute | solution.py:275
  6.0 14.1 %collective-permute-start.1 = (bf16[2,256,128]{2,1,0:T(8,128)(2,1)S(1)}, bf16[2,256,128]{2,1,0:T(8,128)(2,1)S(1)}, u32[]{:S(2)}, u32[]{:S(2)}) collective-permute-start(bf16[2,256,128]{2,1,0:T(8,128)(2,1)S(1)} %pad_maximum_fusion.1), channel_id=1, source_target_pairs={{0,65},{1,64},{64,1},{65,0},{2,67},{3,66},{66,3},{67,2},{4,69},{5,... | collective-permute-start | bytes 393224 | tf_op jit(solution)/shard_map/ppermute | solution.py:279
  20.2 1.1 %spread.1.after_ref = bf16[4,2,2,256,128]{4,3,2,1,0:T(8,128)(2,1)} custom-call(bf16[2,256,128]{2,1,0:T(8,128)(2,1)S(1)} %pad_maximum_fusion.own_ref, bf16[2,256,128]{2,1,0:T(8,128)(2,1)S(1)} %collective-permute-done.mate_ref), custom_call_target="tpu_custom_call" | custom-call | tf_op jit(solution)/shard_map/spread/pallas_call | solution.py:283
  21.3 4.0 %all-to-all-start = ((bf16[4,2,2,256,128]{4,3,2,1,0:T(8,128)(2,1)}), bf16[4,2,2,256,128]{4,3,2,1,0:T(8,128)(2,1)S(1)}, u32[]{:S(2)}, u32[]{:S(2)}) async-start(bf16[4,2,2,256,128]{4,3,2,1,0:T(8,128)(2,1)} %spread.1.after_ref), calls=%async_computation | async-start | bytes 2097152 | tf_op jit(solution)/shard_map/all_to_all | solution.py:423
  25.3 0.9 %masks.1 = (f32[4,2,8,256]{3,2,1,0:T(8,128)S(1)}, s32[8]{0:T(128)S(1)}) custom-call(s32[64,32]{1,0:T(8,128)S(1)} %copy.14.tiles_ref, bf16[4,2,2,256,128]{4,3,2,1,0:T(8,128)(2,1)} %spread.1.after_ref), custom_call_target="tpu_custom_call" | custom-call | flops 10000000000 | bytes 1048576 | tf_op jit(solution)/shard_map/masks/pallas_call | solution.py:295
  26.2 3.1 %all-gather = bf16[4,256,128]{2,1,0:T(8,128)(2,1)S(1)} all-gather(bf16[2,256,128]{2,1,0:T(8,128)(2,1)S(1)} %pad_maximum_fusion.1), channel_id=2, replica_groups=mesh['x'=4,'zh'=2,'c'=2,'n'=16,'p'=2] {'c'}, dimensions={0}, use_global_device_ids=true | all-gather | bytes 393216 | tf_op jit(solution)/shard_map/all_gather | solution.py:426
  29.4 4.5 %all-gather.1 = bf16[4,256,128]{2,1,0:T(8,128)(2,1)S(1)} all-gather(bf16[2,256,128]{2,1,0:T(8,128)(2,1)S(1)} %collective-permute-done.1), channel_id=3, replica_groups=mesh['x'=4,'zh'=2,'c'=2,'n'=16,'p'=2] {'c'}, dimensions={0}, use_global_device_ids=true | all-gather | bytes 393216 | tf_op jit(solution)/shard_map/all_gather | solution.py:426
  33.8 5.1 %all-to-all-done.qg_ref = bf16[4,2,2,256,128]{4,3,2,1,0:T(8,128)(2,1)S(1)} async-done(((bf16[4,2,2,256,128]{4,3,2,1,0:T(8,128)(2,1)}), bf16[4,2,2,256,128]{4,3,2,1,0:T(8,128)(2,1)S(1)}, u32[]{:S(2)}, u32[]{:S(2)}) %all-to-all-start) | async-done | bytes 1048608 | tf_op jit(solution)/shard_map/all_to_all | solution.py:423
  38.9 3.4 %stats.1.after_ref = f32[8,4,2,1,512]{4,3,2,1,0:T(1,128)} custom-call(s32[8]{0:T(128)S(1)} %get-tuple-element.14.live_ref, bf16[4,2,2,256,128]{4,3,2,1,0:T(8,128)(2,1)S(1)} %all-to-all-done.qg_ref, bf16[2,2,256,128]{3,2,1,0:T(8,128)(2,1)S(1)} %bitcast.18, bf16[2,2,256,128]{3,2,1,0:T(8,128)(2,1)S(1)} %bitcast.21, f32[4,2,8,256]{3,2,1,0:T(8,128)S(1)} %get-tuple-element.15.far_ref), custom_call_target="tpu_custom_call" | custom-call | flops 1000000000 | bytes 2097152 | tf_op jit(solution)/shard_map/stats/pallas_call | solution.py:311
  42.4 3.5 %all-to-all-start.1 = ((f32[8,4,2,1,512]{4,3,2,1,0:T(1,128)}), f32[8,4,2,1,512]{4,3,2,1,0:T(1,128)S(1)}, u32[]{:S(2)}, u32[]{:S(2)}) async-start(f32[8,4,2,1,512]{4,3,2,1,0:T(1,128)} %stats.1.after_ref), calls=%async_computation.1 | async-start | bytes 262144 | tf_op jit(solution)/shard_map/all_to_all | solution.py:431
  45.9 0.1 copy.15
  46.1 0.1 turn.1.kt_ref
  46.2 5.3 %all-to-all-done.1.stats_ref = f32[8,4,2,1,512]{4,3,2,1,0:T(1,128)S(1)} async-done(((f32[8,4,2,1,512]{4,3,2,1,0:T(1,128)}), f32[8,4,2,1,512]{4,3,2,1,0:T(1,128)S(1)}, u32[]{:S(2)}, u32[]{:S(2)}) %all-to-all-start.1) | async-done | bytes 131104 | tf_op jit(solution)/shard_map/all_to_all | solution.py:431
  51.5 2.4 %there.1 = (f32[2,256,128]{2,1,0:T(8,128)S(1)}, bf16[2,256,128]{2,1,0:T(8,128)(2,1)S(1)}, f32[4,2,128,256]{3,2,1,0:T(8,128)S(1)}) custom-call(s32[8]{0:T(128)S(1)} %get-tuple-element.14.live_ref, bf16[4,2,2,256,128]{4,3,2,1,0:T(8,128)(2,1)S(1)} %all-to-all-done.qg_ref, bf16[2,2,256,128]{3,2,1,0:T(8,128)(2,1)S(1)} %bitcast.23, ...), custom_call_target="tpu_custom_call" | custom-call | flops 1000000000 | bytes 2097152 | tf_op jit(solution)/shard_map/there/pallas_call | solution.py:346
  53.9 6.3 %all-gather.2 = bf16[4,256,128]{2,1,0:T(8,128)(2,1)S(1)} all-gather(bf16[2,256,128]{2,1,0:T(8,128)(2,1)S(1)} %get-tuple-element.19), channel_id=4, replica_groups=mesh['x'=4,'zh'=2,'c'=2,'n'=16,'p'=2] {'c'}, dimensions={0}, use_global_device_ids=true | all-gather | bytes 393216 | tf_op jit(solution)/shard_map/all_gather | solution.py:434
  60.2 6.1 %collective-permute-start.2 = (bf16[2,256,128]{2,1,0:T(8,128)(2,1)S(1)}, bf16[2,256,128]{2,1,0:T(8,128)(2,1)S(1)}, u32[]{:S(2)}, u32[]{:S(2)}) collective-permute-start(bf16[2,256,128]{2,1,0:T(8,128)(2,1)S(1)} %fusion.after_ref), channel_id=1, source_target_pairs={{0,65},{1,64},{64,1},{65,0},{2,67},{3,66},{66,3},{67,2},{4,69},{5,... | collective-permute-start | bytes 393224 | tf_op jit(solution)/shard_map/ppermute | solution.py:279
  66.4 3.5 %here.1 = (f32[2,256,128]{2,1,0:T(8,128)S(1)}, bf16[2,256,128]{2,1,0:T(8,128)(2,1)S(1)}, bf16[4,4,128,128]{3,2,1,0:T(8,128)(2,1)}) custom-call(s32[8]{0:T(128)S(1)} %get-tuple-element.14.live_ref, s32[16,64]{1,0:T(8,128)S(1)} %copy.16.work_ref, bf16[4,2,2,256,128]{4,3,2,1,0:T(8,128)(2,1)S(1)} %all-to-all-done.qg_ref, bf16[2,2,256,128]{3,2,1,0:T(8,128)(2,1)S(1)} %bitcast.20, ...), custom_call_target="tpu_custom_call" | custom-call | flops 99999997952 | bytes 2097152 | tf_op jit(solution)/shard_map/here/pallas_call | solution.py:364
  69.9 7.0 %all-to-all-start.2 = ((bf16[8,256,128]{2,1,0:T(8,128)(2,1)}), bf16[8,256,128]{2,1,0:T(8,128)(2,1)S(1)}, u32[]{:S(2)}, u32[]{:S(2)}) async-start(bf16[8,256,128]{2,1,0:T(8,128)(2,1)} %bitcast.9), calls=%async_computation.2 | async-start | bytes 1048576 | tf_op jit(solution)/shard_map/all_to_all | solution.py:438
  76.9 2.5 %all-gather.3 = bf16[4,256,128]{2,1,0:T(8,128)(2,1)S(1)} all-gather(bf16[2,256,128]{2,1,0:T(8,128)(2,1)S(1)} %get-tuple-element.22), channel_id=5, replica_groups=mesh['x'=4,'zh'=2,'c'=2,'n'=16,'p'=2] {'c'}, dimensions={0}, use_global_device_ids=true | all-gather | bytes 393216 | tf_op jit(solution)/shard_map/all_gather | solution.py:439
  79.5 2.9 %collective-permute-done.2.arrived_ref = bf16[2,256,128]{2,1,0:T(8,128)(2,1)S(1)} collective-permute-done((bf16[2,256,128]{2,1,0:T(8,128)(2,1)S(1)}, bf16[2,256,128]{2,1,0:T(8,128)(2,1)S(1)}, u32[]{:S(2)}, u32[]{:S(2)}) %collective-permute-start.2) | collective-permute-done | bytes 131104 | tf_op jit(solution)/shard_map/ppermute | solution.py:279
  82.4 0.7 finish.1
  83.0 3.1 %all-to-all-done.2.parts_ref = bf16[8,256,128]{2,1,0:T(8,128)(2,1)S(1)} async-done(((bf16[8,256,128]{2,1,0:T(8,128)(2,1)}), bf16[8,256,128]{2,1,0:T(8,128)(2,1)S(1)}, u32[]{:S(2)}, u32[]{:S(2)}) %all-to-all-start.2) | async-done | bytes 524320 | tf_op jit(solution)/shard_map/all_to_all | solution.py:438
  86.1 0.7 sum.1
  (15 shorter events, 0.2 us)
Async XLA Ops:
  0.6 5.3 %copy-start = (bf16[1,1,256,128]{3,2,1,0:T(8,128)(2,1)S(1)}, bf16[1,1,256,128]{3,2,1,0:T(8,128)(2,1)}, u32[]{:S(2)}) copy-start(bf16[1,1,256,128]{3,2,1,0:T(8,128)(2,1)} %param.8) | copy-start | bytes 196612
  0.6 5.3 %copy-start.1 = (bf16[1,1,256,128]{3,2,1,0:T(8,128)(2,1)S(1)}, bf16[1,1,256,128]{3,2,1,0:T(8,128)(2,1)}, u32[]{:S(2)}) copy-start(bf16[1,1,256,128]{3,2,1,0:T(8,128)(2,1)} %param.7) | copy-start | bytes 196612
  1.6 18.6 %collective-permute-start = (bf16[2,256,128]{2,1,0:T(8,128)(2,1)S(1)}, bf16[2,256,128]{2,1,0:T(8,128)(2,1)S(1)}, u32[]{:S(2)}, u32[]{:S(2)}) collective-permute-start(bf16[2,256,128]{2,1,0:T(8,128)(2,1)S(1)} %pad_maximum_fusion.own_ref), channel_id=1, source_target_pairs={{0,1},{1,0},{2,3},{3,2},{4,5},{5,4},{6,7},{7,6},{8,9},{9,8},{10,11... | collective-permute-start | bytes 393224 | tf_op jit(solution)/shard_map/ppermute | solution.py:275
  6.0 14.1 %copy-start.2 = (s32[64,32]{0,1:T(8,128)S(1)}, s32[64,32]{0,1:T(8,128)}, u32[]{:S(2)}) copy-start(s32[64,32]{0,1:T(8,128)} %param.10) | copy-start | bytes 24580
  6.0 23.3 %collective-permute-start.1 = (bf16[2,256,128]{2,1,0:T(8,128)(2,1)S(1)}, bf16[2,256,128]{2,1,0:T(8,128)(2,1)S(1)}, u32[]{:S(2)}, u32[]{:S(2)}) collective-permute-start(bf16[2,256,128]{2,1,0:T(8,128)(2,1)S(1)} %pad_maximum_fusion.1), channel_id=1, source_target_pairs={{0,65},{1,64},{64,1},{65,0},{2,67},{3,66},{66,3},{67,2},{4,69},{5,... | collective-permute-start | bytes 393224 | tf_op jit(solution)/shard_map/ppermute | solution.py:279
  21.3 17.6 %all-to-all-start = ((bf16[4,2,2,256,128]{4,3,2,1,0:T(8,128)(2,1)}), bf16[4,2,2,256,128]{4,3,2,1,0:T(8,128)(2,1)S(1)}, u32[]{:S(2)}, u32[]{:S(2)}) async-start(bf16[4,2,2,256,128]{4,3,2,1,0:T(8,128)(2,1)} %spread.1.after_ref), calls=%async_computation | async-start | bytes 2097152 | tf_op jit(solution)/shard_map/all_to_all | solution.py:423
  42.3 3.6 %copy-start.3 = (s32[16,32,2]{1,2,0:T(2,128)S(1)}, s32[16,32,2]{1,2,0:T(2,128)}, u32[]{:S(2)}) copy-start(s32[16,32,2]{1,2,0:T(2,128)} %param.11) | copy-start | bytes 12292
  42.4 9.1 %all-to-all-start.1 = ((f32[8,4,2,1,512]{4,3,2,1,0:T(1,128)}), f32[8,4,2,1,512]{4,3,2,1,0:T(1,128)S(1)}, u32[]{:S(2)}, u32[]{:S(2)}) async-start(f32[8,4,2,1,512]{4,3,2,1,0:T(1,128)} %stats.1.after_ref), calls=%async_computation.1 | async-start | bytes 262144 | tf_op jit(solution)/shard_map/all_to_all | solution.py:431
  60.2 22.1 %collective-permute-start.2 = (bf16[2,256,128]{2,1,0:T(8,128)(2,1)S(1)}, bf16[2,256,128]{2,1,0:T(8,128)(2,1)S(1)}, u32[]{:S(2)}, u32[]{:S(2)}) collective-permute-start(bf16[2,256,128]{2,1,0:T(8,128)(2,1)S(1)} %fusion.after_ref), channel_id=1, source_target_pairs={{0,65},{1,64},{64,1},{65,0},{2,67},{3,66},{66,3},{67,2},{4,69},{5,... | collective-permute-start | bytes 393224 | tf_op jit(solution)/shard_map/ppermute | solution.py:279
  69.9 16.2 %all-to-all-start.2 = ((bf16[8,256,128]{2,1,0:T(8,128)(2,1)}), bf16[8,256,128]{2,1,0:T(8,128)(2,1)S(1)}, u32[]{:S(2)}, u32[]{:S(2)}) async-start(bf16[8,256,128]{2,1,0:T(8,128)(2,1)} %bitcast.9), calls=%async_computation.2 | async-start | bytes 1048576 | tf_op jit(solution)/shard_map/all_to_all | solution.py:438
